TPU v7x, 32 devices: a whole 2x2x4 slice. The times are simulated.
32 devices in a mesh: rep: 16 (over z, x, core), grp: 2 (over y).
Axes of the slice: x: 2, y: 2, z: 4, core: 2. Of those that a mesh axis runs over, the one named last changes fastest.
Arguments:
- tokens: bfloat16 [16384, 1536], P(('rep', 'grp')), may hold values from -6 to 6
- cotangent: bfloat16 [16384, 1536], P(('rep', 'grp')), may hold values from -6 to 6
- routes: int32 [16384, 8], P(('rep', 'grp')), may hold values from 0 to 39, all different within a row; in each aligned block of 512 rows (0 to 511, 512 to 1023, ...) at most 143 rows name the same one
- padding: int32 [16384], P(('rep', 'grp')), may hold values 0 or 1
- parents: int32 [16, 8], P('rep'), may hold values from 0 to 6, as said below
- adapter_ids: int32 [16], P('rep'), may hold values from 0 to 3
- w_query: bfloat16 [1536, 1536], P('grp'), may hold values from -0.15625 to 0.15625
- w_keyval: bfloat16 [1536, 1024], P('grp'), may hold values from -0.15625 to 0.15625
- w_output: bfloat16 [1536, 1536], P('grp'), may hold values from -1 to 1
- w_router: bfloat16 [1536, 40], P('grp'), may hold values from -0.078125 to 0.078125
- gain_attn: bfloat16 [1536], P('grp'), may hold values from 0.5 to 1.5
- gain_ffn: bfloat16 [1536], P('grp'), may hold values from 0.5 to 1.5
- w_gateup: bfloat16 [40, 1536, 1024], P('grp'), may hold values from -0.15625 to 0.15625
- w_down: bfloat16 [40, 512, 1536], P('grp'), may hold values from -1 to 1
- a_qkv: bfloat16 [4, 1536, 48], P(None, 'grp'), may hold values from -0.15625 to 0.15625
- b_query: bfloat16 [4, 16, 1536], P(None, None, 'grp'), may hold values from -0.75 to 0.75
- b_keyval: bfloat16 [4, 2, 16, 512], P(None, None, None, 'grp'), may hold values from -0.75 to 0.75
- a_output: bfloat16 [4, 1536, 16], P(None, 'grp'), may hold values from -0.15625 to 0.15625
- b_output: bfloat16 [4, 16, 1536], P(None, None, 'grp'), may hold values from -6 to 6
- a_router: bfloat16 [4, 1536, 16], P(None, 'grp'), may hold values from -0.15625 to 0.15625
- b_router: bfloat16 [4, 16, 40], P(None, None, 'grp'), may hold values from -0.375 to 0.375
- a_gateup: bfloat16 [4, 40, 1536, 32], P(None, 'grp'), may hold values from -0.15625 to 0.15625
- b_gateup: bfloat16 [4, 40, 2, 16, 512], P(None, 'grp'), may hold values from -0.75 to 0.75
- a_down: bfloat16 [4, 40, 512, 16], P(None, 'grp'), may hold values from -0.25 to 0.25
- b_down: bfloat16 [4, 40, 16, 1536], P(None, 'grp'), may hold values from -1.5 to 1.5
Outputs:
- result: bfloat16 [16384, 1536], P(('rep', 'grp'))
- grad_tokens: bfloat16 [16384, 1536], P(('rep', 'grp'))
- grad_a_qkv: float32 [4, 1536, 48], P(None, 'grp')
- grad_b_query: float32 [4, 16, 1536], P(None, None, 'grp')
- grad_b_keyval: float32 [4, 2, 16, 512], P(None, None, None, 'grp')
- grad_a_output: float32 [4, 1536, 16], P(None, 'grp')
- grad_b_output: float32 [4, 16, 1536], P(None, None, 'grp')
- grad_a_router: float32 [4, 1536, 16], P(None, 'grp')
- grad_b_router: float32 [4, 16, 40], P(None, None, 'grp')
- grad_a_gateup: float32 [4, 40, 1536, 32], P(None, 'grp')
- grad_b_gateup: float32 [4, 40, 2, 16, 512], P(None, 'grp')
- grad_a_down: float32 [4, 40, 512, 16], P(None, 'grp')
- grad_b_down: float32 [4, 40, 16, 1536], P(None, 'grp')
Inputs may be any that keep to these rules, and one draw needn't show every extreme that they name: `routes`: each row names 8 different experts. Among the 512 rows of one device no expert is named by more than 143 rows, and in some of these blocks one expert is named by exactly 143. parents[t, s] is s - 1 or s - 2 for s >= 2, and 0 for segments 0 and 1.
All inputs are finite; a program needn't handle non-finite values. No bound on the sum of `padding` on one device may be relied on, other than what follows from the above.
Results may differ from a plain program's by a relative error of at most 0.022.
Values may be sent and summed in bfloat16 or wider, within the bound.
No kernel may reach another device: no remote copies, remote signals or barrier semaphores. Data moves between devices by JAX's collectives and lax.ppermute only.
A program may use at most 512 MiB of HBM per device.

v0:
```python
import jax
import jax.numpy as jnp
from jax import lax
from jax.sharding import PartitionSpec as P

QUERY_HEADS = 24
KEY_VALUE_HEADS = 8
HEAD_SIZE = 64
FF = 512
TOPK = 8
RANK = 16
SEG = 128


EPSILON = 1e-05


def product(left, right):
    return jnp.dot(left, right, preferred_element_type=jnp.float32)


def product_back(left, right):
    return lax.dot_general(
        left, right, (((1,), (1,)), ((), ())), preferred_element_type=jnp.float32
    )


def product_outer(left, right):
    return lax.dot_general(
        left, right, (((0,), (0,)), ((), ())), preferred_element_type=jnp.float32
    )


def precise_back(left, right):
    return lax.dot_general(
        left,
        right.astype(jnp.float32),
        (((1,), (1,)), ((), ())),
        precision=lax.Precision.HIGHEST,
        preferred_element_type=jnp.float32,
    )


def precise_outer(left, right):
    return lax.dot_general(
        left.astype(jnp.float32),
        right,
        (((0,), (0,)), ((), ())),
        precision=lax.Precision.HIGHEST,
        preferred_element_type=jnp.float32,
    )


def rms_norm(value_rows, gain):
    return (
        value_rows
        * lax.rsqrt(jnp.mean(value_rows * value_rows, axis=-1, keepdims=True) + EPSILON)
        * gain
    )


def rms_back(value_rows, gain, upstream):
    factor = lax.rsqrt(jnp.mean(value_rows * value_rows, axis=-1, keepdims=True) + EPSILON)
    scaled = value_rows * factor
    incoming = upstream * gain
    return factor * (incoming - scaled * jnp.mean(incoming * scaled, axis=-1, keepdims=True))


def ancestry(parent_row):
    total = parent_row.shape[0]
    labels = jnp.arange(total, dtype=jnp.int32)

    def climb(count, state):
        current, table = state
        current = jnp.sum(
            jnp.where(current[:, None] == labels[None, :], parent_row[None, :], 0), axis=1
        )
        table = jnp.maximum(table, (current[:, None] == labels[None, :]).astype(jnp.int32))
        return (current, table)

    start_index = (labels[:, None] == labels[None, :]).astype(jnp.int32)
    return lax.fori_loop(0, total, climb, (labels, start_index))[1]


def tree_mask(parent_row, pad_row, first, count, tree_length):
    table = ancestry(parent_row)
    segs_here = count // SEG
    segs_all = tree_length // SEG
    rows = lax.dynamic_slice_in_dim(table, first // SEG, segs_here, 0)
    linked = jnp.broadcast_to(rows[:, None, :, None] > 0, (segs_here, SEG, segs_all, SEG)).reshape(
        count, tree_length
    )
    query_pos = first + jnp.arange(count, dtype=jnp.int32)
    key_pos = jnp.arange(tree_length, dtype=jnp.int32)
    same = query_pos[:, None] // SEG == key_pos[None, :] // SEG
    causal = jnp.logical_or(jnp.logical_not(same), key_pos[None, :] <= query_pos[:, None])
    live = jnp.logical_or(pad_row[None, :] > 0, key_pos[None, :] == query_pos[:, None])
    return jnp.logical_and(jnp.logical_and(linked, causal), live)


def expert_forward(rows_in, gateup_w, down_w, adapt_in, adapt_out, down_in, down_out):
    gate_up = jnp.einsum("erd,edf->erf", rows_in, gateup_w, preferred_element_type=jnp.float32)
    rank_in = jnp.einsum(
        "erd,edk->erk", rows_in, adapt_in, preferred_element_type=jnp.float32
    ).astype(jnp.bfloat16)
    gate_pre = gate_up[..., :FF] + jnp.einsum(
        "erk,ekf->erf", rank_in[..., :RANK], adapt_out[:, 0], preferred_element_type=jnp.float32
    )
    up_pre = gate_up[..., FF:] + jnp.einsum(
        "erk,ekf->erf", rank_in[..., RANK:], adapt_out[:, 1], preferred_element_type=jnp.float32
    )
    hidden = (jax.nn.silu(gate_pre) * up_pre).astype(jnp.bfloat16)
    rank_down = jnp.einsum(
        "erf,efk->erk", hidden, down_in, preferred_element_type=jnp.float32
    ).astype(jnp.bfloat16)
    expert_out = jnp.einsum(
        "erf,efd->erd", hidden, down_w, preferred_element_type=jnp.float32
    ) + jnp.einsum("erk,ekd->erd", rank_down, down_out, preferred_element_type=jnp.float32)
    return (gate_pre, up_pre, rank_in, hidden, rank_down, expert_out)


def local(
    tokens,
    cotangent,
    routes,
    padding,
    parents,
    adapter_ids,
    w_query,
    w_keyval,
    w_output,
    w_router,
    gain_attn,
    gain_ffn,
    w_gateup,
    w_down,
    a_qkv,
    b_query,
    b_keyval,
    a_output,
    b_output,
    a_router,
    b_router,
    a_gateup,
    b_gateup,
    a_down,
    b_down,
):
    groups = lax.axis_size("grp")
    member = lax.axis_index("grp")
    tokens_per_chip_local = tokens.shape[0]
    width = tokens.shape[1]
    tree_length = tokens_per_chip_local * groups
    experts_dev = w_gateup.shape[0]
    experts = experts_dev * groups
    capacity = tokens_per_chip_local * TOPK * 7 // (experts * 5)
    key_value_width = KEY_VALUE_HEADS * HEAD_SIZE
    group_index = QUERY_HEADS // KEY_VALUE_HEADS
    scale = HEAD_SIZE ** (-0.5)
    chosen = adapter_ids[0]
    first = member * tokens_per_chip_local
    (
        query_full,
        keyval_full,
        output_full,
        router_full,
        attn_gain,
        ffn_gain,
        qkv_in,
        query_out,
        keyval_out,
        output_in,
        output_out,
        router_in,
        router_out,
    ) = (
        lax.all_gather(w_query, "grp", axis=0, tiled=True),
        lax.all_gather(w_keyval, "grp", axis=0, tiled=True),
        lax.all_gather(w_output, "grp", axis=0, tiled=True),
        lax.all_gather(w_router, "grp", axis=0, tiled=True),
        lax.all_gather(gain_attn, "grp", axis=0, tiled=True),
        lax.all_gather(gain_ffn, "grp", axis=0, tiled=True),
        lax.all_gather(a_qkv[chosen], "grp", axis=0, tiled=True),
        lax.all_gather(b_query[chosen], "grp", axis=1, tiled=True),
        lax.all_gather(b_keyval[chosen], "grp", axis=2, tiled=True),
        lax.all_gather(a_output[chosen], "grp", axis=0, tiled=True),
        lax.all_gather(b_output[chosen], "grp", axis=1, tiled=True),
        lax.all_gather(a_router[chosen], "grp", axis=0, tiled=True),
        lax.all_gather(b_router[chosen], "grp", axis=1, tiled=True),
    )
    tokens_f = tokens.astype(jnp.float32)
    normed = rms_norm(tokens_f, attn_gain.astype(jnp.float32)).astype(jnp.bfloat16)
    low_rank = product(normed, qkv_in).astype(jnp.bfloat16)
    query_rows = (product(normed, query_full) + product(low_rank[:, :RANK], query_out)).astype(
        jnp.bfloat16
    )
    keyvals = product(normed, keyval_full)
    key_rows = (
        keyvals[:, :key_value_width] + product(low_rank[:, RANK : 2 * RANK], keyval_out[0])
    ).astype(jnp.bfloat16)
    value_rows = (
        keyvals[:, key_value_width:] + product(low_rank[:, 2 * RANK :], keyval_out[1])
    ).astype(jnp.bfloat16)
    pad_local = padding.astype(jnp.bfloat16)
    every_key_row, every_value_row, pad_all = (
        lax.all_gather(key_rows, "grp", axis=0, tiled=True),
        lax.all_gather(value_rows, "grp", axis=0, tiled=True),
        lax.all_gather(pad_local, "grp", axis=0, tiled=True),
    )
    mask = tree_mask(parents[0], pad_all, first, tokens_per_chip_local, tree_length)
    heads_of_query = query_rows.reshape(
        tokens_per_chip_local, KEY_VALUE_HEADS, group_index, HEAD_SIZE
    ).transpose(1, 0, 2, 3)
    heads_of_key = every_key_row.reshape(tree_length, KEY_VALUE_HEADS, HEAD_SIZE).transpose(1, 0, 2)
    heads_of_value = every_value_row.reshape(tree_length, KEY_VALUE_HEADS, HEAD_SIZE).transpose(
        1, 0, 2
    )

    def attend(operands):
        query_grp, key_grp, value_grp = operands
        scores = (
            jnp.einsum("qrd,kd->rqk", query_grp, key_grp, preferred_element_type=jnp.float32)
            * scale
        )
        scores = jnp.where(mask[None], scores, -1e30)
        top = jnp.max(scores, axis=-1, keepdims=True)
        weights = jnp.exp(scores - top)
        total = jnp.sum(weights, axis=-1, keepdims=True)
        probs = (weights / total).astype(jnp.bfloat16)
        mixed = jnp.einsum("rqk,kd->qrd", probs, value_grp, preferred_element_type=jnp.float32)
        return (mixed.astype(jnp.bfloat16), top[..., 0] + jnp.log(total[..., 0]))

    mixed_heads, log_totals = lax.map(attend, (heads_of_query, heads_of_key, heads_of_value))
    attended = mixed_heads.transpose(1, 0, 2, 3).reshape(tokens_per_chip_local, width)
    out_rank = product(attended, output_in).astype(jnp.bfloat16)
    middle = tokens_f + product(attended, output_full) + product(out_rank, output_out)
    normed_ffn = rms_norm(middle, ffn_gain.astype(jnp.float32)).astype(jnp.bfloat16)
    router_rank = product(normed_ffn, router_in).astype(jnp.bfloat16)
    logits = product(normed_ffn, router_full) + product(router_rank, router_out)
    labels = jnp.arange(experts, dtype=jnp.int32)
    chosen_hot = routes[:, :, None] == labels[None, None, :]
    picked = jnp.sum(jnp.where(chosen_hot, logits[:, None, :], 0.0), axis=-1)
    gates = jax.nn.softmax(picked, axis=-1)
    flat_hot = chosen_hot.reshape(tokens_per_chip_local * TOPK, experts).astype(jnp.int32)
    position = jnp.sum(flat_hot * (jnp.cumsum(flat_hot, axis=0) - 1), axis=1)
    target = routes.reshape(-1) * capacity + position
    slot_rows = jnp.broadcast_to(
        normed_ffn[:, None, :], (tokens_per_chip_local, TOPK, width)
    ).reshape(tokens_per_chip_local * TOPK, width)
    outgoing = (
        jnp.zeros((experts * capacity, width), jnp.bfloat16)
        .at[target]
        .set(slot_rows)
        .reshape(groups, experts_dev, 1, capacity, width)
    )
    incoming = lax.all_to_all(outgoing, "grp", split_axis=0, concat_axis=2, tiled=True)
    rows_in = incoming.reshape(experts_dev, groups * capacity, width)
    adapt_in = a_gateup[chosen]
    adapt_out = b_gateup[chosen]
    down_in = a_down[chosen]
    down_out = b_down[chosen]
    expert_out = expert_forward(rows_in, w_gateup, w_down, adapt_in, adapt_out, down_in, down_out)[
        5
    ].astype(jnp.bfloat16)
    returned = lax.all_to_all(
        expert_out.reshape(1, experts_dev, groups, capacity, width),
        "grp",
        split_axis=2,
        concat_axis=0,
        tiled=True,
    )
    slot_out = (
        returned.reshape(experts * capacity, width)[target]
        .reshape(tokens_per_chip_local, TOPK, width)
        .astype(jnp.float32)
    )
    result = (middle + jnp.sum(gates[:, :, None] * slot_out, axis=1)).astype(jnp.bfloat16)
    upstream = cotangent.astype(jnp.float32)
    d_slots = (
        (gates[:, :, None] * upstream[:, None, :])
        .astype(jnp.bfloat16)
        .reshape(tokens_per_chip_local * TOPK, width)
    )
    d_outgoing = (
        jnp.zeros((experts * capacity, width), jnp.bfloat16)
        .at[target]
        .set(d_slots)
        .reshape(groups, experts_dev, 1, capacity, width)
    )
    d_gates = jnp.sum(upstream[:, None, :] * slot_out, axis=-1)
    d_picked = gates * (d_gates - jnp.sum(gates * d_gates, axis=-1, keepdims=True))
    d_logits = jnp.sum(jnp.where(chosen_hot, d_picked[:, :, None], 0.0), axis=1).astype(
        jnp.bfloat16
    )
    rows_again, d_incoming = (
        lax.all_to_all(outgoing, "grp", split_axis=0, concat_axis=2, tiled=True),
        lax.all_to_all(d_outgoing, "grp", split_axis=0, concat_axis=2, tiled=True),
    )
    rows_back = rows_again.reshape(experts_dev, groups * capacity, width)
    d_expert = d_incoming.reshape(experts_dev, groups * capacity, width)
    gate_pre, up_pre, rank_in, hidden, rank_down, unused_out = expert_forward(
        rows_back, w_gateup, w_down, adapt_in, adapt_out, down_in, down_out
    )
    d_rank_down = jnp.einsum("erd,ekd->erk", d_expert, down_out, preferred_element_type=jnp.float32)
    d_hidden = jnp.einsum(
        "erd,efd->erf", d_expert, w_down, preferred_element_type=jnp.float32
    ) + jnp.einsum(
        "erk,efk->erf", d_rank_down, down_in.astype(jnp.float32), precision=lax.Precision.HIGHEST
    )
    grad_down_out = jnp.einsum(
        "erk,erd->ekd", rank_down, d_expert, preferred_element_type=jnp.float32
    )
    grad_down_in = jnp.einsum(
        "erf,erk->efk", hidden.astype(jnp.float32), d_rank_down, precision=lax.Precision.HIGHEST
    )
    sigmoid = jax.nn.sigmoid(gate_pre)
    d_gate = (d_hidden * up_pre * sigmoid * (1.0 + gate_pre * (1.0 - sigmoid))).astype(jnp.bfloat16)
    d_up = (d_hidden * gate_pre * sigmoid).astype(jnp.bfloat16)
    d_rank_in = jnp.concatenate(
        [
            jnp.einsum("erf,ekf->erk", d_gate, adapt_out[:, 0], preferred_element_type=jnp.float32),
            jnp.einsum("erf,ekf->erk", d_up, adapt_out[:, 1], preferred_element_type=jnp.float32),
        ],
        axis=-1,
    )
    d_rows = jnp.einsum(
        "erf,edf->erd",
        jnp.concatenate([d_gate, d_up], axis=-1),
        w_gateup,
        preferred_element_type=jnp.float32,
    )
    d_rows = (
        d_rows
        + jnp.einsum(
            "erk,edk->erd", d_rank_in, adapt_in.astype(jnp.float32), precision=lax.Precision.HIGHEST
        )
    ).astype(jnp.bfloat16)
    grad_adapt_out = jnp.stack(
        [
            jnp.einsum(
                "erk,erf->ekf", rank_in[..., :RANK], d_gate, preferred_element_type=jnp.float32
            ),
            jnp.einsum(
                "erk,erf->ekf", rank_in[..., RANK:], d_up, preferred_element_type=jnp.float32
            ),
        ],
        axis=1,
    )
    grad_adapt_in = jnp.einsum(
        "erd,erk->edk", rows_back.astype(jnp.float32), d_rank_in, precision=lax.Precision.HIGHEST
    )
    d_returned = lax.all_to_all(
        d_rows.reshape(1, experts_dev, groups, capacity, width),
        "grp",
        split_axis=2,
        concat_axis=0,
        tiled=True,
    )
    d_slot_rows = (
        d_returned.reshape(experts * capacity, width)[target]
        .reshape(tokens_per_chip_local, TOPK, width)
        .astype(jnp.float32)
    )
    backward_set = (
        lax.all_gather(w_query, "grp", axis=0, tiled=True),
        lax.all_gather(w_keyval, "grp", axis=0, tiled=True),
        lax.all_gather(w_output, "grp", axis=0, tiled=True),
        lax.all_gather(w_router, "grp", axis=0, tiled=True),
        lax.all_gather(gain_attn, "grp", axis=0, tiled=True),
        lax.all_gather(gain_ffn, "grp", axis=0, tiled=True),
        lax.all_gather(a_qkv[chosen], "grp", axis=0, tiled=True),
        lax.all_gather(b_query[chosen], "grp", axis=1, tiled=True),
        lax.all_gather(b_keyval[chosen], "grp", axis=2, tiled=True),
        lax.all_gather(a_output[chosen], "grp", axis=0, tiled=True),
        lax.all_gather(b_output[chosen], "grp", axis=1, tiled=True),
        lax.all_gather(a_router[chosen], "grp", axis=0, tiled=True),
        lax.all_gather(b_router[chosen], "grp", axis=1, tiled=True),
        lax.all_gather(key_rows, "grp", axis=0, tiled=True),
        lax.all_gather(value_rows, "grp", axis=0, tiled=True),
        lax.all_gather(pad_local, "grp", axis=0, tiled=True),
    )
    (
        query_back,
        keyval_back,
        output_back,
        router_back,
        attn_gain_back,
        ffn_gain_back,
        qkv_in_back,
        query_out_back,
        keyval_out_back,
        output_in_back,
        output_out_back,
        router_in_back,
        router_out_back,
        backward_keys,
        backward_values,
        pad_back,
    ) = backward_set
    d_router_rank = product_back(d_logits, router_out_back)
    d_normed_ffn = (
        jnp.sum(d_slot_rows, axis=1)
        + product_back(d_logits, router_back)
        + precise_back(d_router_rank, router_in_back)
    )
    grad_router_out = product_outer(router_rank, d_logits)
    grad_router_in = precise_outer(normed_ffn, d_router_rank)
    d_middle = upstream + rms_back(middle, ffn_gain_back.astype(jnp.float32), d_normed_ffn)
    d_attn = d_middle.astype(jnp.bfloat16)
    d_out_rank = product_back(d_attn, output_out_back)
    attended_gradient = (
        product_back(d_attn, output_back) + precise_back(d_out_rank, output_in_back)
    ).astype(jnp.bfloat16)
    grad_output_out = product_outer(out_rank, d_attn)
    grad_output_in = precise_outer(attended, d_out_rank)
    mask_back = tree_mask(parents[0], pad_back, first, tokens_per_chip_local, tree_length)
    backward_key_heads = backward_keys.reshape(tree_length, KEY_VALUE_HEADS, HEAD_SIZE).transpose(
        1, 0, 2
    )
    backward_value_heads = backward_values.reshape(
        tree_length, KEY_VALUE_HEADS, HEAD_SIZE
    ).transpose(1, 0, 2)
    heads_gradient = attended_gradient.reshape(
        tokens_per_chip_local, KEY_VALUE_HEADS, group_index, HEAD_SIZE
    ).transpose(1, 0, 2, 3)

    def attend_back(operands):
        query_grp, key_grp, value_grp, d_grp, log_total = operands
        scores = (
            jnp.einsum("qrd,kd->rqk", query_grp, key_grp, preferred_element_type=jnp.float32)
            * scale
        )
        scores = jnp.where(mask_back[None], scores, -1e30)
        probs = jnp.exp(scores - log_total[..., None])
        d_value = jnp.einsum(
            "rqk,qrd->kd", probs.astype(jnp.bfloat16), d_grp, preferred_element_type=jnp.float32
        )
        d_probs = jnp.einsum("qrd,kd->rqk", d_grp, value_grp, preferred_element_type=jnp.float32)
        d_scores = (probs * (d_probs - jnp.sum(probs * d_probs, axis=-1, keepdims=True))).astype(
            jnp.bfloat16
        )
        d_query = (
            jnp.einsum("rqk,kd->qrd", d_scores, key_grp, preferred_element_type=jnp.float32) * scale
        )
        d_key = (
            jnp.einsum("rqk,qrd->kd", d_scores, query_grp, preferred_element_type=jnp.float32)
            * scale
        )
        return (d_query, d_key, d_value)

    d_query_heads, d_key_heads, d_value_heads = lax.map(
        attend_back,
        (heads_of_query, backward_key_heads, backward_value_heads, heads_gradient, log_totals),
    )
    d_queries = (
        d_query_heads.transpose(1, 0, 2, 3)
        .reshape(tokens_per_chip_local, width)
        .astype(jnp.bfloat16)
    )
    d_keys_part = d_key_heads.transpose(1, 0, 2).reshape(tree_length, key_value_width)
    d_values_part = d_value_heads.transpose(1, 0, 2).reshape(tree_length, key_value_width)
    d_keys_sum, d_values_sum = (
        lax.psum_scatter(
            d_keys_part.astype(jnp.bfloat16), "grp", scatter_dimension=0, tiled=True
        ).astype(jnp.float32),
        lax.psum_scatter(
            d_values_part.astype(jnp.bfloat16), "grp", scatter_dimension=0, tiled=True
        ).astype(jnp.float32),
    )
    d_keys = d_keys_sum.astype(jnp.bfloat16)
    d_values = d_values_sum.astype(jnp.bfloat16)
    d_rank_qkv = jnp.concatenate(
        [
            product_back(d_queries, query_out_back),
            product_back(d_keys, keyval_out_back[0]),
            product_back(d_values, keyval_out_back[1]),
        ],
        axis=-1,
    )
    d_normed = (
        product_back(d_queries, query_back)
        + product_back(jnp.concatenate([d_keys, d_values], axis=-1), keyval_back)
        + precise_back(d_rank_qkv, qkv_in_back)
    )
    grad_input = (
        d_middle + rms_back(tokens_f, attn_gain_back.astype(jnp.float32), d_normed)
    ).astype(jnp.bfloat16)
    grad_qkv_in = precise_outer(normed, d_rank_qkv)
    grad_query_out = product_outer(low_rank[:, :RANK], d_queries)
    grad_keyval_out = jnp.stack(
        [
            product_outer(low_rank[:, RANK : 2 * RANK], d_keys),
            product_outer(low_rank[:, 2 * RANK :], d_values),
        ],
        axis=0,
    )
    (
        owned_qkv_in,
        owned_query_out,
        owned_keyval_out,
        owned_output_in,
        owned_output_out,
        owned_router_in,
        owned_router_out,
    ) = (
        lax.psum_scatter(
            grad_qkv_in.astype(jnp.bfloat16), "grp", scatter_dimension=0, tiled=True
        ).astype(jnp.float32),
        lax.psum_scatter(
            grad_query_out.astype(jnp.bfloat16), "grp", scatter_dimension=1, tiled=True
        ).astype(jnp.float32),
        lax.psum_scatter(
            grad_keyval_out.astype(jnp.bfloat16), "grp", scatter_dimension=2, tiled=True
        ).astype(jnp.float32),
        lax.psum_scatter(
            grad_output_in.astype(jnp.bfloat16), "grp", scatter_dimension=0, tiled=True
        ).astype(jnp.float32),
        lax.psum_scatter(
            grad_output_out.astype(jnp.bfloat16), "grp", scatter_dimension=1, tiled=True
        ).astype(jnp.float32),
        lax.psum_scatter(
            grad_router_in.astype(jnp.bfloat16), "grp", scatter_dimension=0, tiled=True
        ).astype(jnp.float32),
        lax.psum_scatter(
            grad_router_out.astype(jnp.bfloat16), "grp", scatter_dimension=1, tiled=True
        ).astype(jnp.float32),
    )
    selector = (jnp.arange(a_qkv.shape[0], dtype=jnp.int32) == chosen).astype(jnp.float32)

    def spread(gradient):
        return selector.reshape((-1,) + (1,) * gradient.ndim) * gradient[None]

    (
        grad_a_qkv,
        grad_b_query,
        grad_b_keyval,
        grad_a_output,
        grad_b_output,
        grad_a_router,
        grad_b_router,
        grad_a_gateup,
        grad_b_gateup,
        grad_a_down,
        grad_b_down,
    ) = (
        lax.psum(spread(owned_qkv_in).astype(jnp.bfloat16), "rep").astype(jnp.float32),
        lax.psum(spread(owned_query_out).astype(jnp.bfloat16), "rep").astype(jnp.float32),
        lax.psum(spread(owned_keyval_out).astype(jnp.bfloat16), "rep").astype(jnp.float32),
        lax.psum(spread(owned_output_in).astype(jnp.bfloat16), "rep").astype(jnp.float32),
        lax.psum(spread(owned_output_out).astype(jnp.bfloat16), "rep").astype(jnp.float32),
        lax.psum(spread(owned_router_in).astype(jnp.bfloat16), "rep").astype(jnp.float32),
        lax.psum(spread(owned_router_out).astype(jnp.bfloat16), "rep").astype(jnp.float32),
        lax.psum(spread(grad_adapt_in).astype(jnp.bfloat16), "rep").astype(jnp.float32),
        lax.psum(spread(grad_adapt_out).astype(jnp.bfloat16), "rep").astype(jnp.float32),
        lax.psum(spread(grad_down_in).astype(jnp.bfloat16), "rep").astype(jnp.float32),
        lax.psum(spread(grad_down_out).astype(jnp.bfloat16), "rep").astype(jnp.float32),
    )
    return (
        result,
        grad_input,
        grad_a_qkv,
        grad_b_query,
        grad_b_keyval,
        grad_a_output,
        grad_b_output,
        grad_a_router,
        grad_b_router,
        grad_a_gateup,
        grad_b_gateup,
        grad_a_down,
        grad_b_down,
    )


def solution(mesh):
    in_specs = (
        P(("rep", "grp"), None),
        P(("rep", "grp"), None),
        P(("rep", "grp"), None),
        P(("rep", "grp")),
        P("rep", None),
        P("rep"),
        P("grp", None),
        P("grp", None),
        P("grp", None),
        P("grp", None),
        P("grp"),
        P("grp"),
        P("grp", None, None),
        P("grp", None, None),
        P(None, "grp", None),
        P(None, None, "grp"),
        P(None, None, None, "grp"),
        P(None, "grp", None),
        P(None, None, "grp"),
        P(None, "grp", None),
        P(None, None, "grp"),
        P(None, "grp", None, None),
        P(None, "grp", None, None, None),
        P(None, "grp", None, None),
        P(None, "grp", None, None),
    )
    out_specs = (
        P(("rep", "grp"), None),
        P(("rep", "grp"), None),
        P(None, "grp", None),
        P(None, None, "grp"),
        P(None, None, None, "grp"),
        P(None, "grp", None),
        P(None, None, "grp"),
        P(None, "grp", None),
        P(None, None, "grp"),
        P(None, "grp", None, None),
        P(None, "grp", None, None, None),
        P(None, "grp", None, None),
        P(None, "grp", None, None),
    )
    return jax.shard_map(local, mesh=mesh, in_specs=in_specs, out_specs=out_specs, check_vma=False)
```

profile of v0, /device:TPU:0, one launch (start us, length us, event | category | flops | bytes accessed | tf_op | source)
XLA Modules:
  0.0 2035.9 jit_solution(8938011380563626346)
XLA Ops:
  31.1 26.9 %all-gather.16.cloned.1.call-done = bf16[1536,1024]{1,0:T(8,128)(2,1)} async-done(((bf16[768,1024]{1,0:T(8,128)(2,1)}), bf16[1536,1024]{1,0:T(8,128)(2,1)}) %all-gather.16.cloned.1.call-update) | async-done | bytes 3145744 | tf_op jit(solution)/shard_map/all_gather | solution.py:178
  130.9 44.9 %all-gather.22.cloned.1.call-done = bf16[1536,1536]{1,0:T(8,128)(2,1)} async-done(((bf16[768,1536]{1,0:T(8,128)(2,1)}), bf16[1536,1536]{1,0:T(8,128)(2,1)}) %all-gather.22.cloned.1.call-update) | async-done | bytes 4718608 | tf_op jit(solution)/shard_map/all_gather | solution.py:177
  185.3 77.3 %while.47 = (s32[]{:T(128)}, bf16[8,512,3,64]{1,3,2,0:T(8,128)(2,1)}, f32[8,3,512]{2,1,0:T(4,128)}, bf16[8,1024,64]{1,2,0:T(8,128)(2,1)}, bf16[8,1024,64]{1,2,0:...) while((s32[]{:T(128)}, ...), condition=%wide.region_7.8_spmd.clone, body=%wide.region_4.7_spmd.clone.sunk | while | flops 425818624 | bytes 22738580 | solution.py:233
  274.4 29.1 %scatter_custom_fusion = bf16[5720,1536]{1,0:T(8,128)(2,1)} fusion(s32[4096]{0:T(1024)S(1)} %bitcast.431, bf16[]{:T(256)} %constant.129.clone.1, bf16[512,1536]{1,0:T(8,128)(2,1)} %multiply_convert_fusion.6), kind=kCustom, calls=%fused_computation.99 | custom fusion | bytes 19144706 | tf_op jit(solution)/shard_map/scatter | solution.py:253
  330.3 191.6 %all-gather.6 = bf16[1,16,40]{1,0,2:T(2,128)(2,1)S(1)} all-gather(bf16[1,16,20]{1,0,2:T(2,128)(2,1)S(1)} %copy.193), channel_id=8, replica_groups=mesh['rep'=16,'grp'=2] {'grp'}, dimensions={2}, use_global_device_ids=true | all-gather | bytes 1920 | tf_op jit(solution)/shard_map/all_gather | solution.py:189
  538.1 30.5 %scatter_custom_fusion.1 = bf16[5720,1536]{1,0:T(8,128)(2,1)} fusion(s32[4096]{0:T(1024)S(1)} %bitcast.432, f32[512,1536]{1,0:T(8,128)} %convert_element_type.311, f32[4096]{0:T(1024)S(1)} %div.94, bf16[]{:T(256)} %constant.129.clone.1), kind=kCustom, calls=%fused_computation.98 | custom fusion | flops 12582912 | bytes 20733954 | tf_op jit(solution)/shard_map/scatter | solution.py:287
  611.1 20.8 %reshape.425 = bf16[20,286,1536]{2,1,0:T(8,128)(2,1)} reshape(bf16[1,20,2,1,143,1536]{5,4,2,1,3,0:T(8,128)(2,1)} %copy.174) | data formatting | bytes 35143680 | tf_op jit(solution)/shard_map/reshape | solution.py:257
  640.9 35.7 %fusion.199 = f32[20,286,1024]{2,1,0:T(8,128)} fusion(bf16[20,286,1536]{2,1,0:T(8,128)(2,1)} %reshape.425, bf16[20,1536,1024]{2,1,0:T(8,128)(2,1)} %param.43), kind=kOutput, calls=%fused_computation.312 | convolution fusion | flops 17993564160 | bytes 103915520 | tf_op jit(solution)/shard_map/erd,edf->erf/dot_general | solution.py:102
  676.6 107.5 %all-to-all-done.2 = bf16[2,20,1,143,1536]{4,3,1,2,0:T(8,128)(2,1)} async-done(((bf16[2,20,1,143,1536]{4,3,1,2,0:T(8,128)(2,1)}), bf16[2,20,1,143,1536]{4,3,1,2,0:T(8,128)(2,1)}, u32[]{:S(2)}, u32[]{:S(2)}) %all-to-all-start.2) | async-done | bytes 17571872 | tf_op jit(solution)/shard_map/all_to_all | solution.py:297
  800.0 20.8 %reshape.429 = bf16[20,286,1536]{2,1,0:T(8,128)(2,1)} reshape(bf16[1,20,2,1,143,1536]{5,4,2,1,3,0:T(8,128)(2,1)} %copy.179) | data formatting | bytes 35143680 | tf_op jit(solution)/shard_map/reshape | solution.py:300
  829.4 23.1 %fusion.201 = f32[20,286,512]{2,1,0:T(8,128)} fusion(bf16[20,286,1536]{2,1,0:T(8,128)(2,1)} %reshape.429, bf16[20,512,1536]{2,1,0:T(8,128)(2,1)} %param.44), kind=kOutput, calls=%fused_computation.314 | convolution fusion | flops 8996782080 | bytes 60743680 | tf_op jit(solution)/shard_map/erd,efd->erf/dot_general | solution.py:305
  864.5 22.5 %multiply_convert_fusion.2 = (bf16[20,286,512]{2,1,0:T(8,128)(2,1)}, bf16[20,286,512]{2,1,0:T(8,128)(2,1)}, bf16[20,286,512]{2,1,0:T(8,128)(2,1)}) fusion(f32[20,286,512]{2,1,0:T(8,128)} %fusion.201, f32[20,286,512]{2,1,0:T(8,128)S(1)} %fusion.128, f32[20,286,512]{2,1,0:T(8,128)} %fusion.133, f32[20,286,1024]{2,1,0:T(8,128)} %fusion.199, ...), kind=kOutput, calls=%fused_computation.110 | convolution fusion | flops 149360640 | bytes 76800000 | tf_op jit(solution)/shard_map/erk,ekf->erf/dot_general | solution.py:106
  886.9 28.0 %fusion.200 = f32[20,286,1536]{2,1,0:T(8,128)} fusion(bf16[20,286,512]{2,1,0:T(8,128)(2,1)} %get-tuple-element.464, bf16[20,512,1536]{2,1,0:T(8,128)(2,1)} %param.44), kind=kOutput, calls=%fused_computation.313 | convolution fusion | flops 8996782080 | bytes 72458240 | tf_op jit(solution)/shard_map/erf,efd->erd/dot_general | solution.py:116
  939.9 20.8 %reshape.426 = bf16[1,20,2,143,1536]{4,3,2,1,0:T(8,128)(2,1)} reshape(bf16[20,286,1536]{2,1,0:T(8,128)(2,1)} %add_convert_fusion.1) | data formatting | bytes 35143680 | tf_op jit(solution)/shard_map/reshape | solution.py:266
  995.6 40.9 %fusion.83 = f32[20,286,1536]{2,1,0:T(8,128)} fusion(bf16[20,1536,1024]{2,1,0:T(8,128)(2,1)} %param.43, bf16[20,286,512]{2,1,0:T(8,128)(2,1)} %get-tuple-element.465, bf16[20,286,512]{2,1,0:T(8,128)(2,1)} %get-tuple-element.463), kind=kOutput, calls=%fused_computation.105 | convolution fusion | flops 18016993280 | bytes 109772800 | tf_op jit(solution)/shard_map/erf,edf->erd/dot_general | solution.py:326
  1036.6 25.5 %add_convert_fusion = bf16[20,286,1536]{2,1,0:T(8,128)(2,1)} fusion(f32[20,286,1536]{2,1,0:T(8,128)} %fusion.83, bf16[4,20,1536,32]{2,3,1,0:T(8,128)(2,1)} %param.52, s32[]{:T(128)S(6)} %select_n.85, f32[20,286,16]{1,2,0:T(8,128)S(1)} %fusion.132, f32[20,286,16]{1,2,0:T(8,128)S(1)} %fusion.131), kind=kOutput, calls=%fused_computation.88 | convolution fusion | flops 3391548160 | bytes 55659524 | tf_op jit(solution)/shard_map/erk,edk->erd/dot_general | solution.py:334
  1098.7 76.4 %all-to-all-done.1 = bf16[1,20,2,143,1536]{4,3,1,0,2:T(8,128)(2,1)} async-done(((bf16[1,20,2,143,1536]{4,3,1,0,2:T(8,128)(2,1)}), bf16[1,20,2,143,1536]{4,3,1,0,2:T(8,128)(2,1)}, u32[]{:S(2)}, u32[]{:S(2)}) %all-to-all-start.1) | async-done | bytes 17571872 | tf_op jit(solution)/shard_map/all_to_all | solution.py:265
  1217.6 33.5 %gather_fusion = bf16[4096,1536]{1,0:T(8,128)(2,1)} fusion(bf16[5720,1536]{1,0:T(8,128)(2,1)} %reshape.427, s32[4096]{0:T(1024)S(1)} %broadcast_clamp_fusion), kind=kCustom, calls=%fused_computation | custom fusion | bytes 25182208 | tf_op jit(solution)/shard_map/gather | solution.py:273
  1270.3 103.1 %all-to-all-done.3 = bf16[1,20,2,143,1536]{4,3,1,0,2:T(8,128)(2,1)} async-done(((bf16[1,20,2,143,1536]{4,3,1,0,2:T(8,128)(2,1)}), bf16[1,20,2,143,1536]{4,3,1,0,2:T(8,128)(2,1)}, u32[]{:S(2)}, u32[]{:S(2)}) %all-to-all-start.3) | async-done | bytes 17571872 | tf_op jit(solution)/shard_map/all_to_all | solution.py:352
  1389.2 33.5 %gather_fusion.1 = bf16[4096,1536]{1,0:T(8,128)(2,1)} fusion(bf16[5720,1536]{1,0:T(8,128)(2,1)} %reshape.431, s32[4096]{0:T(1024)S(1)} %broadcast_clamp_fusion), kind=kCustom, calls=%fused_computation.1 | custom fusion | bytes 25182208 | tf_op jit(solution)/shard_map/gather | solution.py:360
  1448.3 138.0 %while.48 = (s32[]{:T(128)}, bf16[8,512,3,64]{1,3,2,0:T(8,128)(2,1)S(1)}, bf16[8,1024,64]{1,2,0:T(8,128)(2,1)}, bf16[8,1024,64]{1,2,0:T(8,128)(2,1)}, bf16[8,102...) while((s32[]{:T(128)}, ...), condition=%wide.region_25.26_spmd.clone, body=%wide.region_23.25_spmd.clone.sunk | while | flops 1034582528 | bytes 52486320 | solution.py:451
  1649.3 21.4 %reduce-scatter.12.cloned.1.call-done = bf16[512,512]{0,1:T(8,128)(2,1)} async-done(((bf16[1024,512]{0,1:T(8,128)(2,1)}), bf16[512,512]{0,1:T(8,128)(2,1)}) %reduce-scatter.12.cloned.1.call-update) | async-done | bytes 524304 | tf_op jit(solution)/shard_map/reduce_scatter | solution.py:466
  1705.3 63.7 %psum.83 = bf16[4,16,20]{2,1,0:T(8,128)(2,1)S(1)} all-reduce(bf16[4,16,20]{2,1,0:T(8,128)(2,1)S(1)} %multiply_convert_fusion.14), channel_id=1, replica_groups=mesh['rep'=16,'grp'=2] {'rep'}, use_global_device_ids=true, to_apply=%region_42.43 | all-reduce | flops 1280 | bytes 5120 | tf_op jit(solution)/shard_map/psum | solution.py:552
  1780.8 223.1 %all-reduce.4.cloned.1.call-done = (bf16[4,768,48]{1,2,0:T(8,128)(2,1)}, bf16[4,16,768]{2,1,0:T(8,128)(2,1)}, bf16[4,2,16,256]{3,2,1,0:T(8,128)(2,1)}, bf16[4,76...) async-done(((bf16[4,768,48]{1,2,0:T(8,128)(2,1)}, ...) | async-done | bytes 16482320 | tf_op jit(solution)/shard_map/psum | solution.py:546
  (565 shorter events, 796.6 us)
Async XLA Ops:
  7.2 587.7 %copy-start = (bf16[4,20,2,16,512]{4,3,2,1,0:T(8,128)(2,1)S(1)}, bf16[4,20,2,16,512]{4,3,2,1,0:T(8,128)(2,1)}, u32[]{:S(2)}) copy-start(bf16[4,20,2,16,512]{4,3,2,1,0:T(8,128)(2,1)} %param.53) | copy-start | bytes 7864324
  7.2 50.8 %all-gather.16.cloned.1.call-start = ((), (), s32[]{:S(2)}) async-start(), calls=%async_computation.12 | async-start | bytes 4718592 | tf_op jit(solution)/shard_map/all_gather | solution.py:178
  7.9 118.4 %all-gather.18.cloned.1.call-start = ((), (), s32[]{:S(2)}) async-start(), calls=%async_computation.13 | async-start | bytes 1572864 | tf_op jit(solution)/shard_map/all_gather | solution.py:207
  64.7 63.9 %all-gather.20.cloned.1.call-start = ((), (), s32[]{:S(2)}) async-start(), calls=%async_computation.14 | async-start | bytes 1572864 | tf_op jit(solution)/shard_map/all_gather | solution.py:206
  67.1 108.6 %all-gather.22.cloned.1.call-start = ((), (), s32[]{:S(2)}) async-start(), calls=%async_computation.15 | async-start | bytes 7077888 | tf_op jit(solution)/shard_map/all_gather | solution.py:177
  67.7 196.7 %all-gather.24.cloned.1.call-start = ((), (), s32[]{:S(2)}) async-start(), calls=%async_computation.16 | async-start | bytes 7077888 | tf_op jit(solution)/shard_map/all_gather | solution.py:179
  93.1 177.4 %copy-start.53 = (bf16[1,16,1536]{2,1,0:T(8,128)(2,1)}, bf16[1,16,1536]{2,1,0:T(8,128)(2,1)S(1)}, u32[]{:S(2)}) copy-start(bf16[1,16,1536]{2,1,0:T(8,128)(2,1)S(1)} %all-gather.4) | copy-start | bytes 147460
  126.3 411.8 %copy-start.81 = (s32[4096,1]{0,1:T(1,128)}, s32[4096,1]{0,1:T(1,128)S(1)}, u32[]{:S(2)}) copy-start(s32[4096,1]{0,1:T(1,128)S(1)} %compare_select_fusion) | copy-start | bytes 49156
  319.4 265.1 %all-to-all-start = ((bf16[2,20,1,143,1536]{4,3,1,2,0:T(8,128)(2,1)}), bf16[2,20,1,143,1536]{4,3,1,2,0:T(8,128)(2,1)}, u32[]{:S(2)}, u32[]{:S(2)}) async-start(bf16[2,20,1,143,1536]{4,3,1,2,0:T(8,128)(2,1)} %bitcast.414), calls=%async_computation | async-start | bytes 35389440 | tf_op jit(solution)/shard_map/all_to_all | solution.py:256
  329.5 201.4 %copy-start.83 = (bf16[768,40]{0,1:T(8,128)(2,1)S(1)}, bf16[768,40]{0,1:T(8,128)(2,1)}, u32[]{:S(2)}) copy-start(bf16[768,40]{0,1:T(8,128)(2,1)} %param.40) | copy-start | bytes 184324
  584.5 199.5 %all-to-all-start.2 = ((bf16[2,20,1,143,1536]{4,3,1,2,0:T(8,128)(2,1)}), bf16[2,20,1,143,1536]{4,3,1,2,0:T(8,128)(2,1)}, u32[]{:S(2)}, u32[]{:S(2)}) async-start(bf16[2,20,1,143,1536]{4,3,1,2,0:T(8,128)(2,1)} %bitcast.415), calls=%async_computation.2 | async-start | bytes 35389440 | tf_op jit(solution)/shard_map/all_to_all | solution.py:297
  594.9 257.6 %copy-start.21 = (bf16[20,2,16,512]{3,2,0,1:T(8,128)(2,1)}, bf16[20,2,16,512]{3,2,0,1:T(8,128)(2,1)S(1)}, u32[]{:S(2)}) copy-start(bf16[20,2,16,512]{3,2,0,1:T(8,128)(2,1)S(1)} %copy_bitcast_fusion) | copy-start | bytes 1966084
  640.9 223.5 %copy-start.35 = (bf16[20,286,32]{1,2,0:T(8,128)(2,1)}, bf16[20,286,32]{1,2,0:T(8,128)(2,1)S(1)}, u32[]{:S(2)}) copy-start(bf16[20,286,32]{1,2,0:T(8,128)(2,1)S(1)} %fusion.111) | copy-start | bytes 1098244
  976.7 198.4 %all-to-all-start.1 = ((bf16[1,20,2,143,1536]{4,3,1,0,2:T(8,128)(2,1)}), bf16[1,20,2,143,1536]{4,3,1,0,2:T(8,128)(2,1)}, u32[]{:S(2)}, u32[]{:S(2)}) async-start(bf16[1,20,2,143,1536]{4,3,1,0,2:T(8,128)(2,1)} %copy.176), calls=%async_computation.1 | async-start | bytes 35389440 | tf_op jit(solution)/shard_map/all_to_all | solution.py:265
  1175.1 198.2 %all-to-all-start.3 = ((bf16[1,20,2,143,1536]{4,3,1,0,2:T(8,128)(2,1)}), bf16[1,20,2,143,1536]{4,3,1,0,2:T(8,128)(2,1)}, u32[]{:S(2)}, u32[]{:S(2)}) async-start(bf16[1,20,2,143,1536]{4,3,1,0,2:T(8,128)(2,1)} %copy.180), calls=%async_computation.3 | async-start | bytes 35389440 | tf_op jit(solution)/shard_map/all_to_all | solution.py:352
  1185.5 445.6 %reduce-scatter.24.cloned.1.call-start = ((), (), s32[]{:S(2)}) async-start(), calls=%async_computation.24 | async-start | bytes 73728 | tf_op jit(solution)/shard_map/reduce_scatter | solution.py:521
  1270.0 362.0 %reduce-scatter.20.cloned.1.call-start = ((), (), s32[]{:S(2)}) async-start(), calls=%async_computation.22 | async-start | bytes 73728 | tf_op jit(solution)/shard_map/reduce_scatter | solution.py:515
  1590.3 42.5 %reduce-scatter.22.cloned.1.call-start = ((), (), s32[]{:S(2)}) async-start(), calls=%async_computation.23 | async-start | bytes 73728 | tf_op jit(solution)/shard_map/reduce_scatter | solution.py:518
  1593.2 40.3 %reduce-scatter.16.cloned.1.call-start = ((), (), s32[]{:S(2)}) async-start(), calls=%async_computation.20 | async-start | bytes 73728 | tf_op jit(solution)/shard_map/reduce_scatter | solution.py:509
  1595.2 52.8 %reduce-scatter.10.cloned.1.call-start = ((), (), s32[]{:S(2)}) async-start(), calls=%async_computation.17 | async-start | bytes 1572864 | tf_op jit(solution)/shard_map/reduce_scatter | solution.py:463
  1598.8 71.9 %reduce-scatter.12.cloned.1.call-start = ((), (), s32[]{:S(2)}) async-start(), calls=%async_computation.18 | async-start | bytes 1572864 | tf_op jit(solution)/shard_map/reduce_scatter | solution.py:466
  1621.9 61.3 %reduce-scatter.18.cloned.1.call-start = ((), (), s32[]{:S(2)}) async-start(), calls=%async_computation.21 | async-start | bytes 49152 | tf_op jit(solution)/shard_map/reduce_scatter | solution.py:512
  1672.7 23.8 %reduce-scatter.14.cloned.1.call-start = ((), (), s32[]{:S(2)}) async-start(), calls=%async_computation.19 | async-start | bytes 221184 | tf_op jit(solution)/shard_map/reduce_scatter | solution.py:506
  1677.0 326.9 %all-reduce.4.cloned.1.call-start = ((), (), s32[]{:S(2)}) async-start(), calls=%async_computation.25 | async-start | bytes 32964608 | tf_op jit(solution)/shard_map/psum | solution.py:546
  (99 other events, 2155.6 us)
Sparse Core Ops, SparseCore 0:
  9.6 48.4 all-gather.15
  64.8 23.1 all-gather.17
  90.2 21.4 all-gather.19
  113.1 62.6 all-gather.21
  177.2 62.6 all-gather.23
  1270.1 11.2 reduce-scatter.23
  1590.4 9.7 reduce-scatter.19
  1603.0 9.8 reduce-scatter.21
  1615.6 9.8 reduce-scatter.15
  1627.6 20.3 reduce-scatter.9
  1650.4 20.3 reduce-scatter.11
  1673.3 9.8 reduce-scatter.17
  1686.0 10.4 reduce-scatter.13
  1703.7 300.1 all-reduce.3
where the time goes:
time: 2050 us; the launch traced here: 2040 us
  waiting for transfers between devices  636 us (31%)
  matrix products  487 us (24%)
  local copies, waits for them, and re-layouts  346 us (17%)
  blocking collectives  309 us (15%)
  other arithmetic  199 us (10%)
  starting transfers between devices  41.7 us (2%)
    psum x1, waiting for transfers between devices, local(): lax.psum(spread(owned_qkv_in).astype(jnp.bfloat16), 'rep')  223 us
    all_gather x1, blocking collectives, local(): lax.all_gather(b_router[chosen], 'grp', axis=1, tiled=True)  192 us
    all_to_all x1, waiting for transfers between devices, local(): lax.all_to_all(d_outgoing, 'grp', split_axis=0, concat_axis=2, tiled=True)  107 us
    all_to_all x1, waiting for transfers between devices, local(): lax.all_to_all(d_rows.reshape(1, experts_dev, groups, capacity, width), '...  103 us
    all_to_all x1, waiting for transfers between devices, local(): lax.all_to_all(expert_out.reshape(1, experts_dev, groups, capacity, width...  76.4 us
    psum x1, blocking collectives, local(): lax.psum(spread(owned_router_out).astype(jnp.bfloat16), 'rep')  63.7 us
    all_gather x1, waiting for transfers between devices, local(): lax.all_gather(w_query, 'grp', axis=0, tiled=True)  44.9 us
  transfers between devices with their start and end apart: 18, of which 10 were waited for; matrix products, arithmetic and copies ran while one was open for 37% of the time, Pallas kernels for 0%

commit v1 on v0

v1 whole, which is shorter than its diff:
```python
import functools

import jax
import jax.numpy as jnp
from jax import lax
from jax.experimental import pallas as pl
from jax.experimental.pallas import tpu as pltpu
from jax.sharding import PartitionSpec as P

QUERY_HEADS = 24
KEY_VALUE_HEADS = 8
HEAD_SIZE = 64
FF = 512
TOPK = 8
RANK = 16
SEG = 128
FLUSH = 5
LANES = 512

EPSILON = 1e-05
BF16 = jnp.bfloat16
F32 = jnp.float32


def product(left, right):
    return jnp.dot(left, right, preferred_element_type=F32)


def product_back(left, right):
    return lax.dot_general(left, right, (((1,), (1,)), ((), ())), preferred_element_type=F32)


def product_outer(left, right):
    return lax.dot_general(left, right, (((0,), (0,)), ((), ())), preferred_element_type=F32)


def rms_norm(value_rows, gain):
    return (
        value_rows
        * lax.rsqrt(jnp.mean(value_rows * value_rows, axis=-1, keepdims=True) + EPSILON)
        * gain
    )


def rms_back(value_rows, gain, upstream):
    factor = lax.rsqrt(jnp.mean(value_rows * value_rows, axis=-1, keepdims=True) + EPSILON)
    scaled = value_rows * factor
    incoming = upstream * gain
    return factor * (incoming - scaled * jnp.mean(incoming * scaled, axis=-1, keepdims=True))


def ancestry(parent_row):
    total = parent_row.shape[0]
    labels = jnp.arange(total, dtype=jnp.int32)

    def climb(count, state):
        current, table = state
        current = jnp.sum(
            jnp.where(current[:, None] == labels[None, :], parent_row[None, :], 0), axis=1
        )
        table = jnp.maximum(table, (current[:, None] == labels[None, :]).astype(jnp.int32))
        return (current, table)

    start_index = (labels[:, None] == labels[None, :]).astype(jnp.int32)
    return lax.fori_loop(0, total, climb, (labels, start_index))[1]


def tree_mask(parent_row, pad_row, first, count, tree_length):
    table = ancestry(parent_row)
    segs_here = count // SEG
    segs_all = tree_length // SEG
    rows = lax.dynamic_slice_in_dim(table, first // SEG, segs_here, 0)
    linked = jnp.broadcast_to(rows[:, None, :, None] > 0, (segs_here, SEG, segs_all, SEG)).reshape(
        count, tree_length
    )
    query_pos = first + jnp.arange(count, dtype=jnp.int32)
    key_pos = jnp.arange(tree_length, dtype=jnp.int32)
    same = query_pos[:, None] // SEG == key_pos[None, :] // SEG
    causal = jnp.logical_or(jnp.logical_not(same), key_pos[None, :] <= query_pos[:, None])
    live = jnp.logical_or(pad_row[None, :] > 0, key_pos[None, :] == query_pos[:, None])
    return jnp.logical_and(jnp.logical_and(linked, causal), live)


def expert_kernel(
    chosen_ref,
    x_ref,
    g_ref,
    pos_ref,
    gate_ref,
    w1_ref,
    w2_ref,
    a1_ref,
    b1_ref,
    a2_ref,
    b2_ref,
    r_out,
    d_out,
    dg_out,
    grad_out,
    hot_s,
    o_s,
    dx_s,
    accr,
    accd,
    x_s,
    g_s,
    gate_s,
    b1_s,
    dgu_s,
    *,
    blocks,
    rows_block,
    cap,
    flush,
):
    e = pl.program_id(0)
    slot = lax.rem(e, flush)
    width = x_ref.shape[-1]

    @pl.when(e == 0)
    def _():
        b1_s[...] = jnp.zeros_like(b1_s)
        accr[...] = jnp.zeros_like(accr)
        accd[...] = jnp.zeros_like(accd)

    at = pl.multiple_of(slot * cap, 16)
    for b in range(blocks):
        here = pl.ds(b * rows_block, rows_block)
        there = pl.ds(b * cap, cap)
        places = lax.broadcasted_iota(jnp.int32, (cap, rows_block), 0)
        hit = places == pos_ref[0, b : b + 1, :]
        hot = hit.astype(F32).astype(BF16)
        hot_s[b, pl.ds(at, cap), :] = hot
        x_s[there, :] = product(hot, x_ref[here, :]).astype(BF16)
        g_s[there, :] = product(hot, g_ref[here, :]).astype(BF16)
        gate_s[there, :] = jnp.sum(
            jnp.where(hit, gate_ref[0, b : b + 1, :], 0.0), axis=1, keepdims=True
        )
    b1_s[0:RANK, 0:FF] = b1_ref[0, 0, 0]
    b1_s[RANK : 2 * RANK, FF : 2 * FF] = b1_ref[0, 0, 1]

    x = x_s[...]
    gate_col = gate_s[...]
    rank_in = product_back(x, a1_ref[0, 0]).astype(BF16)
    pre = product(x, w1_ref[0]) + product(rank_in, b1_s[...])
    gate_pre = pre[:, :FF]
    up_pre = pre[:, FF:]
    sig = 1.0 / (1.0 + jnp.exp(-gate_pre))
    act = gate_pre * sig
    hidden = (act * up_pre).astype(BF16)
    rank_down = product_back(hidden, a2_ref[0, 0]).astype(BF16)
    out = (product(hidden, w2_ref[0]) + product(rank_down, b2_ref[0, 0])).astype(BF16).astype(F32)
    g = g_s[...].astype(F32)
    d_gate_col = jnp.sum(g * out, axis=1, keepdims=True)
    out = (gate_col * out).astype(BF16)
    d_exp = (gate_col * g).astype(BF16)
    d_rank_down = product_back(d_exp, b2_ref[0, 0]).astype(BF16)
    d_hidden = product_back(d_exp, w2_ref[0]) + product(d_rank_down, a2_ref[0, 0])
    dgu_s[:, :FF] = (d_hidden * up_pre * sig * (1.0 + gate_pre * (1.0 - sig))).astype(BF16)
    dgu_s[:, FF:] = (d_hidden * act).astype(BF16)
    dgu = dgu_s[...]
    d_rank_in = product_back(dgu, b1_s[...]).astype(BF16)
    dx = (product_back(dgu, w1_ref[0]) + product(d_rank_in, a1_ref[0, 0])).astype(BF16)
    for b in range(blocks):
        o_s[b, pl.ds(at, cap), :] = out[b * cap : (b + 1) * cap]
        dx_s[b, pl.ds(at, cap), :] = dx[b * cap : (b + 1) * cap]
        places = lax.broadcasted_iota(jnp.int32, (cap, rows_block), 0)
        hit = places == pos_ref[0, b : b + 1, :]
        dg_out[0, b : b + 1, :] = jnp.sum(
            jnp.where(hit, d_gate_col[b * cap : (b + 1) * cap], 0.0), axis=0, keepdims=True
        )

    grad_a1 = product_outer(d_rank_in, x)
    grad_b1 = product_outer(rank_in, dgu)
    grad_a2 = product_outer(d_rank_down, hidden)
    grad_b2 = product_outer(rank_down, d_exp)
    parts = width // LANES
    base = 0
    for i in range(parts):
        grad_out[0, base : base + 2 * RANK, :] = grad_a1[:, i * LANES : (i + 1) * LANES].astype(BF16)
        base += 2 * RANK
    grad_out[0, base : base + RANK, :] = grad_b1[:RANK, :FF].astype(BF16)
    base += RANK
    grad_out[0, base : base + RANK, :] = grad_b1[RANK:, FF:].astype(BF16)
    base += RANK
    grad_out[0, base : base + RANK, :] = grad_a2.astype(BF16)
    base += RANK
    for i in range(parts):
        grad_out[0, base : base + RANK, :] = grad_b2[:, i * LANES : (i + 1) * LANES].astype(BF16)
        base += RANK

    @pl.when(slot == flush - 1)
    def _():
        for b in range(blocks):
            here = pl.ds(b * rows_block, rows_block)
            accr[here, :] += product_outer(hot_s[b], o_s[b])
            accd[here, :] += product_outer(hot_s[b], dx_s[b])

    @pl.when(e == pl.num_programs(0) - 1)
    def _():
        r_out[...] = accr[...].astype(BF16)
        d_out[...] = accd[...].astype(BF16)


def grad_rows(width):
    return (width // LANES) * 3 * RANK + 3 * RANK


def run_experts(chosen, x, g, pos, gate, w1, w2, a1, b1, a2, b2, cap):
    experts, blocks, rows_block = pos.shape
    width = x.shape[1]
    tokens = x.shape[0]
    rows = blocks * cap
    stored = grad_rows(width)
    flush = FLUSH if experts % FLUSH == 0 else 1
    whole = lambda e, c: (0, 0)
    lead = lambda e, c: (e, 0, 0)
    return pl.pallas_call(
        functools.partial(
            expert_kernel, blocks=blocks, rows_block=rows_block, cap=cap, flush=flush
        ),
        grid_spec=pltpu.PrefetchScalarGridSpec(
            num_scalar_prefetch=1,
            grid=(experts,),
            in_specs=[
                pl.BlockSpec((tokens, width), whole, pipeline_mode=pl.Buffered(1)),
                pl.BlockSpec((tokens, width), whole, pipeline_mode=pl.Buffered(1)),
                pl.BlockSpec((1, blocks, rows_block), lead),
                pl.BlockSpec((1, blocks, rows_block), lead),
                pl.BlockSpec((1, width, 2 * FF), lead),
                pl.BlockSpec((1, FF, width), lead),
                pl.BlockSpec((1, 1, 2 * RANK, width), lambda e, c: (c[0], e, 0, 0)),
                pl.BlockSpec((1, 1, 2, RANK, FF), lambda e, c: (c[0], e, 0, 0, 0)),
                pl.BlockSpec((1, 1, RANK, FF), lambda e, c: (c[0], e, 0, 0)),
                pl.BlockSpec((1, 1, RANK, width), lambda e, c: (c[0], e, 0, 0)),
            ],
            out_specs=[
                pl.BlockSpec((tokens, width), whole, pipeline_mode=pl.Buffered(1)),
                pl.BlockSpec((tokens, width), whole, pipeline_mode=pl.Buffered(1)),
                pl.BlockSpec((1, blocks, rows_block), lead),
                pl.BlockSpec((1, stored, LANES), lead),
            ],
            scratch_shapes=[
                pltpu.VMEM((blocks, flush * cap, rows_block), BF16),
                pltpu.VMEM((blocks, flush * cap, width), BF16),
                pltpu.VMEM((blocks, flush * cap, width), BF16),
                pltpu.VMEM((tokens, width), F32),
                pltpu.VMEM((tokens, width), F32),
                pltpu.VMEM((rows, width), BF16),
                pltpu.VMEM((rows, width), BF16),
                pltpu.VMEM((rows, 1), F32),
                pltpu.VMEM((2 * RANK, 2 * FF), BF16),
                pltpu.VMEM((rows, 2 * FF), BF16),
            ],
        ),
        out_shape=[
            jax.ShapeDtypeStruct((tokens, width), BF16),
            jax.ShapeDtypeStruct((tokens, width), BF16),
            jax.ShapeDtypeStruct((experts, blocks, rows_block), F32),
            jax.ShapeDtypeStruct((experts, stored, LANES), BF16),
        ],
        compiler_params=pltpu.CompilerParams(
            vmem_limit_bytes=62 * 1024 * 1024, dimension_semantics=("arbitrary",)
        ),
        cost_estimate=pl.CostEstimate(
            flops=120_000_000_000 * experts // 20,
            bytes_accessed=5_000_000 * experts,
            transcendentals=rows * FF * experts,
        ),
        name="experts",
    )(chosen, x, g, pos, gate, w1, w2, a1, b1, a2, b2)


def swap_pairs(size):
    return [(i, i ^ 1) for i in range(size)]


def gather_rows(half, groups):
    if groups != 2:
        return lax.all_gather(half, "grp", axis=0, tiled=True)
    rows = half.shape[0] // 2
    core = lax.axis_index("rep") % 2
    member = lax.axis_index("grp")
    mine = lax.dynamic_slice_in_dim(half, core * rows, rows, 0)
    got = lax.ppermute(mine, "grp", swap_pairs(2))
    other = lax.ppermute(got, "rep", swap_pairs(lax.axis_size("rep")))
    out = jnp.zeros((4 * rows,) + half.shape[1:], half.dtype)
    out = lax.dynamic_update_slice_in_dim(out, half, member * 2 * rows, 0)
    away = (1 - member) * 2 * rows
    out = lax.dynamic_update_slice_in_dim(out, got, away + core * rows, 0)
    return lax.dynamic_update_slice_in_dim(out, other, away + (1 - core) * rows, 0)


def pack(pieces, multiple):
    flat = jnp.concatenate([piece.reshape(-1) for piece in pieces])
    return jnp.pad(flat, (0, -flat.shape[0] % multiple))


def unpack(flat, shapes):
    out = []
    offset = 0
    for shape in shapes:
        size = 1
        for extent in shape:
            size *= extent
        out.append(flat[..., offset : offset + size].reshape(flat.shape[:-1] + shape))
        offset += size
    return out


def local(
    tokens,
    cotangent,
    routes,
    padding,
    parents,
    adapter_ids,
    w_query,
    w_keyval,
    w_output,
    w_router,
    gain_attn,
    gain_ffn,
    w_gateup,
    w_down,
    a_qkv,
    b_query,
    b_keyval,
    a_output,
    b_output,
    a_router,
    b_router,
    a_gateup,
    b_gateup,
    a_down,
    b_down,
):
    groups = lax.axis_size("grp")
    reps = lax.axis_size("rep")
    member = lax.axis_index("grp")
    count = tokens.shape[0]
    width = tokens.shape[1]
    part = width // groups
    tree_length = count * groups
    experts_dev = w_gateup.shape[0]
    experts = experts_dev * groups
    capacity = count * TOPK * 7 // (experts * 5)
    cap = -(-capacity // 16) * 16
    kv_width = KEY_VALUE_HEADS * HEAD_SIZE
    per_kv = QUERY_HEADS // KEY_VALUE_HEADS
    scale = HEAD_SIZE ** (-0.5)
    chosen = adapter_ids[0]
    first = member * count
    adapters = a_qkv.shape[0]

    shapes = (
        (3 * RANK, part),
        (RANK, part),
        (2, RANK, kv_width // groups),
        (RANK, part),
        (RANK, part),
        (RANK, part),
        (RANK, experts_dev),
        (experts, part),
        (part,),
        (part,),
        (count,),
    )
    small = pack(
        (
            a_qkv[chosen].T,
            b_query[chosen],
            b_keyval[chosen],
            a_output[chosen].T,
            b_output[chosen],
            a_router[chosen].T,
            b_router[chosen],
            w_router.T,
            gain_attn,
            gain_ffn,
            padding.astype(BF16),
        ),
        1024,
    )
    small_all = lax.all_gather(small, "grp", axis=0)

    def join(piece):
        return jnp.moveaxis(piece, 0, -2).reshape(piece.shape[1:-1] + (-1,))

    (
        qkv_in,
        query_out,
        keyval_out,
        output_in,
        output_out,
        router_in,
        router_out,
        router_full,
        attn_gain,
        ffn_gain,
        pad_all,
    ) = [join(piece) for piece in unpack(small_all, shapes)]
    attn_gain = attn_gain.astype(F32)
    ffn_gain = ffn_gain.astype(F32)
    keyval_full = gather_rows(w_keyval, groups)
    query_full = gather_rows(w_query, groups)
    output_full = gather_rows(w_output, groups)
    routes_all = lax.all_gather(routes, "grp", axis=0)
    upstream_all = lax.all_gather(cotangent, "grp", axis=0, tiled=True)
    ids_all = lax.all_gather(adapter_ids, "rep", axis=0, tiled=True)

    tokens_f = tokens.astype(F32)
    normed = rms_norm(tokens_f, attn_gain).astype(BF16)
    low_rank = product_back(normed, qkv_in).astype(BF16)
    query_rows = (product(normed, query_full) + product(low_rank[:, :RANK], query_out)).astype(BF16)
    keyvals = product(normed, keyval_full)
    key_rows = (keyvals[:, :kv_width] + product(low_rank[:, RANK : 2 * RANK], keyval_out[0])).astype(BF16)
    value_rows = (keyvals[:, kv_width:] + product(low_rank[:, 2 * RANK :], keyval_out[1])).astype(BF16)
    keyval_all = lax.all_gather(
        jnp.concatenate([key_rows, value_rows], axis=1), "grp", axis=0, tiled=True
    )
    every_key = keyval_all[:, :kv_width]
    every_value = keyval_all[:, kv_width:]
    mask = tree_mask(parents[0], pad_all, first, count, tree_length)
    heads_of_query = query_rows.reshape(count, KEY_VALUE_HEADS, per_kv, HEAD_SIZE).transpose(1, 0, 2, 3)
    heads_of_key = every_key.reshape(tree_length, KEY_VALUE_HEADS, HEAD_SIZE).transpose(1, 0, 2)
    heads_of_value = every_value.reshape(tree_length, KEY_VALUE_HEADS, HEAD_SIZE).transpose(1, 0, 2)

    def attend(operands):
        query_grp, key_grp, value_grp = operands
        scores = jnp.einsum("qrd,kd->rqk", query_grp, key_grp, preferred_element_type=F32) * scale
        scores = jnp.where(mask[None], scores, -1e30)
        top = jnp.max(scores, axis=-1, keepdims=True)
        weights = jnp.exp(scores - top)
        total = jnp.sum(weights, axis=-1, keepdims=True)
        probs = (weights / total).astype(BF16)
        mixed = jnp.einsum("rqk,kd->qrd", probs, value_grp, preferred_element_type=F32)
        return (mixed.astype(BF16), top[..., 0] + jnp.log(total[..., 0]))

    mixed_heads, log_totals = lax.map(attend, (heads_of_query, heads_of_key, heads_of_value))
    attended = mixed_heads.transpose(1, 0, 2, 3).reshape(count, width)
    out_rank = product_back(attended, output_in).astype(BF16)
    middle = tokens_f + product(attended, output_full) + product(out_rank, output_out)
    normed_ffn = rms_norm(middle, ffn_gain).astype(BF16)
    router_rank = product_back(normed_ffn, router_in).astype(BF16)
    logits = product_back(normed_ffn, router_full) + product(router_rank, router_out)

    labels = jnp.arange(experts, dtype=jnp.int32)
    named = jnp.any(routes[:, :, None] == labels, axis=1)
    best = jnp.max(jnp.where(named, logits, -jnp.inf), axis=1, keepdims=True)
    powers = jnp.where(named, jnp.exp(jnp.where(named, logits, best) - best), 0.0)
    gates = powers / jnp.sum(powers, axis=1, keepdims=True)

    mine = member * experts_dev + jnp.arange(experts_dev, dtype=jnp.int32)
    hits = jnp.any(routes_all[:, :, :, None] == mine, axis=2)
    before = (jnp.arange(count)[:, None] > jnp.arange(count)[None, :]).astype(BF16)
    ranks = jnp.einsum("ts,gse->get", before, hits.astype(BF16), preferred_element_type=F32)
    places = jnp.where(hits.transpose(0, 2, 1), ranks.astype(jnp.int32), -1).transpose(1, 0, 2)

    rows_all = lax.all_gather(normed_ffn, "grp", axis=0, tiled=True)
    gates_all = lax.all_gather(gates.T, "grp", axis=0)
    gates_mine = lax.dynamic_slice_in_dim(gates_all, member * experts_dev, experts_dev, 1).transpose(1, 0, 2)
    part_result, part_d, part_gates, expert_grads = run_experts(
        adapter_ids,
        rows_all,
        upstream_all,
        places,
        gates_mine,
        w_gateup,
        w_down,
        a_gateup.swapaxes(2, 3),
        b_gateup,
        a_down.swapaxes(2, 3),
        b_down,
        cap,
    )

    owner_hot = (jnp.arange(adapters, dtype=jnp.int32)[:, None] == ids_all[None, :]).astype(F32)
    stored = expert_grads.shape[1]
    share = experts_dev * stored // reps
    swapped = lax.all_to_all(
        expert_grads.reshape(reps, share, LANES), "rep", split_axis=0, concat_axis=0, tiled=True
    )
    summed = jnp.sum(owner_hot[:, :, None, None] * swapped.astype(F32)[None], axis=1).astype(BF16)
    spread = lax.all_gather(summed, "rep", axis=1).reshape(adapters, experts_dev, stored, LANES)

    def lanes_joined(rows, height):
        return rows.reshape(adapters, experts_dev, -1, height, LANES).swapaxes(2, 3).reshape(
            adapters, experts_dev, height, -1
        )

    parts = width // LANES
    edges = [0, parts * 2 * RANK, parts * 2 * RANK + 2 * RANK, parts * 2 * RANK + 3 * RANK, stored]
    grad_a_gateup = lanes_joined(spread[:, :, : edges[1]], 2 * RANK).swapaxes(2, 3).astype(F32)
    grad_b_gateup = spread[:, :, edges[1] : edges[2]].reshape(adapters, experts_dev, 2, RANK, FF).astype(F32)
    grad_a_down = spread[:, :, edges[2] : edges[3]].swapaxes(2, 3).astype(F32)
    grad_b_down = lanes_joined(spread[:, :, edges[3] :], RANK).astype(F32)

    both = lax.psum_scatter(
        jnp.concatenate([part_d, part_result], axis=1), "grp", scatter_dimension=0, tiled=True
    ).astype(F32)
    d_gates = lax.all_to_all(part_gates, "grp", split_axis=1, concat_axis=0, tiled=True)
    d_gates = d_gates.reshape(experts, count).T
    result = (middle + both[:, width:]).astype(BF16)
    upstream = cotangent.astype(F32)
    d_logits = (gates * (d_gates - jnp.sum(gates * d_gates, axis=1, keepdims=True))).astype(BF16)

    d_router_rank = product_back(d_logits, router_out).astype(BF16)
    d_normed_ffn = both[:, :width] + product(d_logits, router_full) + product(d_router_rank, router_in)
    grad_router_out = product_outer(router_rank, d_logits)
    grad_router_in = product_outer(d_router_rank, normed_ffn)
    d_middle = upstream + rms_back(middle, ffn_gain, d_normed_ffn)
    d_attn = d_middle.astype(BF16)
    d_out_rank = product_back(d_attn, output_out).astype(BF16)
    attended_gradient = (product_back(d_attn, output_full) + product(d_out_rank, output_in)).astype(BF16)
    grad_output_out = product_outer(out_rank, d_attn)
    grad_output_in = product_outer(d_out_rank, attended)
    heads_gradient = attended_gradient.reshape(count, KEY_VALUE_HEADS, per_kv, HEAD_SIZE).transpose(1, 0, 2, 3)

    def attend_back(operands):
        query_grp, key_grp, value_grp, d_grp, log_total = operands
        scores = jnp.einsum("qrd,kd->rqk", query_grp, key_grp, preferred_element_type=F32) * scale
        scores = jnp.where(mask[None], scores, -1e30)
        probs = jnp.exp(scores - log_total[..., None])
        d_value = jnp.einsum("rqk,qrd->kd", probs.astype(BF16), d_grp, preferred_element_type=F32)
        d_probs = jnp.einsum("qrd,kd->rqk", d_grp, value_grp, preferred_element_type=F32)
        d_scores = (probs * (d_probs - jnp.sum(probs * d_probs, axis=-1, keepdims=True))).astype(BF16)
        d_query = jnp.einsum("rqk,kd->qrd", d_scores, key_grp, preferred_element_type=F32) * scale
        d_key = jnp.einsum("rqk,qrd->kd", d_scores, query_grp, preferred_element_type=F32) * scale
        return (d_query, d_key, d_value)

    d_query_heads, d_key_heads, d_value_heads = lax.map(
        attend_back, (heads_of_query, heads_of_key, heads_of_value, heads_gradient, log_totals)
    )
    d_queries = d_query_heads.transpose(1, 0, 2, 3).reshape(count, width).astype(BF16)
    d_keys_part = d_key_heads.transpose(1, 0, 2).reshape(tree_length, kv_width)
    d_values_part = d_value_heads.transpose(1, 0, 2).reshape(tree_length, kv_width)
    d_keyvals = lax.psum_scatter(
        jnp.concatenate([d_keys_part, d_values_part], axis=1).astype(BF16),
        "grp",
        scatter_dimension=0,
        tiled=True,
    )
    d_keys = d_keyvals[:, :kv_width]
    d_values = d_keyvals[:, kv_width:]
    d_rank_qkv = jnp.concatenate(
        [
            product_back(d_queries, query_out),
            product_back(d_keys, keyval_out[0]),
            product_back(d_values, keyval_out[1]),
        ],
        axis=-1,
    ).astype(BF16)
    d_normed = (
        product_back(d_queries, query_full)
        + product_back(d_keyvals, keyval_full)
        + product(d_rank_qkv, qkv_in)
    )
    grad_input = (d_middle + rms_back(tokens_f, attn_gain, d_normed)).astype(BF16)
    grad_qkv_in = product_outer(d_rank_qkv, normed)
    grad_query_out = product_outer(low_rank[:, :RANK], d_queries)
    grad_keyval_out = jnp.stack(
        [
            product_outer(low_rank[:, RANK : 2 * RANK], d_keys),
            product_outer(low_rank[:, 2 * RANK :], d_values),
        ],
        axis=0,
    )

    def split(gradient):
        return jnp.moveaxis(
            gradient.astype(BF16).reshape(gradient.shape[:-1] + (groups, -1)), -2, 0
        ).reshape(groups, -1)

    dense = jnp.concatenate(
        [
            split(piece)
            for piece in (
                grad_qkv_in,
                grad_query_out,
                grad_keyval_out,
                grad_output_in,
                grad_output_out,
                grad_router_in,
                grad_router_out,
            )
        ],
        axis=1,
    )
    dense = jnp.pad(dense, ((0, 0), (0, -dense.shape[1] % (reps * 128))))
    dense = dense.reshape(groups, reps, -1).swapaxes(0, 1).reshape(reps * groups, -1)
    dense = lax.all_to_all(dense, ("rep", "grp"), split_axis=0, concat_axis=0, tiled=True)
    dense = jnp.sum(dense.reshape(reps, groups, -1).astype(F32), axis=1)
    dense = jnp.sum(owner_hot[:, :, None] * dense[None], axis=1).astype(BF16)
    dense = lax.all_gather(dense, "rep", axis=1).reshape(adapters, -1)
    owned = [piece.astype(F32) for piece in unpack(dense, shapes[:7])]
    return (
        result,
        grad_input,
        owned[0].swapaxes(1, 2),
        owned[1],
        owned[2],
        owned[3].swapaxes(1, 2),
        owned[4],
        owned[5].swapaxes(1, 2),
        owned[6],
        grad_a_gateup,
        grad_b_gateup,
        grad_a_down,
        grad_b_down,
    )


def solution(mesh):
    in_specs = (
        P(("rep", "grp"), None),
        P(("rep", "grp"), None),
        P(("rep", "grp"), None),
        P(("rep", "grp")),
        P("rep", None),
        P("rep"),
        P("grp", None),
        P("grp", None),
        P("grp", None),
        P("grp", None),
        P("grp"),
        P("grp"),
        P("grp", None, None),
        P("grp", None, None),
        P(None, "grp", None),
        P(None, None, "grp"),
        P(None, None, None, "grp"),
        P(None, "grp", None),
        P(None, None, "grp"),
        P(None, "grp", None),
        P(None, None, "grp"),
        P(None, "grp", None, None),
        P(None, "grp", None, None, None),
        P(None, "grp", None, None),
        P(None, "grp", None, None),
    )
    out_specs = (
        P(("rep", "grp"), None),
        P(("rep", "grp"), None),
        P(None, "grp", None),
        P(None, None, "grp"),
        P(None, None, None, "grp"),
        P(None, "grp", None),
        P(None, None, "grp"),
        P(None, "grp", None),
        P(None, None, "grp"),
        P(None, "grp", None, None),
        P(None, "grp", None, None, None),
        P(None, "grp", None, None),
        P(None, "grp", None, None),
    )
    return jax.shard_map(local, mesh=mesh, in_specs=in_specs, out_specs=out_specs, check_vma=False)
```

time: 2050 us -> 1040 us (0.51)
  waiting for transfers between devices: 636 us -> 227 us
  matrix products: 487 us -> 200 us
  blocking collectives: 309 us -> 66 us
  Pallas kernels: 0 us -> 225 us
  local copies, waits for them, and re-layouts: 346 us -> 170 us
  other arithmetic: 199 us -> 107 us
  starting transfers between devices: 41.7 us -> 19.1 us
    dot_general x93 -> x69, matrix products: 466 us -> 165 us  [the longest x8 27.4 us: attend_back(): jnp.einsum('rqk,qrd->kd', probs.astype(BF16), d_grp, preferred_element_ty...]
    all_to_all x4 -> x3, waiting for transfers between devices: 287 us -> 12.9 us  [the longest x1 8.22 us: local(): lax.all_to_all(dense, ('rep', 'grp'), split_axis=0, concat_axis=0, tiled=...]
    pallas_call x0 -> x1, Pallas kernels: none -> 225 us  [run_experts(): pl.pallas_call(functools.partial(expert_kernel, blocks=blocks, rows_block...]
    psum x1 -> x0, waiting for transfers between devices: 223 us -> none  [local(): lax.psum(spread(owned_qkv_in).astype(jnp.bfloat16), 'rep')]
    all_gather x11 -> x4, blocking collectives: 240 us -> 53.7 us  [the longest x1 27.2 us: local(): dense = lax.all_gather(dense, 'rep', axis=1).reshape(adapters, -1)]
    reshape x10 -> x15, local copies, waits for them, and re-layouts: 178 us -> 4.35 us  [the longest x7 2.43 us: split(): gradient.astype(BF16).reshape(gradient.shape[:-1] + (groups, -1))]
    ppermute x0 -> x6, waiting for transfers between devices: none -> 76.1 us  [the longest x3 76.1 us: gather_rows(): got = lax.ppermute(mine, 'grp', swap_pairs(2))]
    gather x2 -> x0, local copies, waits for them, and re-layouts: 67 us -> none  [the longest x1 33.5 us: local(): returned.reshape(experts * capacity, width)[target]]
  transfers between devices with their start and end apart: 18 -> 15, of which waited for: 10 -> 6; matrix products, arithmetic and copies ran while one was open for 37% -> 35% of each run, Pallas kernels for 0% -> 0%
where the time goes in v1:
time: 1040 us; the launch traced here: 1030 us
  waiting for transfers between devices  227 us (22%)
  Pallas kernels  225 us (22%)
  matrix products  200 us (19%)
  local copies, waits for them, and re-layouts  170 us (16%)
  other arithmetic  107 us (10%)
  blocking collectives  66 us (6%)
  starting transfers between devices  19.1 us (2%)
  between operations  16.3 us (2%)
    pallas_call x1, Pallas kernels, run_experts(): pl.pallas_call(functools.partial(expert_kernel, blocks=blocks, rows_block...  225 us
    ppermute x3, waiting for transfers between devices, gather_rows(): got = lax.ppermute(mine, 'grp', swap_pairs(2))  76.1 us
    reduce_scatter x1, waiting for transfers between devices, local(): lax.psum_scatter(jnp.concatenate([part_d, part_result], axis=1), 'grp', s...  62.4 us
    all_gather x1, waiting for transfers between devices, local(): lax.all_gather(summed, 'rep', axis=1)  44 us
    convert_element_type x2, local copies, waits for them, and re-layouts, local(): lanes_joined(spread[:, :, :edges[1]], 2 * RANK).swapaxes(2, 3).astype(F32)  39.2 us
    all_gather x1, waiting for transfers between devices, local(): rows_all = lax.all_gather(normed_ffn, 'grp', axis=0, tiled=True)  31.3 us
    dot_general x8, matrix products, attend_back(): jnp.einsum('rqk,qrd->kd', probs.astype(BF16), d_grp, preferred_element_ty...  27.4 us
    all_gather x1, blocking collectives, local(): dense = lax.all_gather(dense, 'rep', axis=1).reshape(adapters, -1)  27.2 us
  transfers between devices with their start and end apart: 15, of which 6 were waited for; matrix products, arithmetic and copies ran while one was open for 35% of the time, Pallas kernels for 0%

profile of v1, /device:TPU:0, one launch (start us, length us, event | category | flops | bytes accessed | tf_op | source)
XLA Modules:
  0.0 1031.2 jit_solution(5684382916015150599)
XLA Ops:
  20.8 14.9 %all-gather = bf16[256000]{0:T(1024)(128)(2,1)} all-gather(bf16[128000]{0:T(1024)(128)(2,1)S(1)} %pad.8), channel_id=2, replica_groups=mesh['rep'=16,'grp'=2] {'grp'}, dimensions={0}, use_global_device_ids=true | all-gather | bytes 768000 | tf_op jit(solution)/shard_map/all_gather | solution.py:385
  61.3 76.1 %collective-permute-done.2 = bf16[384,1536]{1,0:T(8,128)(2,1)} collective-permute-done((bf16[384,1536]{1,0:T(8,128)(2,1)}, bf16[384,1536]{1,0:T(8,128)(2,1)}, u32[]{:S(2)}, u32[]{:S(2)}) %collective-permute-start.2) | collective-permute-done | bytes 1179680 | tf_op jit(solution)/shard_map/ppermute | solution.py:285
  166.8 71.8 %while.42 = (s32[]{:T(128)}, bf16[8,512,3,64]{1,3,2,0:T(8,128)(2,1)S(1)}, f32[8,3,512]{2,1,0:T(4,128)}, bf16[8,1024,64]{1,2,0:T(8,128)(2,1)}, bf16[8,1024,64]{1,...) while((s32[]{:T(128)}, ...), condition=%wide.region_7.8_spmd.clone, body=%wide.region_4.7_spmd.clone.sunk | while | flops 425818624 | bytes 22742176 | solution.py:440
  239.6 4.9 multiply_reduce_fusion.2
  257.3 6.7 all-gather.2
  264.8 31.3 %all-gather.12.cloned.1.call-done.x_ref = bf16[1024,1536]{1,0:T(8,128)(2,1)} async-done(((bf16[512,1536]{1,0:T(8,128)(2,1)}), bf16[1024,1536]{1,0:T(8,128)(2,1)}) %all-gather.12.cloned.1.call-update) | async-done | bytes 3145744 | tf_op jit(solution)/shard_map/all_gather | solution.py:460
  296.1 225.3 %experts.1 = (bf16[1024,1536]{1,0:T(8,128)(2,1)}, bf16[1024,1536]{1,0:T(8,128)(2,1)}, f32[20,2,512]{2,1,0:T(2,128)}, bf16[20,192,512]{2,1,0:T(8,128)(2,1)}) custom-call(s32[1]{0:T(128)} %copy.272.chosen_ref, bf16[1024,1536]{1,0:T(8,128)(2,1)} %all-gather.12.cloned.1.call-done.x_ref, bf16[1024,1536]{1,0:T(8,128)(2,1)} %all-gather.14.cloned.1.call-done.g_ref, ...), custom_call_target="tpu_custom_call" | custom-call | flops 120000004096 | bytes 100000000 | tf_op jit(solution)/shard_map/experts/pallas_call | solution.py:218
  521.5 6.3 pad_maximum_fusion
  537.4 6.0 all-to-all-start.2
  543.6 62.4 %reduce-scatter.3.cloned.1.call-done = bf16[512,3072]{1,0:T(8,128)(2,1)} async-done(((bf16[1024,3072]{1,0:T(8,128)(2,1)}), bf16[512,3072]{1,0:T(8,128)(2,1)}) %reduce-scatter.3.cloned.1.call-update) | async-done | bytes 3145744 | tf_op jit(solution)/shard_map/reduce_scatter | solution.py:499
  615.4 6.1 fusion.90
  624.1 143.3 %while.43 = (s32[]{:T(128)}, bf16[8,512,3,64]{1,3,2,0:T(8,128)(2,1)}, bf16[8,1024,64]{1,2,0:T(8,128)(2,1)}, bf16[8,1024,64]{1,2,0:T(8,128)(2,1)}, bf16[8,1024,64...) while((s32[]{:T(128)}, ...), condition=%wide.region_18.19_spmd.clone, body=%wide.region_16.18_spmd.clone.sunk | while | flops 1034582528 | bytes 52486328 | solution.py:532
  771.9 12.3 %all-reduce.2 = s32[16]{0:T(128)S(1)} all-reduce(s32[16]{0:T(128)S(1)} %dynamic-update-slice), channel_id=1, replica_groups=mesh['rep'=16,'grp'=2] {'rep'}, use_global_device_ids=true, to_apply=%add.2 | all-reduce | flops 16 | bytes 128
  784.2 6.5 convert_element_type.319
  790.7 6.8 multiply_reduce_fusion
  842.6 5.3 fusion.82
  849.8 8.2 all-to-all-done.1
  864.8 27.2 %all-gather.3 = bf16[4,96256]{1,0:T(4,128)(2,1)S(1)} all-gather(bf16[4,6016]{1,0:T(4,128)(2,1)S(1)} %multiply_reduce_fusion.3), channel_id=5, replica_groups=mesh['rep'=16,'grp'=2] {'rep'}, dimensions={1}, use_global_device_ids=true | all-gather | bytes 818176 | tf_op jit(solution)/shard_map/all_gather | solution.py:595
  897.2 44.0 %all-gather.16.cloned.1.call-done = bf16[4,3840,512]{2,1,0:T(8,128)(2,1)} async-done(((bf16[4,240,512]{2,1,0:T(8,128)(2,1)}), bf16[4,3840,512]{2,1,0:T(8,128)(2,1)}) %all-gather.16.cloned.1.call-update) | async-done | bytes 15728656 | tf_op jit(solution)/shard_map/all_gather | solution.py:485
  948.8 7.3 slice.178
  959.3 11.9 %copy.206 = f32[4,20,3,16,512]{4,2,3,1,0:T(4,128)} copy(bf16[4,20,3,16,512]{4,3,2,1,0:T(8,128)(2,1)S(1)} %bitcast.450) | data formatting | bytes 11796480 | tf_op jit(solution)/shard_map/convert_element_type | solution.py:497
  971.1 13.7 %reshape.492 = f32[4,20,16,1536]{3,2,1,0:T(8,128)} reshape(f32[4,20,16,3,512]{4,3,2,1,0:T(4,128)} %bitcast.440) | data formatting | bytes 15728640 | tf_op jit(solution)/shard_map/convert_element_type | solution.py:497
  984.9 13.0 %copy.205 = f32[4,20,3,32,512]{4,2,3,1,0:T(4,128)} copy(bf16[4,20,3,32,512]{4,3,2,1,0:T(8,128)(2,1)} %bitcast.441) | data formatting | bytes 23592960 | tf_op jit(solution)/shard_map/convert_element_type | solution.py:494
  997.9 26.2 %reshape.496 = f32[4,20,32,1536]{3,2,1,0:T(8,128)} reshape(f32[4,20,32,3,512]{4,3,2,1,0:T(4,128)} %bitcast.437) | data formatting | bytes 31457280 | tf_op jit(solution)/shard_map/convert_element_type | solution.py:494
  (480 shorter events, 394.0 us)
Async XLA Ops:
  7.2 32.4 %copy-start.6 = (bf16[512,1536]{1,0:T(8,128)(2,1)S(1)}, bf16[512,1536]{1,0:T(8,128)(2,1)}, u32[]{:S(2)}) copy-start(bf16[512,1536]{1,0:T(8,128)(2,1)} %param.31) | copy-start | bytes 4718596
  7.2 152.0 %all-gather.10.cloned.1.call-start = ((), (), s32[]{:S(2)}) async-start(), calls=%async_computation.5 | async-start | bytes 3145728 | tf_op jit(solution)/shard_map/all_gather | solution.py:419
  9.5 30.0 %collective-permute-start = (bf16[384,1024]{1,0:T(8,128)(2,1)}, bf16[384,1024]{1,0:T(8,128)(2,1)}, u32[]{:S(2)}, u32[]{:S(2)}) collective-permute-start(bf16[384,1024]{1,0:T(8,128)(2,1)} %constant_dynamic-slice_fusion.4), channel_id=1, source_target_pairs={{0,1},{1,0},{2,3},{3,2},{4,5},{5,4},{6,7},{7,6},{8,9},{9,8},{10,11... | collective-permute-start | bytes 2359304 | tf_op jit(solution)/shard_map/ppermute | solution.py:285
  39.5 4.2 collective-permute-start.1
  41.0 107.2 %copy-start.56 = (f32[1536]{0:T(1024)}, f32[1536]{0:T(1024)S(1)}, u32[]{:S(2)}) copy-start(f32[1536]{0:T(1024)S(1)} %reshape.484) | copy-start | bytes 18436
  41.8 106.5 %copy-start.59 = (f32[512]{0:T(512)}, f32[512]{0:T(512)S(1)}, u32[]{:S(2)}) copy-start(f32[512]{0:T(512)S(1)} %add_rsqrt_fusion.1) | copy-start | bytes 6148
  42.4 99.4 %copy-start.34 = (bf16[512,48]{0,1:T(8,128)(2,1)}, bf16[512,48]{0,1:T(8,128)(2,1)S(1)}, u32[]{:S(2)}) copy-start(bf16[512,48]{0,1:T(8,128)(2,1)S(1)} %convolution_convert_fusion.6) | copy-start | bytes 147460
  48.6 216.2 %all-gather.14.cloned.1.call-start = ((), (), s32[]{:S(2)}) async-start(), calls=%async_computation.7 | async-start | bytes 4718592 | tf_op jit(solution)/shard_map/all_gather | solution.py:409
  51.1 91.3 %collective-permute-start.4 = (bf16[384,1536]{1,0:T(8,128)(2,1)}, bf16[384,1536]{1,0:T(8,128)(2,1)}, u32[]{:S(2)}, u32[]{:S(2)}) collective-permute-start(bf16[384,1536]{1,0:T(8,128)(2,1)} %constant_dynamic-slice_fusion.1), channel_id=1, source_target_pairs={{0,1},{1,0},{2,3},{3,2},{4,5},{5,4},{6,7},{7,6},{8,9},{9,8},{10,11... | collective-permute-start | bytes 3538952 | tf_op jit(solution)/shard_map/ppermute | solution.py:285
  54.0 83.3 %collective-permute-start.2 = (bf16[384,1536]{1,0:T(8,128)(2,1)}, bf16[384,1536]{1,0:T(8,128)(2,1)}, u32[]{:S(2)}, u32[]{:S(2)}) collective-permute-start(bf16[384,1536]{1,0:T(8,128)(2,1)} %constant_dynamic-slice_fusion.2), channel_id=1, source_target_pairs={{0,1},{1,0},{2,3},{3,2},{4,5},{5,4},{6,7},{7,6},{8,9},{9,8},{10,11... | collective-permute-start | bytes 3538952 | tf_op jit(solution)/shard_map/ppermute | solution.py:285
  54.3 241.8 %all-gather.12.cloned.1.call-start = ((), (), s32[]{:S(2)}) async-start(), calls=%async_computation.6 | async-start | bytes 4718592 | tf_op jit(solution)/shard_map/all_gather | solution.py:460
  137.4 9.5 collective-permute-start.3
  137.5 101.4 %copy-start.28 = (bf16[2,8,2,768]{3,1,2,0:T(8,128)(2,1)}, bf16[2,8,2,768]{3,1,2,0:T(8,128)(2,1)S(1)}, u32[]{:S(2)}) copy-start(bf16[2,8,2,768]{3,1,2,0:T(8,128)(2,1)S(1)} %copy.180) | copy-start | bytes 147460
  137.6 101.1 %copy-start.26 = (bf16[2,8,2,768]{3,1,2,0:T(8,128)(2,1)}, bf16[2,8,2,768]{3,1,2,0:T(8,128)(2,1)S(1)}, u32[]{:S(2)}) copy-start(bf16[2,8,2,768]{3,1,2,0:T(8,128)(2,1)S(1)} %copy.179) | copy-start | bytes 147460
  142.5 14.4 %collective-permute-start.5 = (bf16[384,1536]{1,0:T(8,128)(2,1)}, bf16[384,1536]{1,0:T(8,128)(2,1)}, u32[]{:S(2)}, u32[]{:S(2)}) collective-permute-start(bf16[384,1536]{1,0:T(8,128)(2,1)} %collective-permute-done.4), channel_id=1, source_target_pairs={{0,2},{2,0},{4,6},{6,4},{8,10},{10,8},{12,14},{14,12},{16,18},{18,... | collective-permute-start | bytes 3538952 | tf_op jit(solution)/shard_map/ppermute | solution.py:286
  247.8 358.2 %reduce-scatter.3.cloned.1.call-start = ((), (), s32[]{:S(2)}) async-start(), calls=%async_computation.8 | async-start | bytes 9437184 | tf_op jit(solution)/shard_map/reduce_scatter | solution.py:499
  529.3 8.1 all-to-all-start
  537.4 246.8 %all-to-all-start.2 = ((bf16[16,240,512]{2,1,0:T(8,128)(2,1)}), bf16[16,240,512]{2,1,0:T(8,128)(2,1)}, u32[]{:S(2)}, u32[]{:S(2)}) async-start(bf16[16,240,512]{2,1,0:T(8,128)(2,1)} %bitcast.460), calls=%async_computation.4 | async-start | bytes 7864320 | tf_op jit(solution)/shard_map/all_to_all | solution.py:481
  543.3 264.2 %reduce-scatter.5.cloned.1.call-start = ((), (), s32[]{:S(2)}) async-start(), calls=%async_computation.9 | async-start | bytes 3145728 | tf_op jit(solution)/shard_map/reduce_scatter | solution.py:538
  770.5 170.7 %all-gather.16.cloned.1.call-start = ((), (), s32[]{:S(2)}) async-start(), calls=%async_computation.10 | async-start | bytes 16711680 | tf_op jit(solution)/shard_map/all_gather | solution.py:485
  817.4 19.9 %copy-start.21 = (bf16[6,8,2,768]{3,1,2,0:T(8,128)(2,1)S(1)}, bf16[6,8,2,768]{3,1,2,0:T(8,128)(2,1)}, u32[]{:S(2)}) copy-start(bf16[6,8,2,768]{3,1,2,0:T(8,128)(2,1)} %copy-done.20) | copy-start | bytes 442372
  819.3 18.0 %copy-start.50 = (bf16[512,16]{0,1:T(8,128)(2,1)S(1)}, bf16[512,16]{0,1:T(8,128)(2,1)}, u32[]{:S(2)}) copy-start(bf16[512,16]{0,1:T(8,128)(2,1)} %copy-done.49) | copy-start | bytes 49156
  833.6 24.4 %all-to-all-start.1 = ((bf16[32,2,3008]{2,1,0:T(2,128)(2,1)}), bf16[32,2,3008]{2,1,0:T(2,128)(2,1)}, u32[]{:S(2)}, u32[]{:S(2)}) async-start(bf16[32,2,3008]{2,1,0:T(2,128)(2,1)} %reshape.527), calls=%async_computation.3 | async-start | bytes 786432 | tf_op jit(solution)/shard_map/all_to_all | solution.py:592
  997.9 26.3 %copy-start.1 = (bf16[4,768,48]{1,2,0:T(8,128)(2,1)S(1)}, bf16[4,768,48]{1,2,0:T(8,128)(2,1)}, u32[]{:S(2)}) copy-start(bf16[4,768,48]{1,2,0:T(8,128)(2,1)} %param.45) | copy-start | bytes 884740
  (58 other events, 281.4 us)
Sparse Core Ops, SparseCore 0:
  48.7 57.3 all-gather.9
  107.6 53.7 all-gather.13
  247.9 48.1 all-gather.11
  527.9 78.0 reduce-scatter.2
  770.6 31.9 reduce-scatter.4
  805.3 135.8 all-gather.15

commit v2 on v1

--- a/solution.py
+++ b/solution.py
@@ -15,7 +15,6 @@
 RANK = 16
 SEG = 128
 FLUSH = 5
-LANES = 512
 
 EPSILON = 1e-05
 BF16 = jnp.bfloat16
@@ -65,26 +64,327 @@
     return lax.fori_loop(0, total, climb, (labels, start_index))[1]
 
 
-def tree_mask(parent_row, pad_row, first, count, tree_length):
-    table = ancestry(parent_row)
-    segs_here = count // SEG
-    segs_all = tree_length // SEG
-    rows = lax.dynamic_slice_in_dim(table, first // SEG, segs_here, 0)
-    linked = jnp.broadcast_to(rows[:, None, :, None] > 0, (segs_here, SEG, segs_all, SEG)).reshape(
-        count, tree_length
-    )
-    query_pos = first + jnp.arange(count, dtype=jnp.int32)
-    key_pos = jnp.arange(tree_length, dtype=jnp.int32)
-    same = query_pos[:, None] // SEG == key_pos[None, :] // SEG
-    causal = jnp.logical_or(jnp.logical_not(same), key_pos[None, :] <= query_pos[:, None])
-    live = jnp.logical_or(pad_row[None, :] > 0, key_pos[None, :] == query_pos[:, None])
-    return jnp.logical_and(jnp.logical_and(linked, causal), live)
+def tile_parts(ref_k, seg_a, seg_b):
+    return jnp.concatenate(
+        [
+            ref_k[pl.ds(pl.multiple_of(seg_a * SEG, SEG), SEG), :],
+            ref_k[pl.ds(pl.multiple_of(seg_b * SEG, SEG), SEG), :],
+        ],
+        axis=0,
+    )
+
+
+def fill_doubled(held, near_ref, far_ref, ones=False):
+    near = near_ref.shape[0]
+    for ref, at in ((near_ref, 0), (far_ref, near)):
+        rows = ref[...].astype(F32)
+        low = lax.broadcasted_iota(jnp.int32, rows.shape, 1) < HEAD_SIZE
+        turned = pltpu.roll(rows, HEAD_SIZE, axis=1)
+        there = pl.ds(at, rows.shape[0])
+        held[0, there, :] = jnp.where(low, rows, 1.0 if ones else turned).astype(BF16)
+        held[1, there, :] = jnp.where(low, turned, 1.0 if ones else rows).astype(BF16)
+
+
+PLACES = (((0, 0), (0, 1), (1, 0)), ((1, 1), (2, 0), (2, 1)))
+
+
+def stacked_heads(ref, at, which, scale=None):
+    low = lax.broadcasted_iota(jnp.int32, (SEG, 2 * HEAD_SIZE), 1) < HEAD_SIZE
+    out = []
+    for column, half in PLACES[which]:
+        piece = ref[at, column * 2 * HEAD_SIZE : (column + 1) * 2 * HEAD_SIZE].astype(F32)
+        if scale is not None:
+            piece = piece * scale
+        out.append(jnp.where(low if half == 0 else jnp.logical_not(low), piece, 0.0))
+    return jnp.concatenate(out, axis=0)
+
+
+def unstack(first, second):
+    low = lax.broadcasted_iota(jnp.int32, (SEG, 2 * HEAD_SIZE), 1) < HEAD_SIZE
+    return [
+        jnp.where(low, first[0:SEG], first[SEG : 2 * SEG]),
+        jnp.where(low, first[2 * SEG :], second[0:SEG]),
+        jnp.where(low, second[SEG : 2 * SEG], second[2 * SEG :]),
+    ]
+
+
+def first_bias(own_ref, live_ref, i, seg_b):
+    other = jnp.broadcast_to(live_ref[seg_b], (SEG, SEG))
+    tile = jnp.concatenate([own_ref[i], other], axis=1)
+    return jnp.concatenate([tile] * 3, axis=0)
+
+
+def next_bias(live_ref, seg_a, seg_b):
+    return jnp.concatenate([live_ref[seg_a], live_ref[seg_b]], axis=1)
+
+
+def attend_kernel(
+    list_ref,
+    steps_ref,
+    q_ref,
+    k_ref,
+    v_ref,
+    k_far,
+    v_far,
+    own_ref,
+    live_ref,
+    o_ref,
+    l_ref,
+    kf,
+    vf,
+    *,
+    here,
+    segs,
+    scale,
+):
+    fill_doubled(kf, k_ref, k_far)
+    fill_doubled(vf, v_ref, v_far, ones=True)
+    lanes = lax.broadcasted_iota(jnp.int32, (SEG, 2 * HEAD_SIZE), 1)
+    low = lanes < HEAD_SIZE
+    slots = 2 * segs
+    for i in range(here):
+        at = pl.ds(i * SEG, SEG)
+        queries = [stacked_heads(q_ref, at, which, scale).astype(BF16) for which in range(2)]
+
+        def pair_of(t):
+            return (
+                lax.rem(list_ref[i * slots + 2 * t], segs),
+                lax.rem(list_ref[i * slots + 2 * t + 1], segs),
+            )
+
+        seg_a, seg_b = pair_of(0)
+        bias = first_bias(own_ref, live_ref, i, list_ref[i * slots + 1])
+        state = []
+        for which in range(2):
+            s = product_back(queries[which], tile_parts(kf.at[which], seg_a, seg_b)) + bias
+            top = jnp.max(s, axis=1, keepdims=True)
+            p = jnp.exp(s - top).astype(BF16)
+            state.append((top, product(p, tile_parts(vf.at[which], seg_a, seg_b))))
+
+        def body(t, state):
+            bias = next_bias(live_ref, list_ref[i * slots + 2 * t], list_ref[i * slots + 2 * t + 1])
+            seg_a, seg_b = pair_of(t)
+            out = []
+            for which in range(2):
+                top, acc = state[which]
+                s = product_back(queries[which], tile_parts(kf.at[which], seg_a, seg_b)) + bias
+                higher = jnp.maximum(top, jnp.max(s, axis=1, keepdims=True))
+                p = jnp.exp(s - higher).astype(BF16)
+                acc = acc * jnp.exp(top - higher) + product(p, tile_parts(vf.at[which], seg_a, seg_b))
+                out.append((higher, acc))
+            return tuple(out)
+
+        state = lax.fori_loop(1, steps_ref[i], body, tuple(state))
+        turned = [pltpu.roll(acc, HEAD_SIZE, axis=1) for _, acc in state]
+        logs = jnp.zeros((SEG, 2 * HEAD_SIZE), F32)
+        heads = []
+        for which in range(2):
+            for n, (_, half) in enumerate(PLACES[which]):
+                rows = slice(n * SEG, (n + 1) * SEG)
+                plain, other = state[which][1][rows], turned[which][rows]
+                heads.append(plain / other if half == 0 else other / plain)
+                total = jnp.where(low, other, plain)
+                logs = jnp.where(lanes == which * 3 + n, state[which][0][rows] + jnp.log(total), logs)
+        l_ref[0, at, :] = logs
+        for column in range(3):
+            o_ref[at, column * 2 * HEAD_SIZE : (column + 1) * 2 * HEAD_SIZE] = jnp.where(
+                low, heads[2 * column], heads[2 * column + 1]
+            ).astype(BF16)
+
+
+def attend_back_kernel(
+    list_ref,
+    steps_ref,
+    q_ref,
+    k_ref,
+    v_ref,
+    k_far,
+    v_far,
+    own_ref,
+    live_ref,
+    o_ref,
+    do_ref,
+    l_ref,
+    dq_ref,
+    dk_ref,
+    dv_ref,
+    dk_far,
+    dv_far,
+    kf,
+    vf,
+    dkf,
+    dvf,
+    *,
+    here,
+    segs,
+    scale,
+):
+    fill_doubled(kf, k_ref, k_far)
+    fill_doubled(vf, v_ref, v_far)
+    dkf[...] = jnp.zeros_like(dkf)
+    dvf[...] = jnp.zeros_like(dvf)
+    slots = 2 * segs
+    for i in range(here):
+        at = pl.ds(i * SEG, SEG)
+        fixed = []
+        for which in range(2):
+            d_o = stacked_heads(do_ref, at, which)
+            fixed.append(
+                (
+                    stacked_heads(q_ref, at, which, scale).astype(BF16),
+                    d_o.astype(BF16),
+                    jnp.sum(d_o * stacked_heads(o_ref, at, which), axis=1, keepdims=True),
+                    jnp.concatenate(
+                        [l_ref[0, at, which * 3 + n : which * 3 + n + 1] for n in range(3)], axis=0
+                    ),
+                )
+            )
+
+        def step(t, bias):
+            seg_a = lax.rem(list_ref[i * slots + 2 * t], segs)
+            seg_b = lax.rem(list_ref[i * slots + 2 * t + 1], segs)
+            out = []
+            for which, (q, d_o, delta, log_total) in enumerate(fixed):
+                k = tile_parts(kf.at[which], seg_a, seg_b)
+                v = tile_parts(vf.at[which], seg_a, seg_b)
+                p = jnp.exp(product_back(q, k) + bias - log_total)
+                d_p = product_back(d_o, v)
+                d_s = (p * (d_p - delta)).astype(BF16)
+                d_v = product_outer(p.astype(BF16), d_o)
+                d_k = product_outer(d_s, q)
+                for n, seg in enumerate((seg_a, seg_b)):
+                    rows = pl.ds(pl.multiple_of(seg * SEG, SEG), SEG)
+                    dkf[which, rows, :] += d_k[n * SEG : (n + 1) * SEG]
+                    dvf[which, rows, :] += d_v[n * SEG : (n + 1) * SEG]
+                out.append(product(d_s, k))
+            return tuple(out)
+
+        d_q = step(0, first_bias(own_ref, live_ref, i, list_ref[i * slots + 1]))
+
+        def body(t, carry):
+            bias = next_bias(live_ref, list_ref[i * slots + 2 * t], list_ref[i * slots + 2 * t + 1])
+            return tuple(a + b for a, b in zip(carry, step(t, bias)))
+
+        d_q = lax.fori_loop(1, steps_ref[i], body, d_q)
+        for column, piece in enumerate(unstack(*d_q)):
+            dq_ref[at, column * 2 * HEAD_SIZE : (column + 1) * 2 * HEAD_SIZE] = (piece * scale).astype(BF16)
+    near = dk_ref.shape[0]
+    for out, far_out, held in ((dk_ref, dk_far, dkf), (dv_ref, dv_far, dvf)):
+        first = held[0] + pltpu.roll(held[0], HEAD_SIZE, axis=1)
+        second = held[1] + pltpu.roll(held[1], HEAD_SIZE, axis=1)
+        low = lax.broadcasted_iota(jnp.int32, first.shape, 1) < HEAD_SIZE
+        total = jnp.where(low, first, second).astype(BF16)
+        out[...] = total[:near]
+        far_out[...] = total[near:]
+
+
+def visits(parent_row, pad_near, pad_far, first):
+    count = pad_near.shape[0]
+    tree_length = count + pad_far.shape[0]
+    segs = tree_length // SEG
+    here = count // SEG
+    own = jnp.arange(here, dtype=jnp.int32)
+    labels = jnp.arange(segs, dtype=jnp.int32)
+    table = lax.dynamic_slice_in_dim(ancestry(parent_row), first // SEG, here, 0)
+    turn = (labels[:, None] == (labels[None, :] + segs - first // SEG) % segs).astype(F32)
+    table = product_back(table.astype(F32), turn).astype(jnp.int32)
+    table = jnp.where(labels[None, :] == own[:, None], 0, table)
+    order = jnp.sum(jnp.where(labels[None, :] <= labels[:, None], table[:, None, :], 0), axis=2)
+    spots = jnp.arange(1, 2 * segs, dtype=jnp.int32)
+    found = jnp.logical_and(table[:, None, :] > 0, order[:, None, :] == spots[None, :, None])
+    listing = jnp.where(jnp.any(found, axis=2), jnp.sum(found * labels, axis=2), segs)
+    listing = jnp.concatenate([own[:, None], listing], axis=1).astype(jnp.int32)
+    steps = (2 + order[:, -1]) // 2
+    live = jnp.where(jnp.concatenate([pad_near, pad_far]) > 0, 0.0, -1e30).astype(F32).reshape(segs, SEG)
+    places = jnp.arange(SEG)
+    causal = places[None, :] <= places[:, None]
+    same = places[None, :] == places[:, None]
+    own_bias = jnp.where(same[None], 0.0, jnp.where(causal[None], live[:here, None, :], -1e30))
+    live = jnp.concatenate([live, jnp.full((1, SEG), -1e30, F32)], axis=0)[:, None, :]
+    return listing.reshape(-1), steps.astype(jnp.int32), own_bias, live
+
+
+def attention_specs(count, far, here, segs):
+    narrow = 2 * HEAD_SIZE
+    shift = KEY_VALUE_HEADS // 2
+    return [
+        pl.BlockSpec((count, 3 * narrow), lambda h, a, b: (0, h)),
+        pl.BlockSpec((count, narrow), lambda h, a, b: (0, h)),
+        pl.BlockSpec((count, narrow), lambda h, a, b: (0, h + shift)),
+        pl.BlockSpec((far, narrow), lambda h, a, b: (0, h)),
+        pl.BlockSpec((far, narrow), lambda h, a, b: (0, h + shift)),
+        pl.BlockSpec((here, SEG, SEG), lambda h, a, b: (0, 0, 0)),
+        pl.BlockSpec((segs + 1, 1, SEG), lambda h, a, b: (0, 0, 0)),
+    ]
+
+
+def run_attention(listing, steps, queries, near, far, own_bias, live):
+    count, width = queries.shape
+    tree_length = count + far.shape[0]
+    here, segs = count // SEG, tree_length // SEG
+    pairs = KEY_VALUE_HEADS // 2
+    narrow = 2 * HEAD_SIZE
+    return pl.pallas_call(
+        functools.partial(attend_kernel, here=here, segs=segs, scale=HEAD_SIZE ** (-0.5)),
+        grid_spec=pltpu.PrefetchScalarGridSpec(
+            num_scalar_prefetch=2,
+            grid=(pairs,),
+            in_specs=attention_specs(count, far.shape[0], here, segs),
+            out_specs=[
+                pl.BlockSpec((count, 3 * narrow), lambda h, a, b: (0, h)),
+                pl.BlockSpec((1, count, narrow), lambda h, a, b: (h, 0, 0)),
+            ],
+            scratch_shapes=[pltpu.VMEM((2, tree_length, narrow), BF16)] * 2,
+        ),
+        out_shape=[
+            jax.ShapeDtypeStruct((count, width), BF16),
+            jax.ShapeDtypeStruct((pairs, count, narrow), F32),
+        ],
+        compiler_params=pltpu.CompilerParams(
+            vmem_limit_bytes=40 * 1024 * 1024, dimension_semantics=("arbitrary",)
+        ),
+        cost_estimate=pl.CostEstimate(flops=40_000_000_000, bytes_accessed=8_000_000, transcendentals=10_000_000),
+        name="attention",
+    )(listing, steps, queries, near, near, far, far, own_bias, live)
+
+
+def run_attention_back(listing, steps, queries, near, far, own_bias, live, attended, gradient, logs):
+    count, width = queries.shape
+    tree_length = count + far.shape[0]
+    here, segs = count // SEG, tree_length // SEG
+    pairs = KEY_VALUE_HEADS // 2
+    narrow = 2 * HEAD_SIZE
+    rows = pl.BlockSpec((count, 3 * narrow), lambda h, a, b: (0, h))
+    outs = [pl.BlockSpec((count, narrow), lambda h, a, b: (0, h))] * 2
+    outs += [pl.BlockSpec((far.shape[0], narrow), lambda h, a, b: (0, h))] * 2
+    return pl.pallas_call(
+        functools.partial(attend_back_kernel, here=here, segs=segs, scale=HEAD_SIZE ** (-0.5)),
+        grid_spec=pltpu.PrefetchScalarGridSpec(
+            num_scalar_prefetch=2,
+            grid=(pairs,),
+            in_specs=attention_specs(count, far.shape[0], here, segs)
+            + [rows, rows, pl.BlockSpec((1, count, narrow), lambda h, a, b: (h, 0, 0))],
+            out_specs=[rows] + outs,
+            scratch_shapes=[pltpu.VMEM((2, tree_length, narrow), BF16)] * 2
+            + [pltpu.VMEM((2, tree_length, narrow), F32)] * 2,
+        ),
+        out_shape=[jax.ShapeDtypeStruct((count, width), BF16)]
+        + [jax.ShapeDtypeStruct((count, pairs * narrow), BF16)] * 2
+        + [jax.ShapeDtypeStruct((far.shape[0], pairs * narrow), BF16)] * 2,
+        compiler_params=pltpu.CompilerParams(
+            vmem_limit_bytes=40 * 1024 * 1024, dimension_semantics=("arbitrary",)
+        ),
+        cost_estimate=pl.CostEstimate(flops=70_000_000_000, bytes_accessed=12_000_000, transcendentals=10_000_000),
+        name="attention_back",
+    )(listing, steps, queries, near, near, far, far, own_bias, live, attended, gradient, logs)
 
 
 def expert_kernel(
     chosen_ref,
     x_ref,
+    x_far,
     g_ref,
+    g_far,
     pos_ref,
     gate_ref,
     w1_ref,
@@ -94,7 +394,9 @@
     a2_ref,
     b2_ref,
     r_out,
+    r_far,
     d_out,
+    d_far,
     dg_out,
     grad_out,
     hot_s,
@@ -125,14 +427,15 @@
 
     at = pl.multiple_of(slot * cap, 16)
     for b in range(blocks):
-        here = pl.ds(b * rows_block, rows_block)
+        rows_ref, g_rows_ref = (x_ref, g_ref) if b == 0 else (x_far, g_far)
+        here = pl.ds(max(b - 1, 0) * rows_block, rows_block)
         there = pl.ds(b * cap, cap)
         places = lax.broadcasted_iota(jnp.int32, (cap, rows_block), 0)
         hit = places == pos_ref[0, b : b + 1, :]
         hot = hit.astype(F32).astype(BF16)
         hot_s[b, pl.ds(at, cap), :] = hot
-        x_s[there, :] = product(hot, x_ref[here, :]).astype(BF16)
-        g_s[there, :] = product(hot, g_ref[here, :]).astype(BF16)
+        x_s[there, :] = product(hot, rows_ref[here, :]).astype(BF16)
+        g_s[there, :] = product(hot, g_rows_ref[here, :]).astype(BF16)
         gate_s[there, :] = jnp.sum(
             jnp.where(hit, gate_ref[0, b : b + 1, :], 0.0), axis=1, keepdims=True
         )
@@ -174,20 +477,11 @@
     grad_b1 = product_outer(rank_in, dgu)
     grad_a2 = product_outer(d_rank_down, hidden)
     grad_b2 = product_outer(rank_down, d_exp)
-    parts = width // LANES
-    base = 0
-    for i in range(parts):
-        grad_out[0, base : base + 2 * RANK, :] = grad_a1[:, i * LANES : (i + 1) * LANES].astype(BF16)
-        base += 2 * RANK
-    grad_out[0, base : base + RANK, :] = grad_b1[:RANK, :FF].astype(BF16)
-    base += RANK
-    grad_out[0, base : base + RANK, :] = grad_b1[RANK:, FF:].astype(BF16)
-    base += RANK
-    grad_out[0, base : base + RANK, :] = grad_a2.astype(BF16)
-    base += RANK
-    for i in range(parts):
-        grad_out[0, base : base + RANK, :] = grad_b2[:, i * LANES : (i + 1) * LANES].astype(BF16)
-        base += RANK
+    grad_out[0, 0 : 2 * RANK, :] = grad_a1.astype(BF16)
+    grad_out[0, 2 * RANK : 3 * RANK, :] = grad_b2.astype(BF16)
+    grad_out[0, 3 * RANK :, :FF] = grad_b1[:RANK, :FF].astype(BF16)
+    grad_out[0, 3 * RANK :, FF : 2 * FF] = grad_b1[RANK:, FF:].astype(BF16)
+    grad_out[0, 3 * RANK :, 2 * FF :] = grad_a2.astype(BF16)
 
     @pl.when(slot == flush - 1)
     def _():
@@ -198,23 +492,23 @@
 
     @pl.when(e == pl.num_programs(0) - 1)
     def _():
-        r_out[...] = accr[...].astype(BF16)
-        d_out[...] = accd[...].astype(BF16)
-
-
-def grad_rows(width):
-    return (width // LANES) * 3 * RANK + 3 * RANK
-
-
-def run_experts(chosen, x, g, pos, gate, w1, w2, a1, b1, a2, b2, cap):
+        r_out[...] = accr[0:rows_block, :].astype(BF16)
+        r_far[...] = accr[rows_block:, :].astype(BF16)
+        d_out[...] = accd[0:rows_block, :].astype(BF16)
+        d_far[...] = accd[rows_block:, :].astype(BF16)
+
+
+def run_experts(chosen, x, x_far, g, g_far, pos, gate, w1, w2, a1, b1, a2, b2, cap):
     experts, blocks, rows_block = pos.shape
     width = x.shape[1]
-    tokens = x.shape[0]
+    tokens = blocks * rows_block
     rows = blocks * cap
-    stored = grad_rows(width)
     flush = FLUSH if experts % FLUSH == 0 else 1
-    whole = lambda e, c: (0, 0)
     lead = lambda e, c: (e, 0, 0)
+    near = pl.BlockSpec((rows_block, width), lambda e, c: (0, 0), pipeline_mode=pl.Buffered(1))
+    away = pl.BlockSpec((tokens - rows_block, width), lambda e, c: (0, 0), pipeline_mode=pl.Buffered(1))
+    near_shape = jax.ShapeDtypeStruct((rows_block, width), BF16)
+    away_shape = jax.ShapeDtypeStruct((tokens - rows_block, width), BF16)
     return pl.pallas_call(
         functools.partial(
             expert_kernel, blocks=blocks, rows_block=rows_block, cap=cap, flush=flush
@@ -223,8 +517,10 @@
             num_scalar_prefetch=1,
             grid=(experts,),
             in_specs=[
-                pl.BlockSpec((tokens, width), whole, pipeline_mode=pl.Buffered(1)),
-                pl.BlockSpec((tokens, width), whole, pipeline_mode=pl.Buffered(1)),
+                near,
+                away,
+                near,
+                away,
                 pl.BlockSpec((1, blocks, rows_block), lead),
                 pl.BlockSpec((1, blocks, rows_block), lead),
                 pl.BlockSpec((1, width, 2 * FF), lead),
@@ -235,10 +531,12 @@
                 pl.BlockSpec((1, 1, RANK, width), lambda e, c: (c[0], e, 0, 0)),
             ],
             out_specs=[
-                pl.BlockSpec((tokens, width), whole, pipeline_mode=pl.Buffered(1)),
-                pl.BlockSpec((tokens, width), whole, pipeline_mode=pl.Buffered(1)),
+                near,
+                away,
+                near,
+                away,
                 pl.BlockSpec((1, blocks, rows_block), lead),
-                pl.BlockSpec((1, stored, LANES), lead),
+                pl.BlockSpec((1, 4 * RANK, width), lead),
             ],
             scratch_shapes=[
                 pltpu.VMEM((blocks, flush * cap, rows_block), BF16),
@@ -254,41 +552,127 @@
             ],
         ),
         out_shape=[
-            jax.ShapeDtypeStruct((tokens, width), BF16),
-            jax.ShapeDtypeStruct((tokens, width), BF16),
+            near_shape,
+            away_shape,
+            near_shape,
+            away_shape,
             jax.ShapeDtypeStruct((experts, blocks, rows_block), F32),
-            jax.ShapeDtypeStruct((experts, stored, LANES), BF16),
+            jax.ShapeDtypeStruct((experts, 4 * RANK, width), BF16),
         ],
         compiler_params=pltpu.CompilerParams(
             vmem_limit_bytes=62 * 1024 * 1024, dimension_semantics=("arbitrary",)
         ),
         cost_estimate=pl.CostEstimate(
-            flops=120_000_000_000 * experts // 20,
+            flops=200_000_000_000 * experts // 20,
             bytes_accessed=5_000_000 * experts,
             transcendentals=rows * FF * experts,
         ),
         name="experts",
-    )(chosen, x, g, pos, gate, w1, w2, a1, b1, a2, b2)
+    )(chosen, x, x_far, g, g_far, pos, gate, w1, w2, a1, b1, a2, b2)
+
+
+def unpack_kernel(rows_ref, a1_ref, b1_ref, a2_ref, b2_ref, *, ranks, share):
+    records = ranks * share // (4 * RANK)
+    for e in range(records):
+        unit = []
+        for n in range(4):
+            at = (4 * e + n) * RANK
+            unit.append(rows_ref[at // share, 0, at % share : at % share + RANK, :].astype(F32))
+        a1_ref[0, e, 0:RANK, :] = unit[0]
+        a1_ref[0, e, RANK:, :] = unit[1]
+        b2_ref[0, e] = unit[2]
+        b1_ref[0, e, 0] = unit[3][:, :FF]
+        b1_ref[0, e, 1] = unit[3][:, FF : 2 * FF]
+        a2_ref[0, e] = unit[3][:, 2 * FF :]
+
+
+def unpack_grads(gathered, experts):
+    ranks, adapters, share, width = gathered.shape
+    if share % RANK:
+        flat = gathered.swapaxes(0, 1).reshape(adapters, experts, 4 * RANK, width).astype(F32)
+        last = flat[:, :, 3 * RANK :]
+        return (
+            flat[:, :, : 2 * RANK],
+            jnp.stack([last[..., :FF], last[..., FF : 2 * FF]], axis=2),
+            last[..., 2 * FF :],
+            flat[:, :, 2 * RANK : 3 * RANK],
+        )
+    together = 1
+    while together * share % (4 * RANK):
+        together += 1
+    held = together * share // (4 * RANK)
+    return pl.pallas_call(
+        functools.partial(unpack_kernel, ranks=together, share=share),
+        grid=(adapters, ranks // together),
+        in_specs=[pl.BlockSpec((together, 1, share, width), lambda a, i: (i, a, 0, 0))],
+        out_specs=[
+            pl.BlockSpec((1, held, 2 * RANK, width), lambda a, i: (a, i, 0, 0)),
+            pl.BlockSpec((1, held, 2, RANK, FF), lambda a, i: (a, i, 0, 0, 0)),
+            pl.BlockSpec((1, held, RANK, FF), lambda a, i: (a, i, 0, 0)),
+            pl.BlockSpec((1, held, RANK, width), lambda a, i: (a, i, 0, 0)),
+        ],
+        out_shape=[
+            jax.ShapeDtypeStruct((adapters, experts, 2 * RANK, width), F32),
+            jax.ShapeDtypeStruct((adapters, experts, 2, RANK, FF), F32),
+            jax.ShapeDtypeStruct((adapters, experts, RANK, FF), F32),
+            jax.ShapeDtypeStruct((adapters, experts, RANK, width), F32),
+        ],
+        compiler_params=pltpu.CompilerParams(
+            vmem_limit_bytes=40 * 1024 * 1024, dimension_semantics=("arbitrary", "arbitrary")
+        ),
+        cost_estimate=pl.CostEstimate(flops=0, bytes_accessed=50_000_000, transcendentals=0),
+        name="unpack",
+    )(gathered)
 
 
 def swap_pairs(size):
     return [(i, i ^ 1) for i in range(size)]
 
 
-def gather_rows(half, groups):
-    if groups != 2:
+def from_others(piece):
+    groups = lax.axis_size("grp")
+    if groups == 2:
+        return lax.ppermute(piece, "grp", swap_pairs(2))
+    rows = piece.shape[0]
+    every = lax.all_gather(piece, "grp", axis=0, tiled=True)
+    return jnp.roll(every, -lax.axis_index("grp") * rows, axis=0)[rows:]
+
+
+def to_owners(near, far):
+    groups = lax.axis_size("grp")
+    if groups == 2:
+        return near.astype(F32) + lax.ppermute(far, "grp", swap_pairs(2)).astype(F32)
+    every = jnp.roll(jnp.concatenate([near, far], axis=0), lax.axis_index("grp") * near.shape[0], axis=0)
+    return lax.psum_scatter(every, "grp", scatter_dimension=0, tiled=True).astype(F32)
+
+
+def in_order(near, far):
+    if lax.axis_size("grp") != 2:
+        return jnp.roll(jnp.concatenate([near, far], axis=0), lax.axis_index("grp") * near.shape[0], axis=0)
+    ahead = lax.axis_index("grp") == 0
+    return jnp.where(ahead, jnp.concatenate([near, far], axis=0), jnp.concatenate([far, near], axis=0))
+
+
+def gather_rows(half):
+    if lax.axis_size("grp") != 2:
         return lax.all_gather(half, "grp", axis=0, tiled=True)
     rows = half.shape[0] // 2
     core = lax.axis_index("rep") % 2
-    member = lax.axis_index("grp")
-    mine = lax.dynamic_slice_in_dim(half, core * rows, rows, 0)
+    got = lax.ppermute(lax.dynamic_slice_in_dim(half, core * rows, rows, 0), "grp", swap_pairs(2))
+    other = lax.ppermute(got, "rep", swap_pairs(lax.axis_size("rep")))
+    ahead = core == 0
+    far = jnp.where(ahead, jnp.concatenate([got, other], 0), jnp.concatenate([other, got], 0))
+    return in_order(half, far)
+
+
+def gather_rows_wide(half):
+    reps = lax.axis_size("rep")
+    if lax.axis_size("grp") != 2 or half.shape[0] % (reps * 16):
+        return lax.all_gather(half, "grp", axis=0, tiled=True)
+    rows = half.shape[0] // reps
+    mine = lax.dynamic_slice_in_dim(half, lax.axis_index("rep") * rows, rows, 0)
     got = lax.ppermute(mine, "grp", swap_pairs(2))
-    other = lax.ppermute(got, "rep", swap_pairs(lax.axis_size("rep")))
-    out = jnp.zeros((4 * rows,) + half.shape[1:], half.dtype)
-    out = lax.dynamic_update_slice_in_dim(out, half, member * 2 * rows, 0)
-    away = (1 - member) * 2 * rows
-    out = lax.dynamic_update_slice_in_dim(out, got, away + core * rows, 0)
-    return lax.dynamic_update_slice_in_dim(out, other, away + (1 - core) * rows, 0)
+    return in_order(half, lax.all_gather(got, "rep", axis=0, tiled=True))
 
 
 def pack(pieces, multiple):
@@ -347,8 +731,6 @@
     capacity = count * TOPK * 7 // (experts * 5)
     cap = -(-capacity // 16) * 16
     kv_width = KEY_VALUE_HEADS * HEAD_SIZE
-    per_kv = QUERY_HEADS // KEY_VALUE_HEADS
-    scale = HEAD_SIZE ** (-0.5)
     chosen = adapter_ids[0]
     first = member * count
     adapters = a_qkv.shape[0]
@@ -382,7 +764,7 @@
         ),
         1024,
     )
-    small_all = lax.all_gather(small, "grp", axis=0)
+    small_all = in_order(small[None], from_others(small[None]))
 
     def join(piece):
         return jnp.moveaxis(piece, 0, -2).reshape(piece.shape[1:-1] + (-1,))
@@ -402,43 +784,30 @@
     ) = [join(piece) for piece in unpack(small_all, shapes)]
     attn_gain = attn_gain.astype(F32)
     ffn_gain = ffn_gain.astype(F32)
-    keyval_full = gather_rows(w_keyval, groups)
-    query_full = gather_rows(w_query, groups)
-    output_full = gather_rows(w_output, groups)
-    routes_all = lax.all_gather(routes, "grp", axis=0)
-    upstream_all = lax.all_gather(cotangent, "grp", axis=0, tiled=True)
+    keyval_full = gather_rows(w_keyval)
+    query_full = gather_rows_wide(w_query)
+    output_full = gather_rows_wide(w_output)
+    routes_far = from_others(routes)
     ids_all = lax.all_gather(adapter_ids, "rep", axis=0, tiled=True)
 
     tokens_f = tokens.astype(F32)
     normed = rms_norm(tokens_f, attn_gain).astype(BF16)
     low_rank = product_back(normed, qkv_in).astype(BF16)
+    keyvals = product(normed, keyval_full)
+    keyvals = jnp.concatenate(
+        [
+            keyvals[:, :kv_width] + product(low_rank[:, RANK : 2 * RANK], keyval_out[0]),
+            keyvals[:, kv_width:] + product(low_rank[:, 2 * RANK :], keyval_out[1]),
+        ],
+        axis=1,
+    ).astype(BF16)
+    keyvals_far = from_others(keyvals)
+    cotangent_late, keyvals_far = lax.optimization_barrier((cotangent, keyvals_far))
+    upstream_far = from_others(cotangent_late)
     query_rows = (product(normed, query_full) + product(low_rank[:, :RANK], query_out)).astype(BF16)
-    keyvals = product(normed, keyval_full)
-    key_rows = (keyvals[:, :kv_width] + product(low_rank[:, RANK : 2 * RANK], keyval_out[0])).astype(BF16)
-    value_rows = (keyvals[:, kv_width:] + product(low_rank[:, 2 * RANK :], keyval_out[1])).astype(BF16)
-    keyval_all = lax.all_gather(
-        jnp.concatenate([key_rows, value_rows], axis=1), "grp", axis=0, tiled=True
-    )
-    every_key = keyval_all[:, :kv_width]
-    every_value = keyval_all[:, kv_width:]
-    mask = tree_mask(parents[0], pad_all, first, count, tree_length)
-    heads_of_query = query_rows.reshape(count, KEY_VALUE_HEADS, per_kv, HEAD_SIZE).transpose(1, 0, 2, 3)
-    heads_of_key = every_key.reshape(tree_length, KEY_VALUE_HEADS, HEAD_SIZE).transpose(1, 0, 2)
-    heads_of_value = every_value.reshape(tree_length, KEY_VALUE_HEADS, HEAD_SIZE).transpose(1, 0, 2)
-
-    def attend(operands):
-        query_grp, key_grp, value_grp = operands
-        scores = jnp.einsum("qrd,kd->rqk", query_grp, key_grp, preferred_element_type=F32) * scale
-        scores = jnp.where(mask[None], scores, -1e30)
-        top = jnp.max(scores, axis=-1, keepdims=True)
-        weights = jnp.exp(scores - top)
-        total = jnp.sum(weights, axis=-1, keepdims=True)
-        probs = (weights / total).astype(BF16)
-        mixed = jnp.einsum("rqk,kd->qrd", probs, value_grp, preferred_element_type=F32)
-        return (mixed.astype(BF16), top[..., 0] + jnp.log(total[..., 0]))
-
-    mixed_heads, log_totals = lax.map(attend, (heads_of_query, heads_of_key, heads_of_value))
-    attended = mixed_heads.transpose(1, 0, 2, 3).reshape(count, width)
+    pad_whole = jnp.roll(pad_all, -first)
+    listing, steps, own_bias, live = visits(parents[0], pad_whole[:count], pad_whole[count:], first)
+    attended, logs = run_attention(listing, steps, query_rows, keyvals, keyvals_far, own_bias, live)
     out_rank = product_back(attended, output_in).astype(BF16)
     middle = tokens_f + product(attended, output_full) + product(out_rank, output_out)
     normed_ffn = rms_norm(middle, ffn_gain).astype(BF16)
@@ -452,18 +821,28 @@
     gates = powers / jnp.sum(powers, axis=1, keepdims=True)
 
     mine = member * experts_dev + jnp.arange(experts_dev, dtype=jnp.int32)
+    routes_all = jnp.concatenate([routes, routes_far], axis=0).reshape(groups, count, TOPK)
     hits = jnp.any(routes_all[:, :, :, None] == mine, axis=2)
     before = (jnp.arange(count)[:, None] > jnp.arange(count)[None, :]).astype(BF16)
     ranks = jnp.einsum("ts,gse->get", before, hits.astype(BF16), preferred_element_type=F32)
     places = jnp.where(hits.transpose(0, 2, 1), ranks.astype(jnp.int32), -1).transpose(1, 0, 2)
 
-    rows_all = lax.all_gather(normed_ffn, "grp", axis=0, tiled=True)
-    gates_all = lax.all_gather(gates.T, "grp", axis=0)
-    gates_mine = lax.dynamic_slice_in_dim(gates_all, member * experts_dev, experts_dev, 1).transpose(1, 0, 2)
-    part_result, part_d, part_gates, expert_grads = run_experts(
+    rows_far = from_others(normed_ffn)
+    gates_t = gates.T
+    if groups == 2:
+        gates_near = lax.dynamic_slice_in_dim(gates_t, member * experts_dev, experts_dev, 0)
+        gates_far = from_others(lax.dynamic_slice_in_dim(gates_t, (1 - member) * experts_dev, experts_dev, 0))
+        gates_mine = jnp.stack([gates_near, gates_far], axis=1)
+    else:
+        gates_mine = lax.all_gather(gates_t, "grp", axis=0)
+        gates_mine = lax.dynamic_slice_in_dim(gates_mine, member * experts_dev, experts_dev, 1)
+        gates_mine = jnp.roll(gates_mine, -member, axis=0).transpose(1, 0, 2)
+    result_near, result_far, d_near, d_far, part_gates, expert_grads = run_experts(
         adapter_ids,
-        rows_all,
-        upstream_all,
+        normed_ffn,
+        rows_far,
+        cotangent,
+        upstream_far,
         places,
         gates_mine,
         w_gateup,
@@ -476,37 +855,28 @@
     )
 
     owner_hot = (jnp.arange(adapters, dtype=jnp.int32)[:, None] == ids_all[None, :]).astype(F32)
-    stored = expert_grads.shape[1]
-    share = experts_dev * stored // reps
+    share = experts_dev * 4 * RANK // reps
     swapped = lax.all_to_all(
-        expert_grads.reshape(reps, share, LANES), "rep", split_axis=0, concat_axis=0, tiled=True
+        expert_grads.reshape(reps, share, width), "rep", split_axis=0, concat_axis=0, tiled=True
     )
     summed = jnp.sum(owner_hot[:, :, None, None] * swapped.astype(F32)[None], axis=1).astype(BF16)
-    spread = lax.all_gather(summed, "rep", axis=1).reshape(adapters, experts_dev, stored, LANES)
-
-    def lanes_joined(rows, height):
-        return rows.reshape(adapters, experts_dev, -1, height, LANES).swapaxes(2, 3).reshape(
-            adapters, experts_dev, height, -1
-        )
-
-    parts = width // LANES
-    edges = [0, parts * 2 * RANK, parts * 2 * RANK + 2 * RANK, parts * 2 * RANK + 3 * RANK, stored]
-    grad_a_gateup = lanes_joined(spread[:, :, : edges[1]], 2 * RANK).swapaxes(2, 3).astype(F32)
-    grad_b_gateup = spread[:, :, edges[1] : edges[2]].reshape(adapters, experts_dev, 2, RANK, FF).astype(F32)
-    grad_a_down = spread[:, :, edges[2] : edges[3]].swapaxes(2, 3).astype(F32)
-    grad_b_down = lanes_joined(spread[:, :, edges[3] :], RANK).astype(F32)
-
-    both = lax.psum_scatter(
-        jnp.concatenate([part_d, part_result], axis=1), "grp", scatter_dimension=0, tiled=True
-    ).astype(F32)
-    d_gates = lax.all_to_all(part_gates, "grp", split_axis=1, concat_axis=0, tiled=True)
+    spread = lax.all_gather(summed, "rep", axis=0)
+    grad_a_gateup, grad_b_gateup, grad_a_down, grad_b_down = unpack_grads(spread, experts_dev)
+
+    if groups == 2:
+        d_gates = in_order(part_gates[:, 0], from_others(part_gates[:, 1]))
+    else:
+        d_gates = jnp.roll(part_gates, member, axis=1)
+        d_gates = lax.all_to_all(d_gates, "grp", split_axis=1, concat_axis=0, tiled=True)
     d_gates = d_gates.reshape(experts, count).T
-    result = (middle + both[:, width:]).astype(BF16)
+    d_sum = to_owners(d_near, d_far)
+    result_far, d_sum = lax.optimization_barrier((result_far, d_sum))
+    result = (middle + to_owners(result_near, result_far)).astype(BF16)
     upstream = cotangent.astype(F32)
     d_logits = (gates * (d_gates - jnp.sum(gates * d_gates, axis=1, keepdims=True))).astype(BF16)
 
     d_router_rank = product_back(d_logits, router_out).astype(BF16)
-    d_normed_ffn = both[:, :width] + product(d_logits, router_full) + product(d_router_rank, router_in)
+    d_normed_ffn = d_sum + product(d_logits, router_full) + product(d_router_rank, router_in)
     grad_router_out = product_outer(router_rank, d_logits)
     grad_router_in = product_outer(d_router_rank, normed_ffn)
     d_middle = upstream + rms_back(middle, ffn_gain, d_normed_ffn)
@@ -515,34 +885,12 @@
     attended_gradient = (product_back(d_attn, output_full) + product(d_out_rank, output_in)).astype(BF16)
     grad_output_out = product_outer(out_rank, d_attn)
     grad_output_in = product_outer(d_out_rank, attended)
-    heads_gradient = attended_gradient.reshape(count, KEY_VALUE_HEADS, per_kv, HEAD_SIZE).transpose(1, 0, 2, 3)
-
-    def attend_back(operands):
-        query_grp, key_grp, value_grp, d_grp, log_total = operands
-        scores = jnp.einsum("qrd,kd->rqk", query_grp, key_grp, preferred_element_type=F32) * scale
-        scores = jnp.where(mask[None], scores, -1e30)
-        probs = jnp.exp(scores - log_total[..., None])
-        d_value = jnp.einsum("rqk,qrd->kd", probs.astype(BF16), d_grp, preferred_element_type=F32)
-        d_probs = jnp.einsum("qrd,kd->rqk", d_grp, value_grp, preferred_element_type=F32)
-        d_scores = (probs * (d_probs - jnp.sum(probs * d_probs, axis=-1, keepdims=True))).astype(BF16)
-        d_query = jnp.einsum("rqk,kd->qrd", d_scores, key_grp, preferred_element_type=F32) * scale
-        d_key = jnp.einsum("rqk,qrd->kd", d_scores, query_grp, preferred_element_type=F32) * scale
-        return (d_query, d_key, d_value)
-
-    d_query_heads, d_key_heads, d_value_heads = lax.map(
-        attend_back, (heads_of_query, heads_of_key, heads_of_value, heads_gradient, log_totals)
-    )
-    d_queries = d_query_heads.transpose(1, 0, 2, 3).reshape(count, width).astype(BF16)
-    d_keys_part = d_key_heads.transpose(1, 0, 2).reshape(tree_length, kv_width)
-    d_values_part = d_value_heads.transpose(1, 0, 2).reshape(tree_length, kv_width)
-    d_keyvals = lax.psum_scatter(
-        jnp.concatenate([d_keys_part, d_values_part], axis=1).astype(BF16),
-        "grp",
-        scatter_dimension=0,
-        tiled=True,
-    )
-    d_keys = d_keyvals[:, :kv_width]
-    d_values = d_keyvals[:, kv_width:]
+    d_queries, d_keys, d_values, d_keys_far, d_values_far = run_attention_back(
+        listing, steps, query_rows, keyvals, keyvals_far, own_bias, live, attended, attended_gradient, logs
+    )
+    d_keys = to_owners(d_keys, d_keys_far).astype(BF16)
+    d_values = to_owners(d_values, d_values_far).astype(BF16)
+    d_keyvals = jnp.concatenate([d_keys, d_values], axis=1)
     d_rank_qkv = jnp.concatenate(
         [
             product_back(d_queries, query_out),
@@ -604,9 +952,9 @@
         owned[4],
         owned[5].swapaxes(1, 2),
         owned[6],
-        grad_a_gateup,
+        grad_a_gateup.swapaxes(2, 3),
         grad_b_gateup,
-        grad_a_down,
+        grad_a_down.swapaxes(2, 3),
         grad_b_down,
     )
 

time: 1040 us -> 738 us (0.71)
  matrix products: 200 us -> 49.8 us
  local copies, waits for them, and re-layouts: 170 us -> 38.1 us
  Pallas kernels: 225 us -> 296 us
  waiting for transfers between devices: 227 us -> 157 us
  starting transfers between devices: 19.1 us -> 88.7 us
  other arithmetic: 107 us -> 42.7 us
  blocking collectives: 66 us -> 39.4 us
    dot_general x56 -> x0, matrix products: 149 us -> none  [the longest x8 27.4 us: attend_back(): jnp.einsum('rqk,qrd->kd', probs.astype(BF16), d_grp, preferred_element_ty...]
    pallas_call x0 -> x3, Pallas kernels: none -> 70.7 us  [the longest x1 33.1 us: run_attention_back(): pl.pallas_call(functools.partial(attend_back_kernel, here=here, segs=segs...]
    convert_element_type x6 -> x0, local copies, waits for them, and re-layouts: 70 us -> none  [the longest x2 39.2 us: local(): lanes_joined(spread[:, :, :edges[1]], 2 * RANK).swapaxes(2, 3).astype(F32)]
    reduce_scatter x2 -> x0, waiting for transfers between devices: 62.4 us -> none  [the longest x1 62.4 us: local(): lax.psum_scatter(jnp.concatenate([part_d, part_result], axis=1), 'grp', s...]
    ppermute x3 -> x14, starting transfers between devices: 4.99 us -> 62.4 us  [the longest x4 34.8 us: to_owners(): lax.ppermute(far, 'grp', swap_pairs(2)).astype(F32)]
    all_gather x3 -> x0, blocking collectives: 26.5 us -> none  [the longest x1 14.9 us: local(): small_all = lax.all_gather(small, 'grp', axis=0)]
    convert_element_type x11 -> x2, other arithmetic: 24.9 us -> 2.35 us  [the longest x1 1.18 us: local(): d_keys = to_owners(d_keys, d_keys_far).astype(BF16)]
    and x16 -> x0, other arithmetic: 22.4 us -> none  [tree_mask(): return jnp.logical_and(jnp.logical_and(linked, causal), live)]
  transfers between devices with their start and end apart: 15 -> 20, of which waited for: 6 -> 9; matrix products, arithmetic and copies ran while one was open for 35% -> 16% of each run, Pallas kernels for 0% -> 7%
where the time goes in v2:
time: 738 us; the launch traced here: 728 us
  Pallas kernels  296 us (40%)
  waiting for transfers between devices  157 us (21%)
  starting transfers between devices  88.7 us (12%)
  matrix products  49.8 us (7%)
  other arithmetic  42.7 us (6%)
  blocking collectives  39.4 us (5%)
  local copies, waits for them, and re-layouts  38.1 us (5%)
  between operations  16.4 us (2%)
    pallas_call x1, Pallas kernels, run_experts(): pl.pallas_call(functools.partial(expert_kernel, blocks=blocks, rows_block...  226 us
    all_gather x1, waiting for transfers between devices, local(): spread = lax.all_gather(summed, 'rep', axis=0)  54.1 us
    ppermute x7, waiting for transfers between devices, from_others(): return lax.ppermute(piece, 'grp', swap_pairs(2))  50.6 us
    ppermute x4, starting transfers between devices, to_owners(): lax.ppermute(far, 'grp', swap_pairs(2)).astype(F32)  34.8 us
    pallas_call x1, Pallas kernels, run_attention_back(): pl.pallas_call(functools.partial(attend_back_kernel, here=here, segs=segs...  33.1 us
    ppermute x4, waiting for transfers between devices, to_owners(): lax.ppermute(far, 'grp', swap_pairs(2)).astype(F32)  27.6 us
    dot_general x12, matrix products, product(): return jnp.dot(left, right, preferred_element_type=F32)  25.9 us
    all_gather x1, blocking collectives, local(): dense = lax.all_gather(dense, 'rep', axis=1).reshape(adapters, -1)  24.1 us
  transfers between devices with their start and end apart: 20, of which 9 were waited for; matrix products, arithmetic and copies ran while one was open for 16% of the time, Pallas kernels for 7%

profile of v2, /device:TPU:0, one launch (start us, length us, event | category | flops | bytes accessed | tf_op | source)
XLA Modules:
  0.0 728.4 jit_solution(613382553243091035)
XLA Ops:
  33.1 5.1 collective-permute-done
  40.6 12.6 %collective-permute-done.2 = bf16[384,1024]{1,0:T(8,128)(2,1)} collective-permute-done((bf16[384,1024]{1,0:T(8,128)(2,1)}, bf16[384,1024]{1,0:T(8,128)(2,1)}, u32[]{:S(2)}, u32[]{:S(2)}) %collective-permute-start.2) | collective-permute-done | bytes 786464 | tf_op jit(solution)/shard_map/ppermute | solution.py:661
  64.5 22.5 %collective-permute-done.4.k_far.v_far = bf16[512,1024]{1,0:T(8,128)(2,1)S(1)} collective-permute-done((bf16[512,1024]{1,0:T(8,128)(2,1)S(1)}, bf16[512,1024]{1,0:T(8,128)(2,1)S(1)}, u32[]{:S(2)}, u32[]{:S(2)}) %collective-permute-start.4) | collective-permute-done | bytes 1048608 | tf_op jit(solution)/shard_map/ppermute | solution.py:635
  88.2 6.8 fusion.16.q_ref
  95.1 18.9 %attention.1 = (bf16[512,1536]{1,0:T(8,128)(2,1)S(1)}, f32[4,512,128]{2,1,0:T(8,128)S(1)}) custom-call(s32[64]{0:T(128)S(1)} %reshape.372.list_ref, s32[4]{0:T(128)S(1)} %and_select_fusion.steps_ref, bf16[512,1536]{1,0:T(8,128)(2,1)S(1)} %fusion.16.q_ref, bf16[512,1024]{1,0:T(8,128)(2,1)S(1)} %pad_maximum_fusion.k_ref.v_ref, ...), custom_call_target="tpu_custom_call" | custom-call | flops 40000000000 | bytes 8000000 | tf_op jit(solution)/shard_map/attention/pallas_call | solution.py:327
  117.8 6.9 multiply_reduce_fusion.2
  126.8 19.9 %collective-permute-start.6 = (bf16[512,1536]{1,0:T(8,128)(2,1)S(1)}, bf16[512,1536]{1,0:T(8,128)(2,1)}, u32[]{:S(2)}, u32[]{:S(2)}) collective-permute-start(bf16[512,1536]{1,0:T(8,128)(2,1)S(1)} %multiply_convert_fusion.x_ref), channel_id=1, source_target_pairs={{0,1},{1,0},{2,3},{3,2},{4,5},{5,4},{6,7},{7,6},{8,9},{9,8},{10,11... | collective-permute-start | bytes 4718600 | tf_op jit(solution)/shard_map/ppermute | solution.py:635
  149.8 21.6 %collective-permute-done.9 = f32[20,512]{1,0:T(8,128)S(1)} collective-permute-done((f32[20,512]{1,0:T(8,128)S(1)}, f32[20,512]{1,0:T(8,128)S(1)}, u32[]{:S(2)}, u32[]{:S(2)}) %collective-permute-start.9) | collective-permute-done | bytes 40992 | tf_op jit(solution)/shard_map/ppermute | solution.py:635
  172.1 225.6 %experts.1 = (bf16[512,1536]{1,0:T(8,128)(2,1)}, bf16[512,1536]{1,0:T(8,128)(2,1)}, bf16[512,1536]{1,0:T(8,128)(2,1)}, bf16[512,1536]{1,0:T(8,128)(2,1)}, f32[20...) custom-call(s32[1]{0:T(128)} %copy.185.chosen_ref, bf16[512,1536]{1,0:T(8,128)(2,1)} %copy-done.29, ...), custom_call_target="tpu_custom_call" | custom-call | flops 199999995904 | bytes 100000000 | tf_op jit(solution)/shard_map/experts/pallas_call | solution.py:512
  400.9 15.4 %all-reduce.3 = s32[16]{0:T(128)S(1)} all-reduce(s32[16]{0:T(128)S(1)} %dynamic-update-slice), channel_id=1, replica_groups=mesh['rep'=16,'grp'=2] {'rep'}, use_global_device_ids=true, to_apply=%add.3 | all-reduce | flops 16 | bytes 128
  417.3 5.2 all-to-all-start.1
  434.3 27.6 %collective-permute-done.11 = bf16[512,1536]{1,0:T(8,128)(2,1)} collective-permute-done((bf16[512,1536]{1,0:T(8,128)(2,1)}, bf16[512,1536]{1,0:T(8,128)(2,1)}, u32[]{:S(2)}, u32[]{:S(2)}) %collective-permute-start.11) | collective-permute-done | bytes 1572896 | tf_op jit(solution)/shard_map/ppermute | solution.py:644
  462.0 4.2 multiply_add_fusion
  469.8 5.8 fusion.17.do_ref
  475.7 33.1 %attention_back.1 = (bf16[512,1536]{1,0:T(8,128)(2,1)S(1)}, bf16[512,512]{1,0:T(8,128)(2,1)S(1)}, bf16[512,512]{1,0:T(8,128)(2,1)S(1)}, bf16[512,512]{1,0:T(8,128)(2,1)}, bf16[512,512]{1,0:T(8,128)(2,1)}) custom-call(s32[64]{0:T(128)S(1)} %copy-done.15, s32[4]{0:T(128)S(1)} %copy-done.20, bf16[512,1536]{1,0:T(8,128)(2,1)S(1)} %copy-done.22, ...), custom_call_target="tpu_custom_call" | custom-call | flops 70000001024 | bytes 12000000 | tf_op jit(solution)/shard_map/attention_back/pallas_call | solution.py:360
  510.4 31.5 %collective-permute-start.13 = (bf16[512,512]{1,0:T(8,128)(2,1)}, bf16[512,512]{1,0:T(8,128)(2,1)}, u32[]{:S(2)}, u32[]{:S(2)}) collective-permute-start(bf16[512,512]{1,0:T(8,128)(2,1)} %get-tuple-element.78), channel_id=1, source_target_pairs={{0,1},{1,0},{2,3},{3,2},{4,5},{5,4},{6,7},{7,6},{8,9},{9,8},{10,11... | collective-permute-start | bytes 1572872 | tf_op jit(solution)/shard_map/ppermute | solution.py:644
  542.2 6.4 convert_element_type.289
  548.6 6.8 multiply_reduce_fusion
  571.3 20.9 %all-to-all-start = ((bf16[32,2,3008]{2,1,0:T(2,128)(2,1)}), bf16[32,2,3008]{2,1,0:T(2,128)(2,1)S(1)}, u32[]{:S(2)}, u32[]{:S(2)}) async-start(bf16[32,2,3008]{2,1,0:T(2,128)(2,1)} %reshape.430), calls=%async_computation | async-start | bytes 786432 | tf_op jit(solution)/shard_map/all_to_all | solution.py:940
  597.7 5.2 fusion.10
  604.8 10.1 %all-to-all-done = bf16[32,2,3008]{2,1,0:T(2,128)(2,1)S(1)} async-done(((bf16[32,2,3008]{2,1,0:T(2,128)(2,1)}), bf16[32,2,3008]{2,1,0:T(2,128)(2,1)S(1)}, u32[]{:S(2)}, u32[]{:S(2)}) %all-to-all-start) | async-done | bytes 385056 | tf_op jit(solution)/shard_map/all_to_all | solution.py:940
  619.3 24.1 %all-gather = bf16[4,96256]{1,0:T(4,128)(2,1)S(1)} all-gather(bf16[4,6016]{1,0:T(4,128)(2,1)S(1)} %multiply_reduce_fusion.3), channel_id=2, replica_groups=mesh['rep'=16,'grp'=2] {'rep'}, dimensions={1}, use_global_device_ids=true | all-gather | bytes 818176 | tf_op jit(solution)/shard_map/all_gather | solution.py:943
  648.7 54.1 %all-gather.10.cloned.1.call-done = bf16[64,80,1536]{2,1,0:T(8,128)(2,1)} async-done(((bf16[4,80,1536]{2,1,0:T(8,128)(2,1)}), bf16[64,80,1536]{2,1,0:T(8,128)(2,1)}) %all-gather.10.cloned.1.call-update) | async-done | bytes 15728656 | tf_op jit(solution)/shard_map/all_gather | solution.py:863
  702.8 18.7 %unpack.1 = (f32[4,20,32,1536]{3,2,1,0:T(8,128)}, f32[4,20,2,16,512]{4,3,2,1,0:T(8,128)}, f32[4,20,16,512]{3,2,1,0:T(8,128)}, f32[4,20,16,1536]{3,2,1,0:T(8,128)}) custom-call(bf16[16,4,80,1536]{3,2,1,0:T(8,128)(2,1)} %bitcast.201), custom_call_target="tpu_custom_call" | custom-call | bytes 50000000 | tf_op jit(solution)/shard_map/unpack/pallas_call | solution.py:604
  (404 shorter events, 105.2 us)
Async XLA Ops:
  7.2 81.0 %all-gather.6.cloned.1.call-start = ((), (), s32[]{:S(2)}) async-start(), calls=%async_computation.2 | async-start | bytes 2506752 | tf_op jit(solution)/shard_map/all_gather | solution.py:675
  7.3 24.9 %collective-permute-start.8 = (s32[512,8]{0,1:T(8,128)}, s32[512,8]{0,1:T(8,128)S(1)}, u32[]{:S(2)}, u32[]{:S(2)}) collective-permute-start(s32[512,8]{0,1:T(8,128)} %param.29), channel_id=1, source_target_pairs={{0,1},{1,0},{2,3},{3,2},{4,5},{5,4},{6,7},{7,6},{8,9},{9,8},{10,11... | collective-permute-start | bytes 49160 | tf_op jit(solution)/shard_map/ppermute | solution.py:635
  11.2 21.2 %collective-permute-start.5 = (bf16[48,1536]{1,0:T(8,128)(2,1)S(1)}, bf16[48,1536]{1,0:T(8,128)(2,1)S(1)}, u32[]{:S(2)}, u32[]{:S(2)}) collective-permute-start(bf16[48,1536]{1,0:T(8,128)(2,1)S(1)} %constant_dynamic-slice_fusion), channel_id=1, source_target_pairs={{0,1},{1,0},{2,3},{3,2},{4,5},{5,4},{6,7},{7,6},{8,9},{9,8},{10,11... | collective-permute-start | bytes 442376 | tf_op jit(solution)/shard_map/ppermute | solution.py:674
  13.0 14.8 %collective-permute-start.1 = (bf16[48,1536]{1,0:T(8,128)(2,1)}, bf16[48,1536]{1,0:T(8,128)(2,1)S(1)}, u32[]{:S(2)}, u32[]{:S(2)}) collective-permute-start(bf16[48,1536]{1,0:T(8,128)(2,1)} %constant_dynamic-slice_fusion.2), channel_id=1, source_target_pairs={{0,1},{1,0},{2,3},{3,2},{4,5},{5,4},{6,7},{7,6},{8,9},{9,8},{10,11... | collective-permute-start | bytes 442376 | tf_op jit(solution)/shard_map/ppermute | solution.py:674
  23.6 14.7 %collective-permute-start = (bf16[1,128000]{1,0:T(2,128)(2,1)S(1)}, bf16[1,128000]{1,0:T(2,128)(2,1)S(1)}, u32[]{:S(2)}, u32[]{:S(2)}) collective-permute-start(bf16[1,128000]{1,0:T(2,128)(2,1)S(1)} %broadcast_in_dim.112), channel_id=1, source_target_pairs={{0,1},{1,0},{2,3},{3,2},{4,5},{5,4},{6,7},{7,6},{8,9},{9,8},{10,11... | collective-permute-start | bytes 768008 | tf_op jit(solution)/shard_map/ppermute | solution.py:635
  25.9 27.3 %collective-permute-start.2 = (bf16[384,1024]{1,0:T(8,128)(2,1)}, bf16[384,1024]{1,0:T(8,128)(2,1)}, u32[]{:S(2)}, u32[]{:S(2)}) collective-permute-start(bf16[384,1024]{1,0:T(8,128)(2,1)} %constant_dynamic-slice_fusion.1), channel_id=1, source_target_pairs={{0,1},{1,0},{2,3},{3,2},{4,5},{5,4},{6,7},{7,6},{8,9},{9,8},{10,11... | collective-permute-start | bytes 2359304 | tf_op jit(solution)/shard_map/ppermute | solution.py:661
  28.5 89.4 %all-gather.8.cloned.1.call-start = ((), (), s32[]{:S(2)}) async-start(), calls=%async_computation.3 | async-start | bytes 2506752 | tf_op jit(solution)/shard_map/all_gather | solution.py:675
  53.2 3.1 collective-permute-start.3
  61.7 25.3 %collective-permute-start.4 = (bf16[512,1024]{1,0:T(8,128)(2,1)S(1)}, bf16[512,1024]{1,0:T(8,128)(2,1)S(1)}, u32[]{:S(2)}, u32[]{:S(2)}) collective-permute-start(bf16[512,1024]{1,0:T(8,128)(2,1)S(1)} %pad_maximum_fusion.k_ref.v_ref), channel_id=1, source_target_pairs={{0,1},{1,0},{2,3},{3,2},{4,5},{5,4},{6,7},{7,6},{8,9},{9,8},{10,11... | collective-permute-start | bytes 3145736 | tf_op jit(solution)/shard_map/ppermute | solution.py:635
  87.9 84.2 %collective-permute-start.7 = (bf16[512,1536]{1,0:T(8,128)(2,1)}, bf16[512,1536]{1,0:T(8,128)(2,1)}, u32[]{:S(2)}, u32[]{:S(2)}) collective-permute-start(bf16[512,1536]{1,0:T(8,128)(2,1)} %g_ref.1), channel_id=1, source_target_pairs={{0,1},{1,0},{2,3},{3,2},{4,5},{5,4},{6,7},{7,6},{8,9},{9,8},{10,11... | collective-permute-start | bytes 4718600 | tf_op jit(solution)/shard_map/ppermute | solution.py:635
  126.8 45.3 %collective-permute-start.6 = (bf16[512,1536]{1,0:T(8,128)(2,1)S(1)}, bf16[512,1536]{1,0:T(8,128)(2,1)}, u32[]{:S(2)}, u32[]{:S(2)}) collective-permute-start(bf16[512,1536]{1,0:T(8,128)(2,1)S(1)} %multiply_convert_fusion.x_ref), channel_id=1, source_target_pairs={{0,1},{1,0},{2,3},{3,2},{4,5},{5,4},{6,7},{7,6},{8,9},{9,8},{10,11... | collective-permute-start | bytes 4718600 | tf_op jit(solution)/shard_map/ppermute | solution.py:635
  147.4 250.3 %copy-start.72 = (bf16[16,40]{1,0:T(8,128)(2,1)}, bf16[16,40]{1,0:T(8,128)(2,1)S(1)}, u32[]{:S(2)}) copy-start(bf16[16,40]{1,0:T(8,128)(2,1)S(1)} %reshape.392) | copy-start | bytes 3844
  147.9 249.8 %copy-start.64 = (bf16[512,16]{0,1:T(8,128)(2,1)}, bf16[512,16]{0,1:T(8,128)(2,1)S(1)}, u32[]{:S(2)}) copy-start(bf16[512,16]{0,1:T(8,128)(2,1)S(1)} %convolution_convert_fusion.9) | copy-start | bytes 49156
  148.9 248.8 %copy-start.38 = (f32[512,40]{0,1:T(8,128)}, f32[512,40]{0,1:T(8,128)S(1)}, u32[]{:S(2)}) copy-start(f32[512,40]{0,1:T(8,128)S(1)} %fusion.30) | copy-start | bytes 245764
  149.0 22.4 %collective-permute-start.9 = (f32[20,512]{1,0:T(8,128)S(1)}, f32[20,512]{1,0:T(8,128)S(1)}, u32[]{:S(2)}, u32[]{:S(2)}) collective-permute-start(f32[20,512]{1,0:T(8,128)S(1)} %get-tuple-element.133), channel_id=1, source_target_pairs={{0,1},{1,0},{2,3},{3,2},{4,5},{5,4},{6,7},{7,6},{8,9},{9,8},{10,11... | collective-permute-start | bytes 122888 | tf_op jit(solution)/shard_map/ppermute | solution.py:635
  172.1 227.4 %copy-start.90 = (u32[32]{0:T(128)S(1)}, u32[32]{0:T(128)}, u32[]{:S(2)}) copy-start(u32[32]{0:T(128)} %constant.139) | copy-start | bytes 388
  397.7 26.3 %collective-permute-start.10 = (bf16[512,1536]{1,0:T(8,128)(2,1)}, bf16[512,1536]{1,0:T(8,128)(2,1)S(1)}, u32[]{:S(2)}, u32[]{:S(2)}) collective-permute-start(bf16[512,1536]{1,0:T(8,128)(2,1)} %get-tuple-element.71), channel_id=1, source_target_pairs={{0,1},{1,0},{2,3},{3,2},{4,5},{5,4},{6,7},{7,6},{8,9},{9,8},{10,11... | collective-permute-start | bytes 4718600 | tf_op jit(solution)/shard_map/ppermute | solution.py:644
  417.2 6.8 collective-permute-start.12
  417.3 124.9 %all-to-all-start.1 = ((bf16[16,80,1536]{2,1,0:T(8,128)(2,1)}), bf16[16,80,1536]{2,1,0:T(8,128)(2,1)}, u32[]{:S(2)}, u32[]{:S(2)}) async-start(bf16[16,80,1536]{2,1,0:T(8,128)(2,1)} %bitcast.202), calls=%async_computation.1 | async-start | bytes 7864320 | tf_op jit(solution)/shard_map/all_to_all | solution.py:859
  422.5 280.3 %all-gather.10.cloned.1.call-start = ((), (), s32[]{:S(2)}) async-start(), calls=%async_computation.4 | async-start | bytes 16711680 | tf_op jit(solution)/shard_map/all_gather | solution.py:863
  426.2 35.8 %collective-permute-start.11 = (bf16[512,1536]{1,0:T(8,128)(2,1)}, bf16[512,1536]{1,0:T(8,128)(2,1)}, u32[]{:S(2)}, u32[]{:S(2)}) collective-permute-start(bf16[512,1536]{1,0:T(8,128)(2,1)} %get-tuple-element.72), channel_id=1, source_target_pairs={{0,1},{1,0},{2,3},{3,2},{4,5},{5,4},{6,7},{7,6},{8,9},{9,8},{10,11... | collective-permute-start | bytes 4718600 | tf_op jit(solution)/shard_map/ppermute | solution.py:644
  510.4 47.6 %collective-permute-start.13 = (bf16[512,512]{1,0:T(8,128)(2,1)}, bf16[512,512]{1,0:T(8,128)(2,1)}, u32[]{:S(2)}, u32[]{:S(2)}) collective-permute-start(bf16[512,512]{1,0:T(8,128)(2,1)} %get-tuple-element.78), channel_id=1, source_target_pairs={{0,1},{1,0},{2,3},{3,2},{4,5},{5,4},{6,7},{7,6},{8,9},{9,8},{10,11... | collective-permute-start | bytes 1572872 | tf_op jit(solution)/shard_map/ppermute | solution.py:644
  541.8 18.1 %collective-permute-start.14 = (bf16[512,512]{1,0:T(8,128)(2,1)}, bf16[512,512]{1,0:T(8,128)(2,1)}, u32[]{:S(2)}, u32[]{:S(2)}) collective-permute-start(bf16[512,512]{1,0:T(8,128)(2,1)} %get-tuple-element.80), channel_id=1, source_target_pairs={{0,1},{1,0},{2,3},{3,2},{4,5},{5,4},{6,7},{7,6},{8,9},{9,8},{10,11... | collective-permute-start | bytes 1572872 | tf_op jit(solution)/shard_map/ppermute | solution.py:644
  571.3 43.6 %all-to-all-start = ((bf16[32,2,3008]{2,1,0:T(2,128)(2,1)}), bf16[32,2,3008]{2,1,0:T(2,128)(2,1)S(1)}, u32[]{:S(2)}, u32[]{:S(2)}) async-start(bf16[32,2,3008]{2,1,0:T(2,128)(2,1)} %reshape.430), calls=%async_computation | async-start | bytes 786432 | tf_op jit(solution)/shard_map/all_to_all | solution.py:940
  (88 other events, 1361.5 us)
Sparse Core Ops, SparseCore 0:
  28.6 42.5 all-gather.5
  74.1 41.0 all-gather.7
  555.5 147.1 all-gather.9

commit v3 on v2

--- a/solution.py
+++ b/solution.py
@@ -15,6 +15,7 @@
 RANK = 16
 SEG = 128
 FLUSH = 5
+UNIT = 768
 
 EPSILON = 1e-05
 BF16 = jnp.bfloat16
@@ -205,20 +206,13 @@
     o_ref,
     do_ref,
     l_ref,
-    dq_ref,
-    dk_ref,
-    dv_ref,
-    dk_far,
-    dv_far,
-    kf,
-    vf,
-    dkf,
-    dvf,
-    *,
+    *refs,
     here,
     segs,
     scale,
+    after,
 ):
+    dq_ref, dk_ref, dv_ref, dk_far, dv_far, kf, vf, dkf, dvf = refs[after:]
     fill_doubled(kf, k_ref, k_far)
     fill_doubled(vf, v_ref, v_far)
     dkf[...] = jnp.zeros_like(dkf)
@@ -304,14 +298,14 @@
     return listing.reshape(-1), steps.astype(jnp.int32), own_bias, live
 
 
-def attention_specs(count, far, here, segs):
+def attention_specs(count, far, here, segs, skip=0):
     narrow = 2 * HEAD_SIZE
-    shift = KEY_VALUE_HEADS // 2
+    shift = KEY_VALUE_HEADS // 2 + skip
     return [
-        pl.BlockSpec((count, 3 * narrow), lambda h, a, b: (0, h)),
-        pl.BlockSpec((count, narrow), lambda h, a, b: (0, h)),
+        pl.BlockSpec((count, 3 * narrow), lambda h, a, b: (0, h + skip)),
+        pl.BlockSpec((count, narrow), lambda h, a, b: (0, h + skip)),
         pl.BlockSpec((count, narrow), lambda h, a, b: (0, h + shift)),
-        pl.BlockSpec((far, narrow), lambda h, a, b: (0, h)),
+        pl.BlockSpec((far, narrow), lambda h, a, b: (0, h + skip)),
         pl.BlockSpec((far, narrow), lambda h, a, b: (0, h + shift)),
         pl.BlockSpec((here, SEG, SEG), lambda h, a, b: (0, 0, 0)),
         pl.BlockSpec((segs + 1, 1, SEG), lambda h, a, b: (0, 0, 0)),
@@ -348,35 +342,41 @@
     )(listing, steps, queries, near, near, far, far, own_bias, live)
 
 
-def run_attention_back(listing, steps, queries, near, far, own_bias, live, attended, gradient, logs):
-    count, width = queries.shape
+def run_attention_back(
+    listing, steps, queries, near, far, own_bias, live, attended, gradient, logs, skip, pairs, after=()
+):
+    count = queries.shape[0]
     tree_length = count + far.shape[0]
     here, segs = count // SEG, tree_length // SEG
-    pairs = KEY_VALUE_HEADS // 2
     narrow = 2 * HEAD_SIZE
-    rows = pl.BlockSpec((count, 3 * narrow), lambda h, a, b: (0, h))
+    rows = pl.BlockSpec((count, 3 * narrow), lambda h, a, b: (0, h + skip))
     outs = [pl.BlockSpec((count, narrow), lambda h, a, b: (0, h))] * 2
     outs += [pl.BlockSpec((far.shape[0], narrow), lambda h, a, b: (0, h))] * 2
     return pl.pallas_call(
-        functools.partial(attend_back_kernel, here=here, segs=segs, scale=HEAD_SIZE ** (-0.5)),
+        functools.partial(
+            attend_back_kernel, here=here, segs=segs, scale=HEAD_SIZE ** (-0.5), after=len(after)
+        ),
         grid_spec=pltpu.PrefetchScalarGridSpec(
             num_scalar_prefetch=2,
             grid=(pairs,),
-            in_specs=attention_specs(count, far.shape[0], here, segs)
-            + [rows, rows, pl.BlockSpec((1, count, narrow), lambda h, a, b: (h, 0, 0))],
-            out_specs=[rows] + outs,
+            in_specs=attention_specs(count, far.shape[0], here, segs, skip)
+            + [rows, rows, pl.BlockSpec((1, count, narrow), lambda h, a, b: (h + skip, 0, 0))]
+            + [pl.BlockSpec(memory_space=pl.ANY)] * len(after),
+            out_specs=[pl.BlockSpec((count, 3 * narrow), lambda h, a, b: (0, h))] + outs,
             scratch_shapes=[pltpu.VMEM((2, tree_length, narrow), BF16)] * 2
             + [pltpu.VMEM((2, tree_length, narrow), F32)] * 2,
         ),
-        out_shape=[jax.ShapeDtypeStruct((count, width), BF16)]
+        out_shape=[jax.ShapeDtypeStruct((count, 3 * pairs * narrow), BF16)]
         + [jax.ShapeDtypeStruct((count, pairs * narrow), BF16)] * 2
         + [jax.ShapeDtypeStruct((far.shape[0], pairs * narrow), BF16)] * 2,
         compiler_params=pltpu.CompilerParams(
             vmem_limit_bytes=40 * 1024 * 1024, dimension_semantics=("arbitrary",)
         ),
-        cost_estimate=pl.CostEstimate(flops=70_000_000_000, bytes_accessed=12_000_000, transcendentals=10_000_000),
+        cost_estimate=pl.CostEstimate(
+            flops=17_000_000_000 * pairs, bytes_accessed=3_000_000 * pairs, transcendentals=0
+        ),
         name="attention_back",
-    )(listing, steps, queries, near, near, far, far, own_bias, live, attended, gradient, logs)
+    )(listing, steps, queries, near, near, far, far, own_bias, live, attended, gradient, logs, *after)
 
 
 def expert_kernel(
@@ -393,37 +393,47 @@
     b1_ref,
     a2_ref,
     b2_ref,
-    r_out,
-    r_far,
-    d_out,
-    d_far,
-    dg_out,
-    grad_out,
-    hot_s,
-    o_s,
-    dx_s,
-    accr,
-    accd,
-    x_s,
-    g_s,
-    gate_s,
-    b1_s,
-    dgu_s,
-    *,
+    *refs,
     blocks,
     rows_block,
     cap,
     flush,
+    carried,
 ):
+    held = refs[:4] if carried else ()
+    (
+        r_out,
+        r_far,
+        d_out,
+        d_far,
+        dg_out,
+        grad_out,
+        hot_s,
+        o_s,
+        dx_s,
+        accr,
+        accd,
+        x_s,
+        g_s,
+        gate_s,
+        b1_s,
+        dgu_s,
+    ) = refs[len(held) :]
     e = pl.program_id(0)
     slot = lax.rem(e, flush)
     width = x_ref.shape[-1]
+    halves = width // UNIT
 
     @pl.when(e == 0)
     def _():
         b1_s[...] = jnp.zeros_like(b1_s)
-        accr[...] = jnp.zeros_like(accr)
-        accd[...] = jnp.zeros_like(accd)
+        if carried:
+            for n, acc in enumerate((accr, accd)):
+                acc[0:rows_block, :] = held[2 * n][...].astype(F32)
+                acc[rows_block:, :] = held[2 * n + 1][...].astype(F32)
+        else:
+            accr[...] = jnp.zeros_like(accr)
+            accd[...] = jnp.zeros_like(accd)
 
     at = pl.multiple_of(slot * cap, 16)
     for b in range(blocks):
@@ -444,26 +454,26 @@
 
     x = x_s[...]
     gate_col = gate_s[...]
-    rank_in = product_back(x, a1_ref[0, 0]).astype(BF16)
-    pre = product(x, w1_ref[0]) + product(rank_in, b1_s[...])
+    rank_in = product_back(a1_ref[0, 0], x).astype(BF16)
+    pre = product(x, w1_ref[0])
     gate_pre = pre[:, :FF]
     up_pre = pre[:, FF:]
     sig = 1.0 / (1.0 + jnp.exp(-gate_pre))
     act = gate_pre * sig
     hidden = (act * up_pre).astype(BF16)
-    rank_down = product_back(hidden, a2_ref[0, 0]).astype(BF16)
-    out = (product(hidden, w2_ref[0]) + product(rank_down, b2_ref[0, 0])).astype(BF16).astype(F32)
+    rank_down = product_back(a2_ref[0, 0], hidden).astype(BF16)
+    out = product(hidden, w2_ref[0]).astype(BF16).astype(F32)
     g = g_s[...].astype(F32)
     d_gate_col = jnp.sum(g * out, axis=1, keepdims=True)
     out = (gate_col * out).astype(BF16)
     d_exp = (gate_col * g).astype(BF16)
-    d_rank_down = product_back(d_exp, b2_ref[0, 0]).astype(BF16)
-    d_hidden = product_back(d_exp, w2_ref[0]) + product(d_rank_down, a2_ref[0, 0])
+    d_rank_down = product_back(b2_ref[0, 0], d_exp).astype(BF16)
+    d_hidden = product_back(d_exp, w2_ref[0])
     dgu_s[:, :FF] = (d_hidden * up_pre * sig * (1.0 + gate_pre * (1.0 - sig))).astype(BF16)
     dgu_s[:, FF:] = (d_hidden * act).astype(BF16)
     dgu = dgu_s[...]
-    d_rank_in = product_back(dgu, b1_s[...]).astype(BF16)
-    dx = (product_back(dgu, w1_ref[0]) + product(d_rank_in, a1_ref[0, 0])).astype(BF16)
+    d_rank_in = product_back(b1_s[...], dgu).astype(BF16)
+    dx = product_back(dgu, w1_ref[0]).astype(BF16)
     for b in range(blocks):
         o_s[b, pl.ds(at, cap), :] = out[b * cap : (b + 1) * cap]
         dx_s[b, pl.ds(at, cap), :] = dx[b * cap : (b + 1) * cap]
@@ -473,15 +483,15 @@
             jnp.where(hit, d_gate_col[b * cap : (b + 1) * cap], 0.0), axis=0, keepdims=True
         )
 
-    grad_a1 = product_outer(d_rank_in, x)
-    grad_b1 = product_outer(rank_in, dgu)
-    grad_a2 = product_outer(d_rank_down, hidden)
-    grad_b2 = product_outer(rank_down, d_exp)
-    grad_out[0, 0 : 2 * RANK, :] = grad_a1.astype(BF16)
-    grad_out[0, 2 * RANK : 3 * RANK, :] = grad_b2.astype(BF16)
-    grad_out[0, 3 * RANK :, :FF] = grad_b1[:RANK, :FF].astype(BF16)
-    grad_out[0, 3 * RANK :, FF : 2 * FF] = grad_b1[RANK:, FF:].astype(BF16)
-    grad_out[0, 3 * RANK :, 2 * FF :] = grad_a2.astype(BF16)
+    grad_a1 = product(d_rank_in, x)
+    grad_b1 = product(rank_in, dgu)
+    grad_a2 = product(d_rank_down, hidden)
+    grad_b2 = product(rank_down, d_exp)
+    last = jnp.concatenate([grad_b1[:RANK, :FF], grad_b1[RANK:, FF:], grad_a2], axis=1)
+    for n, piece in enumerate((grad_a1[:RANK], grad_a1[RANK:], grad_b2, last)):
+        for half in range(halves):
+            rows = slice((n * halves + half) * RANK, (n * halves + half + 1) * RANK)
+            grad_out[0, rows, :] = piece[:, half * UNIT : (half + 1) * UNIT].astype(BF16)
 
     @pl.when(slot == flush - 1)
     def _():
@@ -498,45 +508,53 @@
         d_far[...] = accd[rows_block:, :].astype(BF16)
 
 
-def run_experts(chosen, x, x_far, g, g_far, pos, gate, w1, w2, a1, b1, a2, b2, cap):
-    experts, blocks, rows_block = pos.shape
+def run_experts(chosen, x, x_far, g, g_far, pos, gate, w1, w2, a1, b1, a2, b2, held, cap, first, count):
+    _, blocks, rows_block = pos.shape
     width = x.shape[1]
     tokens = blocks * rows_block
     rows = blocks * cap
-    flush = FLUSH if experts % FLUSH == 0 else 1
+    flush = FLUSH if count % FLUSH == 0 else 1
+    record = 4 * RANK * width // UNIT
     lead = lambda e, c: (e, 0, 0)
+    shifted = lambda e, c: (e + first, 0, 0)
     near = pl.BlockSpec((rows_block, width), lambda e, c: (0, 0), pipeline_mode=pl.Buffered(1))
     away = pl.BlockSpec((tokens - rows_block, width), lambda e, c: (0, 0), pipeline_mode=pl.Buffered(1))
     near_shape = jax.ShapeDtypeStruct((rows_block, width), BF16)
     away_shape = jax.ShapeDtypeStruct((tokens - rows_block, width), BF16)
     return pl.pallas_call(
         functools.partial(
-            expert_kernel, blocks=blocks, rows_block=rows_block, cap=cap, flush=flush
+            expert_kernel,
+            blocks=blocks,
+            rows_block=rows_block,
+            cap=cap,
+            flush=flush,
+            carried=bool(held),
         ),
         grid_spec=pltpu.PrefetchScalarGridSpec(
             num_scalar_prefetch=1,
-            grid=(experts,),
+            grid=(count,),
             in_specs=[
                 near,
                 away,
                 near,
                 away,
-                pl.BlockSpec((1, blocks, rows_block), lead),
-                pl.BlockSpec((1, blocks, rows_block), lead),
+                pl.BlockSpec((1, blocks, rows_block), shifted),
+                pl.BlockSpec((1, blocks, rows_block), shifted),
                 pl.BlockSpec((1, width, 2 * FF), lead),
                 pl.BlockSpec((1, FF, width), lead),
-                pl.BlockSpec((1, 1, 2 * RANK, width), lambda e, c: (c[0], e, 0, 0)),
-                pl.BlockSpec((1, 1, 2, RANK, FF), lambda e, c: (c[0], e, 0, 0, 0)),
-                pl.BlockSpec((1, 1, RANK, FF), lambda e, c: (c[0], e, 0, 0)),
-                pl.BlockSpec((1, 1, RANK, width), lambda e, c: (c[0], e, 0, 0)),
-            ],
+                pl.BlockSpec((1, 1, 2 * RANK, width), lambda e, c: (c[0], e + first, 0, 0)),
+                pl.BlockSpec((1, 1, 2, RANK, FF), lambda e, c: (c[0], e + first, 0, 0, 0)),
+                pl.BlockSpec((1, 1, RANK, FF), lambda e, c: (c[0], e + first, 0, 0)),
+                pl.BlockSpec((1, 1, RANK, width), lambda e, c: (c[0], e + first, 0, 0)),
+            ]
+            + ([near, away, near, away] if held else []),
             out_specs=[
                 near,
                 away,
                 near,
                 away,
                 pl.BlockSpec((1, blocks, rows_block), lead),
-                pl.BlockSpec((1, 4 * RANK, width), lead),
+                pl.BlockSpec((1, record, UNIT), lead),
             ],
             scratch_shapes=[
                 pltpu.VMEM((blocks, flush * cap, rows_block), BF16),
@@ -556,40 +574,140 @@
             away_shape,
             near_shape,
             away_shape,
-            jax.ShapeDtypeStruct((experts, blocks, rows_block), F32),
-            jax.ShapeDtypeStruct((experts, 4 * RANK, width), BF16),
+            jax.ShapeDtypeStruct((count, blocks, rows_block), F32),
+            jax.ShapeDtypeStruct((count, record, UNIT), BF16),
         ],
         compiler_params=pltpu.CompilerParams(
-            vmem_limit_bytes=62 * 1024 * 1024, dimension_semantics=("arbitrary",)
+            vmem_limit_bytes=63 * 1024 * 1024, dimension_semantics=("arbitrary",)
         ),
         cost_estimate=pl.CostEstimate(
-            flops=200_000_000_000 * experts // 20,
-            bytes_accessed=5_000_000 * experts,
-            transcendentals=rows * FF * experts,
+            flops=8_000_000_000 * count,
+            bytes_accessed=5_000_000 * count,
+            transcendentals=rows * FF * count,
         ),
         name="experts",
-    )(chosen, x, x_far, g, g_far, pos, gate, w1, w2, a1, b1, a2, b2)
-
-
-def unpack_kernel(rows_ref, a1_ref, b1_ref, a2_ref, b2_ref, *, ranks, share):
-    records = ranks * share // (4 * RANK)
-    for e in range(records):
+    )(chosen, x, x_far, g, g_far, pos, gate, w1, w2, a1, b1, a2, b2, *held)
+
+
+def fold_kernel(chosen_ref, w1_ref, w2_ref, a1_ref, b1_ref, a2_ref, b2_ref, *refs):
+    o1_ref, o2_ref = refs[-2:]
+    for n in range(2):
+        at = slice(n * FF, (n + 1) * FF)
+        a1 = a1_ref[0, 0, n * RANK : (n + 1) * RANK, :]
+        o1_ref[0, :, at] = (w1_ref[0, :, at].astype(F32) + product_outer(a1, b1_ref[0, 0, n])).astype(BF16)
+    o2_ref[0] = (w2_ref[0].astype(F32) + product_outer(a2_ref[0, 0], b2_ref[0, 0])).astype(BF16)
+
+
+def fold_adapters(chosen, w1, w2, a1, b1, a2, b2, first, count, held=(), skip=0, size=None, after=()):
+    size = size or count
+    placed = lambda e, c: (e + skip, 0, 0)
+    _, width, _ = w1.shape
+    shifted = lambda e, c: (e + first, 0, 0)
+    return pl.pallas_call(
+        fold_kernel,
+        grid_spec=pltpu.PrefetchScalarGridSpec(
+            num_scalar_prefetch=1,
+            grid=(count,),
+            in_specs=[
+                pl.BlockSpec((1, width, 2 * FF), shifted),
+                pl.BlockSpec((1, FF, width), shifted),
+                pl.BlockSpec((1, 1, 2 * RANK, width), lambda e, c: (c[0], e + first, 0, 0)),
+                pl.BlockSpec((1, 1, 2, RANK, FF), lambda e, c: (c[0], e + first, 0, 0, 0)),
+                pl.BlockSpec((1, 1, RANK, FF), lambda e, c: (c[0], e + first, 0, 0)),
+                pl.BlockSpec((1, 1, RANK, width), lambda e, c: (c[0], e + first, 0, 0)),
+            ]
+            + [pl.BlockSpec(memory_space=pl.ANY)] * (len(held) + len(after)),
+            out_specs=[pl.BlockSpec((1, width, 2 * FF), placed), pl.BlockSpec((1, FF, width), placed)],
+        ),
+        out_shape=[
+            jax.ShapeDtypeStruct((size, width, 2 * FF), BF16),
+            jax.ShapeDtypeStruct((size, FF, width), BF16),
+        ],
+        input_output_aliases={7 + n: n for n in range(len(held))},
+        compiler_params=pltpu.CompilerParams(
+            vmem_limit_bytes=40 * 1024 * 1024, dimension_semantics=("arbitrary",)
+        ),
+        cost_estimate=pl.CostEstimate(
+            flops=3_000_000_000 * count, bytes_accessed=12_000_000 * count, transcendentals=0
+        ),
+        name="fold",
+    )(chosen, w1, w2, a1, b1, a2, b2, *held, *after)
+
+
+def total_kernel(ids_ref, rows_ref, *refs):
+    out_ref, held = refs[-2:]
+    held[...] = jnp.zeros_like(held)
+    for n in range(rows_ref.shape[0]):
+        held[ids_ref[n]] += rows_ref[n].astype(F32)
+    out_ref[...] = held[...].astype(BF16)
+
+
+def totals(ids, rows, adapters, after=()):
+    shape = (adapters,) + rows.shape[1:]
+    if rows.shape[1] % 16:
+        hot = (jnp.arange(adapters, dtype=jnp.int32)[:, None] == ids[None, :]).astype(F32)
+        return jnp.sum(hot[:, :, None, None] * rows.astype(F32)[None], axis=1).astype(BF16)
+    return pl.pallas_call(
+        total_kernel,
+        grid_spec=pltpu.PrefetchScalarGridSpec(
+            num_scalar_prefetch=1,
+            grid=(1,),
+            in_specs=[pl.BlockSpec(rows.shape, lambda i, c: (0, 0, 0))]
+            + [pl.BlockSpec(memory_space=pl.ANY)] * len(after),
+            out_specs=pl.BlockSpec(shape, lambda i, c: (0, 0, 0)),
+            scratch_shapes=[pltpu.VMEM(shape, F32)],
+        ),
+        out_shape=jax.ShapeDtypeStruct(shape, BF16),
+        compiler_params=pltpu.CompilerParams(vmem_limit_bytes=32 * 1024 * 1024),
+        cost_estimate=pl.CostEstimate(flops=0, bytes_accessed=5_000_000, transcendentals=0),
+        name="totals",
+    )(ids, rows, *after)
+
+
+def add_kernel(first_ref, second_ref, third_ref, *refs):
+    total = first_ref[...] + second_ref[...].astype(F32) + third_ref[...].astype(F32)
+    refs[-1][...] = total.astype(BF16)
+
+
+def add_up(first, second, third, after=()):
+    return pl.pallas_call(
+        add_kernel,
+        in_specs=[pl.BlockSpec(memory_space=pltpu.VMEM)] * 3
+        + [pl.BlockSpec(memory_space=pl.ANY)] * len(after),
+        out_specs=pl.BlockSpec(memory_space=pltpu.VMEM),
+        out_shape=jax.ShapeDtypeStruct(first.shape, BF16),
+        compiler_params=pltpu.CompilerParams(vmem_limit_bytes=32 * 1024 * 1024),
+        name="add_up",
+    )(first, second, third, *after)
+
+
+def unpack_kernel(rows_ref, *refs, share):
+    a1_ref, b1_ref, a2_ref, b2_ref = refs[-4:]
+    halves = a1_ref.shape[-1] // UNIT
+    record = 4 * RANK * halves
+    for e in range(rows_ref.shape[0] * share // record):
         unit = []
-        for n in range(4):
-            at = (4 * e + n) * RANK
+        for n in range(4 * halves):
+            at = e * record + n * RANK
             unit.append(rows_ref[at // share, 0, at % share : at % share + RANK, :].astype(F32))
-        a1_ref[0, e, 0:RANK, :] = unit[0]
-        a1_ref[0, e, RANK:, :] = unit[1]
-        b2_ref[0, e] = unit[2]
-        b1_ref[0, e, 0] = unit[3][:, :FF]
-        b1_ref[0, e, 1] = unit[3][:, FF : 2 * FF]
-        a2_ref[0, e] = unit[3][:, 2 * FF :]
-
-
-def unpack_grads(gathered, experts):
-    ranks, adapters, share, width = gathered.shape
-    if share % RANK:
-        flat = gathered.swapaxes(0, 1).reshape(adapters, experts, 4 * RANK, width).astype(F32)
+        for half in range(halves):
+            at = slice(half * UNIT, (half + 1) * UNIT)
+            a1_ref[0, e, 0:RANK, at] = unit[half]
+            a1_ref[0, e, RANK:, at] = unit[halves + half]
+            b2_ref[0, e, :, at] = unit[2 * halves + half]
+        last = jnp.concatenate(unit[3 * halves :], axis=1)
+        b1_ref[0, e, 0] = last[:, :FF]
+        b1_ref[0, e, 1] = last[:, FF : 2 * FF]
+        a2_ref[0, e] = last[:, 2 * FF :]
+
+
+def unpack_grads(gathered, experts, first, held, width):
+    ranks, adapters, share, _ = gathered.shape
+    halves = width // UNIT
+    record = 4 * RANK * halves
+    if share % 16:
+        flat = gathered.swapaxes(0, 1).reshape(adapters, experts, 4, halves, RANK, UNIT)
+        flat = flat.swapaxes(3, 4).reshape(adapters, experts, 4 * RANK, width).astype(F32)
         last = flat[:, :, 3 * RANK :]
         return (
             flat[:, :, : 2 * RANK],
@@ -598,18 +716,20 @@
             flat[:, :, 2 * RANK : 3 * RANK],
         )
     together = 1
-    while together * share % (4 * RANK):
+    while together * share % record:
         together += 1
-    held = together * share // (4 * RANK)
+    each = together * share // record
+    skip = first // each
     return pl.pallas_call(
-        functools.partial(unpack_kernel, ranks=together, share=share),
+        functools.partial(unpack_kernel, share=share),
         grid=(adapters, ranks // together),
-        in_specs=[pl.BlockSpec((together, 1, share, width), lambda a, i: (i, a, 0, 0))],
+        in_specs=[pl.BlockSpec((together, 1, share, UNIT), lambda a, i: (i, a, 0, 0))]
+        + [pl.BlockSpec(memory_space=pl.ANY)] * len(held),
         out_specs=[
-            pl.BlockSpec((1, held, 2 * RANK, width), lambda a, i: (a, i, 0, 0)),
-            pl.BlockSpec((1, held, 2, RANK, FF), lambda a, i: (a, i, 0, 0, 0)),
-            pl.BlockSpec((1, held, RANK, FF), lambda a, i: (a, i, 0, 0)),
-            pl.BlockSpec((1, held, RANK, width), lambda a, i: (a, i, 0, 0)),
+            pl.BlockSpec((1, each, 2 * RANK, width), lambda a, i: (a, i + skip, 0, 0)),
+            pl.BlockSpec((1, each, 2, RANK, FF), lambda a, i: (a, i + skip, 0, 0, 0)),
+            pl.BlockSpec((1, each, RANK, FF), lambda a, i: (a, i + skip, 0, 0)),
+            pl.BlockSpec((1, each, RANK, width), lambda a, i: (a, i + skip, 0, 0)),
         ],
         out_shape=[
             jax.ShapeDtypeStruct((adapters, experts, 2 * RANK, width), F32),
@@ -617,12 +737,13 @@
             jax.ShapeDtypeStruct((adapters, experts, RANK, FF), F32),
             jax.ShapeDtypeStruct((adapters, experts, RANK, width), F32),
         ],
+        input_output_aliases={1 + n: n for n in range(len(held))},
         compiler_params=pltpu.CompilerParams(
             vmem_limit_bytes=40 * 1024 * 1024, dimension_semantics=("arbitrary", "arbitrary")
         ),
-        cost_estimate=pl.CostEstimate(flops=0, bytes_accessed=50_000_000, transcendentals=0),
+        cost_estimate=pl.CostEstimate(flops=0, bytes_accessed=30_000_000, transcendentals=0),
         name="unpack",
-    )(gathered)
+    )(gathered, *held)
 
 
 def swap_pairs(size):
@@ -636,6 +757,12 @@
     rows = piece.shape[0]
     every = lax.all_gather(piece, "grp", axis=0, tiled=True)
     return jnp.roll(every, -lax.axis_index("grp") * rows, axis=0)[rows:]
+
+
+def owners_terms(near, far):
+    if lax.axis_size("grp") == 2:
+        return near, lax.ppermute(far, "grp", swap_pairs(2))
+    return to_owners(near, far), jnp.zeros_like(near)
 
 
 def to_owners(near, far):
@@ -788,7 +915,17 @@
     query_full = gather_rows_wide(w_query)
     output_full = gather_rows_wide(w_output)
     routes_far = from_others(routes)
-    ids_all = lax.all_gather(adapter_ids, "rep", axis=0, tiled=True)
+    labels_rep = (jnp.arange(128, dtype=jnp.int32) == chosen).astype(BF16)
+    ids_hot = lax.all_to_all(
+        jnp.broadcast_to(labels_rep, (reps, 128)), "rep", split_axis=0, concat_axis=0, tiled=True
+    )
+    ids_all = jnp.sum(ids_hot.astype(jnp.int32) * jnp.arange(128, dtype=jnp.int32), axis=1)
+    maps = (a_gateup.swapaxes(2, 3), b_gateup, a_down.swapaxes(2, 3), b_down)
+    calls = 2 if experts_dev % (2 * FLUSH) == 0 and groups == 2 else 1
+    each = experts_dev // calls
+    folded = [fold_adapters(adapter_ids, w_gateup, w_down, *maps, 0, each)]
+    tokens, ids_all = lax.optimization_barrier((tokens, ids_all))
+    upstream_far = from_others(cotangent)
 
     tokens_f = tokens.astype(F32)
     normed = rms_norm(tokens_f, attn_gain).astype(BF16)
@@ -801,9 +938,12 @@
         ],
         axis=1,
     ).astype(BF16)
+    if calls == 2:
+        some = each // 2
+        second = fold_adapters(
+            adapter_ids, w_gateup, w_down, *maps, each, some, size=each, after=(keyvals,)
+        )
     keyvals_far = from_others(keyvals)
-    cotangent_late, keyvals_far = lax.optimization_barrier((cotangent, keyvals_far))
-    upstream_far = from_others(cotangent_late)
     query_rows = (product(normed, query_full) + product(low_rank[:, :RANK], query_out)).astype(BF16)
     pad_whole = jnp.roll(pad_all, -first)
     listing, steps, own_bias, live = visits(parents[0], pad_whole[:count], pad_whole[count:], first)
@@ -811,6 +951,21 @@
     out_rank = product_back(attended, output_in).astype(BF16)
     middle = tokens_f + product(attended, output_full) + product(out_rank, output_out)
     normed_ffn = rms_norm(middle, ffn_gain).astype(BF16)
+    if calls == 2:
+        folded.append(
+            fold_adapters(
+                adapter_ids,
+                w_gateup,
+                w_down,
+                *maps,
+                each + some,
+                each - some,
+                second,
+                some,
+                each,
+                after=(normed_ffn,),
+            )
+        )
     router_rank = product_back(normed_ffn, router_in).astype(BF16)
     logits = product_back(normed_ffn, router_full) + product(router_rank, router_out)
 
@@ -837,32 +992,35 @@
         gates_mine = lax.all_gather(gates_t, "grp", axis=0)
         gates_mine = lax.dynamic_slice_in_dim(gates_mine, member * experts_dev, experts_dev, 1)
         gates_mine = jnp.roll(gates_mine, -member, axis=0).transpose(1, 0, 2)
-    result_near, result_far, d_near, d_far, part_gates, expert_grads = run_experts(
-        adapter_ids,
-        normed_ffn,
-        rows_far,
-        cotangent,
-        upstream_far,
-        places,
-        gates_mine,
-        w_gateup,
-        w_down,
-        a_gateup.swapaxes(2, 3),
-        b_gateup,
-        a_down.swapaxes(2, 3),
-        b_down,
-        cap,
-    )
-
+    sums = ()
+    gate_terms = []
+    spread = []
+    for n in range(calls):
+        *sums, terms, grads = run_experts(
+            adapter_ids,
+            normed_ffn,
+            rows_far,
+            cotangent,
+            upstream_far,
+            places,
+            gates_mine,
+            *folded[n],
+            *maps,
+            tuple(sums),
+            cap,
+            n * each,
+            each,
+        )
+        gate_terms.append(terms)
+        if n:
+            sums[3], swapped = lax.optimization_barrier((sums[3], swapped))
+            spread.append(lax.all_gather(totals(ids_all, swapped, adapters), "rep", axis=0))
+        swapped = lax.all_to_all(
+            grads.reshape(reps, -1, UNIT), "rep", split_axis=0, concat_axis=0, tiled=True
+        )
+    result_near, result_far, d_near, d_far = sums
+    part_gates = jnp.concatenate(gate_terms, axis=0)
     owner_hot = (jnp.arange(adapters, dtype=jnp.int32)[:, None] == ids_all[None, :]).astype(F32)
-    share = experts_dev * 4 * RANK // reps
-    swapped = lax.all_to_all(
-        expert_grads.reshape(reps, share, width), "rep", split_axis=0, concat_axis=0, tiled=True
-    )
-    summed = jnp.sum(owner_hot[:, :, None, None] * swapped.astype(F32)[None], axis=1).astype(BF16)
-    spread = lax.all_gather(summed, "rep", axis=0)
-    grad_a_gateup, grad_b_gateup, grad_a_down, grad_b_down = unpack_grads(spread, experts_dev)
-
     if groups == 2:
         d_gates = in_order(part_gates[:, 0], from_others(part_gates[:, 1]))
     else:
@@ -871,7 +1029,7 @@
     d_gates = d_gates.reshape(experts, count).T
     d_sum = to_owners(d_near, d_far)
     result_far, d_sum = lax.optimization_barrier((result_far, d_sum))
-    result = (middle + to_owners(result_near, result_far)).astype(BF16)
+    mixture = owners_terms(result_near, result_far)
     upstream = cotangent.astype(F32)
     d_logits = (gates * (d_gates - jnp.sum(gates * d_gates, axis=1, keepdims=True))).astype(BF16)
 
@@ -885,11 +1043,26 @@
     attended_gradient = (product_back(d_attn, output_full) + product(d_out_rank, output_in)).astype(BF16)
     grad_output_out = product_outer(out_rank, d_attn)
     grad_output_in = product_outer(d_out_rank, attended)
-    d_queries, d_keys, d_values, d_keys_far, d_values_far = run_attention_back(
-        listing, steps, query_rows, keyvals, keyvals_far, own_bias, live, attended, attended_gradient, logs
-    )
-    d_keys = to_owners(d_keys, d_keys_far).astype(BF16)
-    d_values = to_owners(d_values, d_values_far).astype(BF16)
+    parts = []
+    pairs = KEY_VALUE_HEADS // 4
+    for n in range(2):
+        d_q, *d_kv = run_attention_back(
+            listing,
+            steps,
+            query_rows,
+            keyvals,
+            keyvals_far,
+            own_bias,
+            live,
+            attended,
+            attended_gradient,
+            logs,
+            n * pairs,
+            pairs,
+        )
+        d_kv = to_owners(jnp.concatenate(d_kv[:2], axis=1), jnp.concatenate(d_kv[2:], axis=1)).astype(BF16)
+        parts.append((d_q, d_kv[:, : kv_width // 2], d_kv[:, kv_width // 2 :]))
+    d_queries, d_keys, d_values = [jnp.concatenate(pair, axis=1) for pair in zip(*parts)]
     d_keyvals = jnp.concatenate([d_keys, d_values], axis=1)
     d_rank_qkv = jnp.concatenate(
         [
@@ -915,6 +1088,13 @@
         axis=0,
     )
 
+    last = totals(ids_all, swapped, adapters, after=(parts[0][0],))
+    spread.append(lax.all_gather(last, "rep", axis=0))
+    expert_grads = ()
+    for n in range(calls):
+        expert_grads = unpack_grads(spread[n], experts_dev, n * each, tuple(expert_grads), width)
+    grad_a_gateup, grad_b_gateup, grad_a_down, grad_b_down = expert_grads
+
     def split(gradient):
         return jnp.moveaxis(
             gradient.astype(BF16).reshape(gradient.shape[:-1] + (groups, -1)), -2, 0
@@ -940,6 +1120,7 @@
     dense = lax.all_to_all(dense, ("rep", "grp"), split_axis=0, concat_axis=0, tiled=True)
     dense = jnp.sum(dense.reshape(reps, groups, -1).astype(F32), axis=1)
     dense = jnp.sum(owner_hot[:, :, None] * dense[None], axis=1).astype(BF16)
+    result = add_up(middle, *mixture, after=(dense,))
     dense = lax.all_gather(dense, "rep", axis=1).reshape(adapters, -1)
     owned = [piece.astype(F32) for piece in unpack(dense, shapes[:7])]
     return (

time: 738 us -> 637 us (0.86)
  waiting for transfers between devices: 157 us -> 44.3 us
  local copies, waits for them, and re-layouts: 38.1 us -> 66.1 us
  blocking collectives: 39.4 us -> 21.3 us
    pallas_call x1 -> x8, Pallas kernels: 18.7 us -> 93.1 us  [the longest x3 71.9 us: fold_adapters(): pl.pallas_call(fold_kernel, grid_spec=pltpu.PrefetchScalarGridSpec(num_sc...]
    pallas_call x1 -> x2, Pallas kernels: 226 us -> 153 us  [run_experts(): pl.pallas_call(functools.partial(expert_kernel, blocks=blocks, rows_block...]
    all_gather x1 -> x2, waiting for transfers between devices: 54.1 us -> 0.01 us  [the longest x1 0.01 us: local(): lax.all_gather(totals(ids_all, swapped, adapters), 'rep', axis=0)]
    ppermute x7, waiting for transfers between devices: 50.6 us -> 5.34 us  [from_others(): return lax.ppermute(piece, 'grp', swap_pairs(2))]
    all_to_all x1 -> x3, starting transfers between devices: 5.18 us -> 29 us  [the longest x2 23.1 us: local(): lax.all_to_all(grads.reshape(reps, -1, UNIT), 'rep', split_axis=0, concat...]
    unnamed x210 -> x206, local copies, waits for them, and re-layouts: 18.6 us -> 35.5 us
    ppermute x4 -> x3, starting transfers between devices: 34.8 us -> 18.3 us  [to_owners(): lax.ppermute(far, 'grp', swap_pairs(2)).astype(F32)]
    unnamed x1 -> x0, blocking collectives: 15.4 us -> none
  transfers between devices with their start and end apart: 20 -> 23, of which waited for: 9 -> 3; matrix products, arithmetic and copies ran while one was open for 16% -> 20% of each run, Pallas kernels for 7% -> 34%
where the time goes in v3:
time: 637 us; the launch traced here: 634 us
  Pallas kernels  300 us (47%)
  starting transfers between devices  91.9 us (14%)
  local copies, waits for them, and re-layouts  66.1 us (10%)
  matrix products  55.9 us (9%)
  waiting for transfers between devices  44.3 us (7%)
  other arithmetic  37.7 us (6%)
  blocking collectives  21.3 us (3%)
  between operations  16.3 us (3%)
    pallas_call x2, Pallas kernels, run_experts(): pl.pallas_call(functools.partial(expert_kernel, blocks=blocks, rows_block...  153 us
    pallas_call x3, Pallas kernels, fold_adapters(): pl.pallas_call(fold_kernel, grid_spec=pltpu.PrefetchScalarGridSpec(num_sc...  71.9 us
    unnamed x206, local copies, waits for them, and re-layouts  35.5 us
    pallas_call x2, Pallas kernels, run_attention_back(): pl.pallas_call(functools.partial(attend_back_kernel, here=here, segs=segs...  34.4 us
    ppermute x3, waiting for transfers between devices, to_owners(): lax.ppermute(far, 'grp', swap_pairs(2)).astype(F32)  27.3 us
    dot_general x12, matrix products, product(): return jnp.dot(left, right, preferred_element_type=F32)  26.4 us
    dot_general x13, matrix products, product_back(): lax.dot_general(left, right, (((1,), (1,)), ((), ())), preferred_element_...  24.9 us
    all_to_all x2, starting transfers between devices, local(): lax.all_to_all(grads.reshape(reps, -1, UNIT), 'rep', split_axis=0, concat...  23.1 us
  transfers between devices with their start and end apart: 23, of which 3 were waited for; matrix products, arithmetic and copies ran while one was open for 20% of the time, Pallas kernels for 34%

profile of v3, /device:TPU:0, one launch (start us, length us, event | category | flops | bytes accessed | tf_op | source)
XLA Modules:
  0.0 633.9 jit_solution(8771968906472016268)
XLA Ops:
  19.9 5.9 all-to-all-start
  42.5 34.1 %fold.5 = (bf16[10,1536,1024]{2,1,0:T(8,128)(2,1)}, bf16[10,512,1536]{2,1,0:T(8,128)(2,1)}) custom-call(s32[1]{0:T(128)} %copy.214.chosen_ref, bf16[20,1536,1024]{2,1,0:T(8,128)(2,1)} %w1_ref.5, bf16[20,512,1536]{2,1,0:T(8,128)(2,1)} %w2_ref.5, bf16[4,20,32,1536]{3,2,1,0:T(8,128)(2,1)} %bitcast.207, bf16[4,20,2,16,512]{4,3,2,1,0:T(8,128)(2,1)S(1)} %copy-done.9, ...), custom_call_target="tpu_custom_call" | custom-call | flops 30000001024 | bytes 120000000 | tf_op jit(solution)/shard_map/fold/pallas_call | solution.py:606
  98.5 18.9 %fold.3 = (bf16[10,1536,1024]{2,1,0:T(8,128)(2,1)}, bf16[10,512,1536]{2,1,0:T(8,128)(2,1)}) custom-call(s32[1]{0:T(128)} %copy.214.chosen_ref, bf16[20,1536,1024]{2,1,0:T(8,128)(2,1)} %w1_ref.5, bf16[20,512,1536]{2,1,0:T(8,128)(2,1)} %w2_ref.5, bf16[4,20,32,1536]{3,2,1,0:T(8,128)(2,1)} %bitcast.208, bf16[4,20,2,16,512]{4,3,2,1,0:T(8,128)(2,1)S(1)} %copy-done.9, ...), custom_call_target="tpu_custom_call" | custom-call | flops 15000000512 | bytes 60000000 | tf_op jit(solution)/shard_map/fold/pallas_call | solution.py:606
  117.4 7.1 %fusion.16.q_ref = bf16[512,1536]{1,0:T(8,128)(2,1)S(1)} fusion(f32[512,1536]{1,0:T(8,128)} %fusion.52, bf16[768,1536]{1,0:T(8,128)(2,1)} %all-gather.8.cloned.1.call-done, bf16[768,1536]{1,0:T(8,128)(2,1)} %param.33, pred[]{:T(512)S(6)} %eq.187, bf16[512,1536]{1,0:T(8,128)(2,1)} %param.27, f32[1536]{0:T(1024)S(1)} %reshape.394, f32[512]{0:T(512)S(1)} %add_rsqrt_fusion.1), kind=kOutput, calls=%fused_computation.34 | convolution fusion | flops 2441871360 | bytes 11018241 | tf_op jit(solution)/shard_map/dot_general | solution.py:26
  124.6 19.7 %attention.1 = (bf16[512,1536]{1,0:T(8,128)(2,1)S(1)}, f32[4,512,128]{2,1,0:T(8,128)S(1)}) custom-call(s32[64]{0:T(128)S(1)} %reshape.355.list_ref, s32[4]{0:T(128)S(1)} %and_select_fusion.steps_ref, bf16[512,1536]{1,0:T(8,128)(2,1)S(1)} %fusion.16.q_ref, bf16[512,1024]{1,0:T(8,128)(2,1)} %pad_maximum_fusion.k_ref.v_ref.refs_0_, ...), custom_call_target="tpu_custom_call" | custom-call | flops 40000000000 | bytes 8000000 | tf_op jit(solution)/shard_map/attention/pallas_call | solution.py:321
  148.3 7.4 %multiply_reduce_fusion.1 = (f32[512]{0:T(512)S(1)}, f32[512,1536]{1,0:T(8,128)S(1)}) fusion(f32[512,1536]{1,0:T(8,128)} %fusion.84, bf16[512,1536]{1,0:T(8,128)(2,1)} %copy-done.12, bf16[768,1536]{1,0:T(8,128)(2,1)} %all-gather.10.cloned.1.call-done, bf16[768,1536]{1,0:T(8,128)(2,1)} %param.35, pred[]{:T(512)S(6)} %eq.187, bf16[512,1536]{1,0:T(8,128)(2,1)} %param.27), kind=kOutput, calls=%fused_computation.33 | convolution fusion | flops 2441084416 | bytes 14157825 | tf_op jit(solution)/shard_map/dot_general | solution.py:26
  156.1 11.8 %collective-permute-start.6 = (bf16[512,1536]{1,0:T(8,128)(2,1)S(1)}, bf16[512,1536]{1,0:T(8,128)(2,1)S(1)}, u32[]{:S(2)}, u32[]{:S(2)}) collective-permute-start(bf16[512,1536]{1,0:T(8,128)(2,1)S(1)} %multiply_convert_fusion.refs_2_.x_ref), channel_id=1, source_target_pairs={{0,1},{1,0},{2,3},{3,2},{4,5},{5,4},{6,7},{7,6},{8,9},{9,8},{10,11... | collective-permute-start | bytes 4718600 | tf_op jit(solution)/shard_map/ppermute | solution.py:756
  170.0 18.9 %fold.4 = (bf16[10,1536,1024]{2,1,0:T(8,128)(2,1)}, bf16[10,512,1536]{2,1,0:T(8,128)(2,1)}) custom-call(s32[1]{0:T(128)} %copy.214.chosen_ref, bf16[20,1536,1024]{2,1,0:T(8,128)(2,1)} %w1_ref.5, bf16[20,512,1536]{2,1,0:T(8,128)(2,1)} %w2_ref.5, bf16[4,20,32,1536]{3,2,1,0:T(8,128)(2,1)} %bitcast.209, ...), custom_call_target="tpu_custom_call", output_to_operand_aliasing={{0}: (7, {}), {1}: (8, {})} | custom-call | flops 15000000512 | bytes 60000000 | tf_op jit(solution)/shard_map/fold/pallas_call | solution.py:606
  196.2 75.5 %experts.2 = (bf16[512,1536]{1,0:T(8,128)(2,1)}, bf16[512,1536]{1,0:T(8,128)(2,1)}, bf16[512,1536]{1,0:T(8,128)(2,1)}, bf16[512,1536]{1,0:T(8,128)(2,1)}, f32[10...) custom-call(s32[1]{0:T(128)} %copy.214.chosen_ref, bf16[512,1536]{1,0:T(8,128)(2,1)} %copy-done.4, ...), custom_call_target="tpu_custom_call" | custom-call | flops 80000000000 | bytes 50000000 | tf_op jit(solution)/shard_map/experts/pallas_call | solution.py:524
  271.7 17.1 %all-to-all-start.1 = ((bf16[16,80,768]{2,1,0:T(8,128)(2,1)}), bf16[16,80,768]{2,1,0:T(8,128)(2,1)}, u32[]{:S(2)}, u32[]{:S(2)}) async-start(bf16[16,80,768]{2,1,0:T(8,128)(2,1)} %bitcast.216), calls=%async_computation.1 | async-start | bytes 3932160 | tf_op jit(solution)/shard_map/all_to_all | solution.py:1018
  288.9 77.6 %experts.3 = (bf16[512,1536]{1,0:T(8,128)(2,1)}, bf16[512,1536]{1,0:T(8,128)(2,1)}, bf16[512,1536]{1,0:T(8,128)(2,1)}, bf16[512,1536]{1,0:T(8,128)(2,1)}, f32[10...) custom-call(s32[1]{0:T(128)} %copy.214.chosen_ref, bf16[512,1536]{1,0:T(8,128)(2,1)} %copy-done.4, ...), custom_call_target="tpu_custom_call" | custom-call | flops 80000000000 | bytes 50000000 | tf_op jit(solution)/shard_map/experts/pallas_call | solution.py:524
  373.5 6.0 all-to-all-start.3
  382.2 27.2 %collective-permute-done.10 = bf16[512,1536]{1,0:T(8,128)(2,1)S(1)} collective-permute-done((bf16[512,1536]{1,0:T(8,128)(2,1)}, bf16[512,1536]{1,0:T(8,128)(2,1)S(1)}, u32[]{:S(2)}, u32[]{:S(2)}) %collective-permute-start.10) | collective-permute-done | bytes 1572896 | tf_op jit(solution)/shard_map/ppermute | solution.py:771
  419.2 6.2 fusion.17.do_ref
  425.5 17.0 %attention_back.3 = (bf16[512,768]{1,0:T(8,128)(2,1)S(1)}, bf16[512,256]{1,0:T(8,128)(2,1)S(1)}, bf16[512,256]{1,0:T(8,128)(2,1)S(1)}, bf16[512,256]{1,0:T(8,128)(2,1)S(1)}, bf16[512,256]{1,0:T(8,128)(2,1)S(1)}) custom-call(s32[64]{0:T(128)S(1)} %reshape.355.list_ref, s32[4]{0:T(128)S(1)} %and_select_fusion.steps_ref, bf16[512,1536]{1,0:T(8,128)(2,1)S(1)} %copy-done.29, ...), custom_call_target="tpu_custom_call" | custom-call | flops 33999998976 | bytes 6000000 | tf_op jit(solution)/shard_map/attention_back/pallas_call | solution.py:355
  443.4 9.6 %collective-permute-start.14 = (bf16[512,512]{1,0:T(8,128)(2,1)}, bf16[512,512]{1,0:T(8,128)(2,1)}, u32[]{:S(2)}, u32[]{:S(2)}) collective-permute-start(bf16[512,512]{1,0:T(8,128)(2,1)} %pad_maximum_fusion.2), channel_id=1, source_target_pairs={{0,1},{1,0},{2,3},{3,2},{4,5},{5,4},{6,7},{7,6},{8,9},{9,8},{10,11... | collective-permute-start | bytes 1572872 | tf_op jit(solution)/shard_map/ppermute | solution.py:771
  453.1 17.4 %attention_back.2 = (bf16[512,768]{1,0:T(8,128)(2,1)S(1)}, bf16[512,256]{1,0:T(8,128)(2,1)S(1)}, bf16[512,256]{1,0:T(8,128)(2,1)S(1)}, bf16[512,256]{1,0:T(8,128)(2,1)S(1)}, bf16[512,256]{1,0:T(8,128)(2,1)S(1)}) custom-call(s32[64]{0:T(128)S(1)} %reshape.355.list_ref, s32[4]{0:T(128)S(1)} %and_select_fusion.steps_ref, bf16[512,1536]{1,0:T(8,128)(2,1)S(1)} %copy-done.29, ...), custom_call_target="tpu_custom_call" | custom-call | flops 33999998976 | bytes 6000000 | tf_op jit(solution)/shard_map/attention_back/pallas_call | solution.py:355
  471.4 8.6 %collective-permute-start.13 = (bf16[512,512]{1,0:T(8,128)(2,1)}, bf16[512,512]{1,0:T(8,128)(2,1)}, u32[]{:S(2)}, u32[]{:S(2)}) collective-permute-start(bf16[512,512]{1,0:T(8,128)(2,1)} %pad_maximum_fusion.1), channel_id=1, source_target_pairs={{0,1},{1,0},{2,3},{3,2},{4,5},{5,4},{6,7},{7,6},{8,9},{9,8},{10,11... | collective-permute-start | bytes 1572872 | tf_op jit(solution)/shard_map/ppermute | solution.py:771
  518.8 20.8 %all-to-all-start.2 = ((bf16[32,2,3008]{2,1,0:T(2,128)(2,1)}), bf16[32,2,3008]{2,1,0:T(2,128)(2,1)}, u32[]{:S(2)}, u32[]{:S(2)}) async-start(bf16[32,2,3008]{2,1,0:T(2,128)(2,1)} %reshape.411), calls=%async_computation.2 | async-start | bytes 786432 | tf_op jit(solution)/shard_map/all_to_all | solution.py:1120
  539.6 9.7 %fusion.10 = (f32[512]{0:T(512)S(1)}, f32[512,1536]{1,0:T(8,128)S(1)}) fusion(bf16[512,1536]{1,0:T(8,128)(2,1)} %param.27, f32[512]{0:T(512)} %copy-done.84, f32[1536]{0:T(1024)} %copy-done.82, f32[512,1536]{1,0:T(8,128)} %fusion.39, f32[512,1536]{1,0:T(8,128)} %fusion.21, bf16[512,1536]{1,0:T(8,128)(2,1)} %copy-done.34, ...), kind=kOutput, calls=%fused_computation.22 | convolution fusion | flops 2442657280 | bytes 17311744 | tf_op jit(solution)/shard_map/dot_general | solution.py:30
  551.3 11.6 %all-to-all-done.2 = bf16[32,2,3008]{2,1,0:T(2,128)(2,1)} async-done(((bf16[32,2,3008]{2,1,0:T(2,128)(2,1)}), bf16[32,2,3008]{2,1,0:T(2,128)(2,1)}, u32[]{:S(2)}, u32[]{:S(2)}) %all-to-all-start.2) | async-done | bytes 385056 | tf_op jit(solution)/shard_map/all_to_all | solution.py:1120
  577.2 21.3 %all-gather = bf16[4,96256]{1,0:T(4,128)(2,1)S(1)} all-gather(bf16[4,6016]{1,0:T(4,128)(2,1)S(1)} %multiply_reduce_fusion.2.refs_0_), channel_id=2, replica_groups=mesh['rep'=16,'grp'=2] {'rep'}, dimensions={1}, use_global_device_ids=true | all-gather | bytes 818176 | tf_op jit(solution)/shard_map/all_gather | solution.py:1124
  611.5 6.2 unpack.2
  620.9 6.2 unpack.3
  (422 shorter events, 157.9 us)
Async XLA Ops:
  16.3 63.6 %collective-permute-start = (bf16[1,128000]{1,0:T(2,128)(2,1)S(1)}, bf16[1,128000]{1,0:T(2,128)(2,1)}, u32[]{:S(2)}, u32[]{:S(2)}) collective-permute-start(bf16[1,128000]{1,0:T(2,128)(2,1)S(1)} %broadcast_in_dim.164), channel_id=1, source_target_pairs={{0,1},{1,0},{2,3},{3,2},{4,5},{5,4},{6,7},{7,6},{8,9},{9,8},{10,11... | collective-permute-start | bytes 768008 | tf_op jit(solution)/shard_map/ppermute | solution.py:756
  19.9 56.7 %all-to-all-start = ((bf16[16,1,128]{2,1,0:T(2,128)(2,1)}), bf16[16,1,128]{2,1,0:T(2,128)(2,1)S(1)}, u32[]{:S(2)}, u32[]{:S(2)}) async-start(bf16[16,1,128]{2,1,0:T(2,128)(2,1)} %broadcast_in_dim.109), calls=%async_computation | async-start | bytes 16384 | tf_op jit(solution)/shard_map/all_to_all | solution.py:919
  25.9 91.6 %all-gather.8.cloned.1.call-start = ((), (), s32[]{:S(2)}) async-start(), calls=%async_computation.4 | async-start | bytes 2506752 | tf_op jit(solution)/shard_map/all_gather | solution.py:802
  27.5 10.7 %collective-permute-start.1 = (bf16[48,1536]{1,0:T(8,128)(2,1)}, bf16[48,1536]{1,0:T(8,128)(2,1)S(1)}, u32[]{:S(2)}, u32[]{:S(2)}) collective-permute-start(bf16[48,1536]{1,0:T(8,128)(2,1)} %constant_dynamic-slice_fusion.2), channel_id=1, source_target_pairs={{0,1},{1,0},{2,3},{3,2},{4,5},{5,4},{6,7},{7,6},{8,9},{9,8},{10,11... | collective-permute-start | bytes 442376 | tf_op jit(solution)/shard_map/ppermute | solution.py:801
  30.1 56.6 %collective-permute-start.2 = (bf16[384,1024]{1,0:T(8,128)(2,1)}, bf16[384,1024]{1,0:T(8,128)(2,1)}, u32[]{:S(2)}, u32[]{:S(2)}) collective-permute-start(bf16[384,1024]{1,0:T(8,128)(2,1)} %constant_dynamic-slice_fusion.1), channel_id=1, source_target_pairs={{0,1},{1,0},{2,3},{3,2},{4,5},{5,4},{6,7},{7,6},{8,9},{9,8},{10,11... | collective-permute-start | bytes 2359304 | tf_op jit(solution)/shard_map/ppermute | solution.py:788
  33.2 46.7 %collective-permute-start.5 = (bf16[48,1536]{1,0:T(8,128)(2,1)}, bf16[48,1536]{1,0:T(8,128)(2,1)}, u32[]{:S(2)}, u32[]{:S(2)}) collective-permute-start(bf16[48,1536]{1,0:T(8,128)(2,1)} %constant_dynamic-slice_fusion), channel_id=1, source_target_pairs={{0,1},{1,0},{2,3},{3,2},{4,5},{5,4},{6,7},{7,6},{8,9},{9,8},{10,11... | collective-permute-start | bytes 442376 | tf_op jit(solution)/shard_map/ppermute | solution.py:801
  33.7 44.9 %collective-permute-start.8 = (s32[512,8]{0,1:T(8,128)S(1)}, s32[512,8]{0,1:T(8,128)S(1)}, u32[]{:S(2)}, u32[]{:S(2)}) collective-permute-start(s32[512,8]{0,1:T(8,128)S(1)} %copy-done.74), channel_id=1, source_target_pairs={{0,1},{1,0},{2,3},{3,2},{4,5},{5,4},{6,7},{7,6},{8,9},{9,8},{10,11... | collective-permute-start | bytes 49160 | tf_op jit(solution)/shard_map/ppermute | solution.py:756
  38.2 156.9 %collective-permute-start.7 = (bf16[512,1536]{1,0:T(8,128)(2,1)}, bf16[512,1536]{1,0:T(8,128)(2,1)}, u32[]{:S(2)}, u32[]{:S(2)}) collective-permute-start(bf16[512,1536]{1,0:T(8,128)(2,1)} %g_ref.3), channel_id=1, source_target_pairs={{0,1},{1,0},{2,3},{3,2},{4,5},{5,4},{6,7},{7,6},{8,9},{9,8},{10,11... | collective-permute-start | bytes 4718600 | tf_op jit(solution)/shard_map/ppermute | solution.py:756
  38.9 109.4 %all-gather.10.cloned.1.call-start = ((), (), s32[]{:S(2)}) async-start(), calls=%async_computation.5 | async-start | bytes 2506752 | tf_op jit(solution)/shard_map/all_gather | solution.py:802
  85.7 82.8 %copy-start.49 = (bf16[2,8,2,768]{3,1,2,0:T(8,128)(2,1)}, bf16[2,8,2,768]{3,1,2,0:T(8,128)(2,1)S(1)}, u32[]{:S(2)}) copy-start(bf16[2,8,2,768]{3,1,2,0:T(8,128)(2,1)S(1)} %copy.167) | copy-start | bytes 147460
  86.7 4.6 collective-permute-start.3
  97.1 27.5 %collective-permute-start.4 = (bf16[512,1024]{1,0:T(8,128)(2,1)}, bf16[512,1024]{1,0:T(8,128)(2,1)}, u32[]{:S(2)}, u32[]{:S(2)}) collective-permute-start(bf16[512,1024]{1,0:T(8,128)(2,1)} %pad_maximum_fusion.k_ref.v_ref.refs_0_), channel_id=1, source_target_pairs={{0,1},{1,0},{2,3},{3,2},{4,5},{5,4},{6,7},{7,6},{8,9},{9,8},{10,11... | collective-permute-start | bytes 3145736 | tf_op jit(solution)/shard_map/ppermute | solution.py:756
  156.1 39.0 %collective-permute-start.6 = (bf16[512,1536]{1,0:T(8,128)(2,1)S(1)}, bf16[512,1536]{1,0:T(8,128)(2,1)S(1)}, u32[]{:S(2)}, u32[]{:S(2)}) collective-permute-start(bf16[512,1536]{1,0:T(8,128)(2,1)S(1)} %multiply_convert_fusion.refs_2_.x_ref), channel_id=1, source_target_pairs={{0,1},{1,0},{2,3},{3,2},{4,5},{5,4},{6,7},{7,6},{8,9},{9,8},{10,11... | collective-permute-start | bytes 4718600 | tf_op jit(solution)/shard_map/ppermute | solution.py:756
  169.4 24.9 %collective-permute-start.9 = (f32[20,512]{1,0:T(8,128)S(1)}, f32[20,512]{1,0:T(8,128)S(1)}, u32[]{:S(2)}, u32[]{:S(2)}) collective-permute-start(f32[20,512]{1,0:T(8,128)S(1)} %get-tuple-element.181), channel_id=1, source_target_pairs={{0,1},{1,0},{2,3},{3,2},{4,5},{5,4},{6,7},{7,6},{8,9},{9,8},{10,11... | collective-permute-start | bytes 122888 | tf_op jit(solution)/shard_map/ppermute | solution.py:756
  271.7 94.8 %all-to-all-start.1 = ((bf16[16,80,768]{2,1,0:T(8,128)(2,1)}), bf16[16,80,768]{2,1,0:T(8,128)(2,1)}, u32[]{:S(2)}, u32[]{:S(2)}) async-start(bf16[16,80,768]{2,1,0:T(8,128)(2,1)} %bitcast.216), calls=%async_computation.1 | async-start | bytes 3932160 | tf_op jit(solution)/shard_map/all_to_all | solution.py:1018
  288.8 319.5 %all-gather.14.cloned.1.call-start = ((), (), s32[]{:S(2)}) async-start(), calls=%async_computation.7 | async-start | bytes 8355840 | tf_op jit(solution)/shard_map/all_gather | solution.py:1017
  370.8 8.7 %collective-permute-start.12 = (f32[20,512]{1,0:T(8,128)S(1)}, f32[20,512]{1,0:T(8,128)S(1)}, u32[]{:S(2)}, u32[]{:S(2)}) collective-permute-start(f32[20,512]{1,0:T(8,128)S(1)} %get-tuple-element.178), channel_id=1, source_target_pairs={{0,1},{1,0},{2,3},{3,2},{4,5},{5,4},{6,7},{7,6},{8,9},{9,8},{10,11... | collective-permute-start | bytes 122888 | tf_op jit(solution)/shard_map/ppermute | solution.py:756
  372.9 36.6 %collective-permute-start.10 = (bf16[512,1536]{1,0:T(8,128)(2,1)}, bf16[512,1536]{1,0:T(8,128)(2,1)S(1)}, u32[]{:S(2)}, u32[]{:S(2)}) collective-permute-start(bf16[512,1536]{1,0:T(8,128)(2,1)} %get-tuple-element.105), channel_id=1, source_target_pairs={{0,1},{1,0},{2,3},{3,2},{4,5},{5,4},{6,7},{7,6},{8,9},{9,8},{10,11... | collective-permute-start | bytes 4718600 | tf_op jit(solution)/shard_map/ppermute | solution.py:771
  373.5 110.9 %all-to-all-start.3 = ((bf16[16,80,768]{2,1,0:T(8,128)(2,1)}), bf16[16,80,768]{2,1,0:T(8,128)(2,1)}, u32[]{:S(2)}, u32[]{:S(2)}) async-start(bf16[16,80,768]{2,1,0:T(8,128)(2,1)} %bitcast.215), calls=%async_computation.3 | async-start | bytes 3932160 | tf_op jit(solution)/shard_map/all_to_all | solution.py:1018
  379.5 238.2 %all-gather.12.cloned.1.call-start = ((), (), s32[]{:S(2)}) async-start(), calls=%async_computation.6 | async-start | bytes 8355840 | tf_op jit(solution)/shard_map/all_gather | solution.py:1092
  443.4 45.5 %collective-permute-start.14 = (bf16[512,512]{1,0:T(8,128)(2,1)}, bf16[512,512]{1,0:T(8,128)(2,1)}, u32[]{:S(2)}, u32[]{:S(2)}) collective-permute-start(bf16[512,512]{1,0:T(8,128)(2,1)} %pad_maximum_fusion.2), channel_id=1, source_target_pairs={{0,1},{1,0},{2,3},{3,2},{4,5},{5,4},{6,7},{7,6},{8,9},{9,8},{10,11... | collective-permute-start | bytes 1572872 | tf_op jit(solution)/shard_map/ppermute | solution.py:771
  471.4 18.9 %collective-permute-start.13 = (bf16[512,512]{1,0:T(8,128)(2,1)}, bf16[512,512]{1,0:T(8,128)(2,1)}, u32[]{:S(2)}, u32[]{:S(2)}) collective-permute-start(bf16[512,512]{1,0:T(8,128)(2,1)} %pad_maximum_fusion.1), channel_id=1, source_target_pairs={{0,1},{1,0},{2,3},{3,2},{4,5},{5,4},{6,7},{7,6},{8,9},{9,8},{10,11... | collective-permute-start | bytes 1572872 | tf_op jit(solution)/shard_map/ppermute | solution.py:771
  482.9 121.0 %collective-permute-start.11 = (bf16[512,1536]{1,0:T(8,128)(2,1)}, bf16[512,1536]{1,0:T(8,128)(2,1)}, u32[]{:S(2)}, u32[]{:S(2)}) collective-permute-start(bf16[512,1536]{1,0:T(8,128)(2,1)} %get-tuple-element.106), channel_id=1, source_target_pairs={{0,1},{1,0},{2,3},{3,2},{4,5},{5,4},{6,7},{7,6},{8,9},{9,8},{10,11... | collective-permute-start | bytes 4718600 | tf_op jit(solution)/shard_map/ppermute | solution.py:764
  518.8 44.1 %all-to-all-start.2 = ((bf16[32,2,3008]{2,1,0:T(2,128)(2,1)}), bf16[32,2,3008]{2,1,0:T(2,128)(2,1)}, u32[]{:S(2)}, u32[]{:S(2)}) async-start(bf16[32,2,3008]{2,1,0:T(2,128)(2,1)} %reshape.411), calls=%async_computation.2 | async-start | bytes 786432 | tf_op jit(solution)/shard_map/all_to_all | solution.py:1120
  (89 other events, 1220.2 us)
Sparse Core Ops, SparseCore 0:
  39.0 43.5 all-gather.7
  84.9 41.1 all-gather.9
  370.0 105.0 all-gather.13
  489.0 90.9 all-gather.11

commit v4 on v3

--- a/solution.py
+++ b/solution.py
@@ -792,14 +792,34 @@
     return in_order(half, far)
 
 
-def gather_rows_wide(half):
+def gather_rows_wide(half, note=None):
     reps = lax.axis_size("rep")
     if lax.axis_size("grp") != 2 or half.shape[0] % (reps * 16):
-        return lax.all_gather(half, "grp", axis=0, tiled=True)
+        whole = lax.all_gather(half, "grp", axis=0, tiled=True)
+        return (whole, lax.all_gather(note, "rep", axis=0)) if note is not None else whole
     rows = half.shape[0] // reps
     mine = lax.dynamic_slice_in_dim(half, lax.axis_index("rep") * rows, rows, 0)
     got = lax.ppermute(mine, "grp", swap_pairs(2))
-    return in_order(half, lax.all_gather(got, "rep", axis=0, tiled=True))
+    if note is None:
+        return in_order(half, lax.all_gather(got, "rep", axis=0, tiled=True))
+    got = jnp.concatenate([got, jnp.broadcast_to(note[None], (8, note.shape[0]))], axis=0)
+    every = lax.all_gather(got, "rep", axis=0)
+    return in_order(half, every[:, :rows].reshape(half.shape)), every[:, rows]
+
+
+def delayed_kernel(rows_ref, *refs):
+    refs[-1][...] = rows_ref[...]
+
+
+def delayed(rows, after):
+    return pl.pallas_call(
+        delayed_kernel,
+        in_specs=[pl.BlockSpec(memory_space=pltpu.VMEM)] + [pl.BlockSpec(memory_space=pl.ANY)] * len(after),
+        out_specs=pl.BlockSpec(memory_space=pltpu.VMEM),
+        out_shape=jax.ShapeDtypeStruct(rows.shape, rows.dtype),
+        compiler_params=pltpu.CompilerParams(vmem_limit_bytes=16 * 1024 * 1024),
+        name="delayed",
+    )(rows, *after)
 
 
 def pack(pieces, multiple):
@@ -913,19 +933,25 @@
     ffn_gain = ffn_gain.astype(F32)
     keyval_full = gather_rows(w_keyval)
     query_full = gather_rows_wide(w_query)
-    output_full = gather_rows_wide(w_output)
+    note = (jnp.arange(width, dtype=jnp.int32) == chosen).astype(BF16)
+    output_full, notes = gather_rows_wide(w_output, note)
+    ids_all = jnp.sum(
+        notes[:, :adapters].astype(jnp.int32) * jnp.arange(adapters, dtype=jnp.int32), axis=1
+    )
     routes_far = from_others(routes)
-    labels_rep = (jnp.arange(128, dtype=jnp.int32) == chosen).astype(BF16)
-    ids_hot = lax.all_to_all(
-        jnp.broadcast_to(labels_rep, (reps, 128)), "rep", split_axis=0, concat_axis=0, tiled=True
-    )
-    ids_all = jnp.sum(ids_hot.astype(jnp.int32) * jnp.arange(128, dtype=jnp.int32), axis=1)
     maps = (a_gateup.swapaxes(2, 3), b_gateup, a_down.swapaxes(2, 3), b_down)
-    calls = 2 if experts_dev % (2 * FLUSH) == 0 and groups == 2 else 1
+    calls = 2 if experts_dev % (4 * FLUSH) == 0 and groups == 2 else 1
     each = experts_dev // calls
-    folded = [fold_adapters(adapter_ids, w_gateup, w_down, *maps, 0, each)]
-    tokens, ids_all = lax.optimization_barrier((tokens, ids_all))
-    upstream_far = from_others(cotangent)
+    some = -(-each // 2)
+
+    def fold(call, late, held, after):
+        at = some if late else 0
+        count = each - some if late else some
+        return fold_adapters(
+            adapter_ids, w_gateup, w_down, *maps, call * each + at, count, held, at, each, after
+        )
+
+    first_fold = fold(0, False, (), ())
 
     tokens_f = tokens.astype(F32)
     normed = rms_norm(tokens_f, attn_gain).astype(BF16)
@@ -938,12 +964,9 @@
         ],
         axis=1,
     ).astype(BF16)
-    if calls == 2:
-        some = each // 2
-        second = fold_adapters(
-            adapter_ids, w_gateup, w_down, *maps, each, some, size=each, after=(keyvals,)
-        )
+    folded = [fold(0, True, first_fold, (keyvals,))]
     keyvals_far = from_others(keyvals)
+    upstream_far = from_others(delayed(cotangent, (keyvals_far,)))
     query_rows = (product(normed, query_full) + product(low_rank[:, :RANK], query_out)).astype(BF16)
     pad_whole = jnp.roll(pad_all, -first)
     listing, steps, own_bias, live = visits(parents[0], pad_whole[:count], pad_whole[count:], first)
@@ -952,20 +975,7 @@
     middle = tokens_f + product(attended, output_full) + product(out_rank, output_out)
     normed_ffn = rms_norm(middle, ffn_gain).astype(BF16)
     if calls == 2:
-        folded.append(
-            fold_adapters(
-                adapter_ids,
-                w_gateup,
-                w_down,
-                *maps,
-                each + some,
-                each - some,
-                second,
-                some,
-                each,
-                after=(normed_ffn,),
-            )
-        )
+        folded.append(fold(1, True, fold(1, False, (), (normed_ffn,)), ()))
     router_rank = product_back(normed_ffn, router_in).astype(BF16)
     logits = product_back(normed_ffn, router_full) + product(router_rank, router_out)
 
@@ -1020,7 +1030,6 @@
         )
     result_near, result_far, d_near, d_far = sums
     part_gates = jnp.concatenate(gate_terms, axis=0)
-    owner_hot = (jnp.arange(adapters, dtype=jnp.int32)[:, None] == ids_all[None, :]).astype(F32)
     if groups == 2:
         d_gates = in_order(part_gates[:, 0], from_others(part_gates[:, 1]))
     else:
@@ -1088,41 +1097,43 @@
         axis=0,
     )
 
-    last = totals(ids_all, swapped, adapters, after=(parts[0][0],))
+    last = totals(ids_all, swapped, adapters, after=(attended_gradient,))
     spread.append(lax.all_gather(last, "rep", axis=0))
     expert_grads = ()
     for n in range(calls):
         expert_grads = unpack_grads(spread[n], experts_dev, n * each, tuple(expert_grads), width)
     grad_a_gateup, grad_b_gateup, grad_a_down, grad_b_down = expert_grads
 
-    def split(gradient):
-        return jnp.moveaxis(
-            gradient.astype(BF16).reshape(gradient.shape[:-1] + (groups, -1)), -2, 0
-        ).reshape(groups, -1)
-
-    dense = jnp.concatenate(
-        [
-            split(piece)
-            for piece in (
-                grad_qkv_in,
-                grad_query_out,
-                grad_keyval_out,
-                grad_output_in,
-                grad_output_out,
-                grad_router_in,
-                grad_router_out,
-            )
-        ],
-        axis=1,
-    )
-    dense = jnp.pad(dense, ((0, 0), (0, -dense.shape[1] % (reps * 128))))
-    dense = dense.reshape(groups, reps, -1).swapaxes(0, 1).reshape(reps * groups, -1)
+    tall = jnp.concatenate(
+        [grad_qkv_in, grad_query_out, grad_output_in, grad_output_out, grad_router_in], axis=0
+    ).astype(BF16)
+    high = tall.shape[0]
+    kv_part = kv_width // groups
+    tall = tall.reshape(high, groups, part).swapaxes(0, 1)
+    wide = [
+        grad_keyval_out[0].reshape(RANK, groups, kv_part),
+        grad_keyval_out[1].reshape(RANK, groups, kv_part),
+        grad_router_out.reshape(RANK, groups, experts_dev),
+        jnp.zeros((RANK, groups, part - 2 * kv_part - experts_dev), F32),
+    ]
+    wide = jnp.concatenate(wide, axis=2).astype(BF16).swapaxes(0, 1)
+    dense = jnp.concatenate([tall, wide], axis=1).reshape(groups, reps, -1, part).swapaxes(0, 1)
+    dense = dense.reshape(reps * groups, -1, part)
+    result = add_up(middle, *mixture, after=(dense,))
     dense = lax.all_to_all(dense, ("rep", "grp"), split_axis=0, concat_axis=0, tiled=True)
-    dense = jnp.sum(dense.reshape(reps, groups, -1).astype(F32), axis=1)
-    dense = jnp.sum(owner_hot[:, :, None] * dense[None], axis=1).astype(BF16)
-    result = add_up(middle, *mixture, after=(dense,))
-    dense = lax.all_gather(dense, "rep", axis=1).reshape(adapters, -1)
-    owned = [piece.astype(F32) for piece in unpack(dense, shapes[:7])]
+    owner_hot = (jnp.arange(adapters, dtype=jnp.int32)[:, None] == jnp.repeat(ids_all, groups)[None, :])
+    dense = jnp.sum(jnp.where(owner_hot[:, :, None, None], dense.astype(F32)[None], 0.0), axis=1).astype(BF16)
+    dense = lax.all_gather(dense, "rep", axis=0).swapaxes(0, 1).reshape(adapters, -1, part).astype(F32)
+    wide = dense[:, high:]
+    owned = [
+        dense[:, : 3 * RANK],
+        dense[:, 3 * RANK : 4 * RANK],
+        jnp.stack([wide[:, :, :kv_part], wide[:, :, kv_part : 2 * kv_part]], axis=1),
+        dense[:, 4 * RANK : 5 * RANK],
+        dense[:, 5 * RANK : 6 * RANK],
+        dense[:, 6 * RANK : 7 * RANK],
+        wide[:, :, 2 * kv_part : 2 * kv_part + experts_dev],
+    ]
     return (
         result,
         grad_input,

time: 637 us -> 649 us (1.019)
  starting transfers between devices: 91.9 us -> 109 us
  waiting for transfers between devices: 44.3 us -> 59.8 us
  other arithmetic: 37.7 us -> 23.6 us
  blocking collectives: 21.3 us -> 34.6 us
  matrix products: 55.9 us -> 44.8 us
  local copies, waits for them, and re-layouts: 66.1 us -> 55.9 us
    all_to_all x1, starting transfers between devices: 20.8 us -> 45.7 us  [local(): lax.all_to_all(dense, ('rep', 'grp'), split_axis=0, concat_axis=0, tiled=...]
    ppermute x2, waiting for transfers between devices: 0.01 us -> 15.1 us  [gather_rows_wide(): got = lax.ppermute(mine, 'grp', swap_pairs(2))]
    all_gather x1, blocking collectives: 21.3 us -> 34.6 us  [local(): lax.all_gather(dense, 'rep', axis=0).swapaxes(0, 1)]
    all_to_all x1, waiting for transfers between devices: 11.6 us -> 0.01 us  [local(): lax.all_to_all(dense, ('rep', 'grp'), split_axis=0, concat_axis=0, tiled=...]
    all_to_all x2, waiting for transfers between devices: 0.01 us -> 9.7 us  [local(): lax.all_to_all(grads.reshape(reps, -1, UNIT), 'rep', split_axis=0, concat...]
    all_to_all x2, starting transfers between devices: 23.1 us -> 16.2 us  [local(): lax.all_to_all(grads.reshape(reps, -1, UNIT), 'rep', split_axis=0, concat...]
    dot_general x13, matrix products: 24.9 us -> 18.1 us  [product_back(): lax.dot_general(left, right, (((1,), (1,)), ((), ())), preferred_element_...]
    pallas_call x3 -> x4, Pallas kernels: 71.9 us -> 76.5 us  [fold_adapters(): pl.pallas_call(fold_kernel, grid_spec=pltpu.PrefetchScalarGridSpec(num_sc...]
  transfers between devices with their start and end apart: 23 -> 22, of which waited for: 3 -> 5; matrix products, arithmetic and copies ran while one was open for 20% -> 14% of each run, Pallas kernels for 34% -> 33%
where the time goes in v4:
time: 649 us; the launch traced here: 642 us
  Pallas kernels  297 us (46%)
  starting transfers between devices  109 us (17%)
  waiting for transfers between devices  59.8 us (9%)
  local copies, waits for them, and re-layouts  55.9 us (9%)
  matrix products  44.8 us (7%)
  blocking collectives  34.6 us (5%)
  other arithmetic  23.6 us (4%)
  between operations  16.5 us (3%)
    pallas_call x2, Pallas kernels, run_experts(): pl.pallas_call(functools.partial(expert_kernel, blocks=blocks, rows_block...  153 us
    pallas_call x4, Pallas kernels, fold_adapters(): pl.pallas_call(fold_kernel, grid_spec=pltpu.PrefetchScalarGridSpec(num_sc...  76.5 us
    all_to_all x1, starting transfers between devices, local(): lax.all_to_all(dense, ('rep', 'grp'), split_axis=0, concat_axis=0, tiled=...  45.7 us
    all_gather x1, blocking collectives, local(): lax.all_gather(dense, 'rep', axis=0).swapaxes(0, 1)  34.6 us
    unnamed x222, local copies, waits for them, and re-layouts  34.4 us
    ppermute x3, waiting for transfers between devices, to_owners(): lax.ppermute(far, 'grp', swap_pairs(2)).astype(F32)  30.5 us
    pallas_call x2, Pallas kernels, run_attention_back(): pl.pallas_call(functools.partial(attend_back_kernel, here=here, segs=segs...  29 us
    dot_general x12, matrix products, product(): return jnp.dot(left, right, preferred_element_type=F32)  24 us
  transfers between devices with their start and end apart: 22, of which 5 were waited for; matrix products, arithmetic and copies ran while one was open for 14% of the time, Pallas kernels for 33%

profile of v4, /device:TPU:0, one launch (start us, length us, event | category | flops | bytes accessed | tf_op | source)
XLA Modules:
  0.0 641.8 jit_solution(4309742566231995135)
XLA Ops:
  30.1 15.1 %collective-permute-done.1 = bf16[48,1536]{1,0:T(8,128)(2,1)S(1)} collective-permute-done((bf16[48,1536]{1,0:T(8,128)(2,1)S(1)}, bf16[48,1536]{1,0:T(8,128)(2,1)S(1)}, u32[]{:S(2)}, u32[]{:S(2)}) %collective-permute-start.1) | collective-permute-done | bytes 147488 | tf_op jit(solution)/shard_map/ppermute | solution.py:802
  51.7 19.5 %fold.6 = (bf16[10,1536,1024]{2,1,0:T(8,128)(2,1)}, bf16[10,512,1536]{2,1,0:T(8,128)(2,1)}) custom-call(s32[1]{0:T(128)} %copy.247.chosen_ref, bf16[20,1536,1024]{2,1,0:T(8,128)(2,1)} %w1_ref.7, bf16[20,512,1536]{2,1,0:T(8,128)(2,1)} %w2_ref.7, bf16[4,20,32,1536]{3,2,1,0:T(8,128)(2,1)} %bitcast.204, bf16[4,20,2,16,512]{4,3,2,1,0:T(8,128)(2,1)S(1)} %copy-done.7, ...), custom_call_target="tpu_custom_call" | custom-call | flops 15000000512 | bytes 60000000 | tf_op jit(solution)/shard_map/fold/pallas_call | solution.py:606
  89.5 19.2 %fold.7 = (bf16[10,1536,1024]{2,1,0:T(8,128)(2,1)}, bf16[10,512,1536]{2,1,0:T(8,128)(2,1)}) custom-call(s32[1]{0:T(128)} %copy.247.chosen_ref, bf16[20,1536,1024]{2,1,0:T(8,128)(2,1)} %w1_ref.7, bf16[20,512,1536]{2,1,0:T(8,128)(2,1)} %w2_ref.7, bf16[4,20,32,1536]{3,2,1,0:T(8,128)(2,1)} %bitcast.205, ...), custom_call_target="tpu_custom_call", output_to_operand_aliasing={{0}: (7, {}), {1}: (8, {})} | custom-call | flops 15000000512 | bytes 60000000 | tf_op jit(solution)/shard_map/fold/pallas_call | solution.py:606
  116.5 7.1 %fusion.16.q_ref = bf16[512,1536]{1,0:T(8,128)(2,1)S(1)} fusion(f32[512,1536]{1,0:T(8,128)} %fusion.53, bf16[768,1536]{1,0:T(8,128)(2,1)} %all-gather.9.cloned.1.call-done, bf16[768,1536]{1,0:T(8,128)(2,1)} %param.33, pred[]{:T(512)S(6)} %eq.191, bf16[512,1536]{1,0:T(8,128)(2,1)} %param.27, f32[1536]{0:T(1024)S(1)} %reshape.329, f32[512]{0:T(512)S(1)} %add_rsqrt_fusion.1), kind=kOutput, calls=%fused_computation.35 | convolution fusion | flops 2441871360 | bytes 11018241 | tf_op jit(solution)/shard_map/dot_general | solution.py:26
  123.7 16.1 %attention.1 = (bf16[512,1536]{1,0:T(8,128)(2,1)S(1)}, f32[4,512,128]{2,1,0:T(8,128)S(1)}) custom-call(s32[64]{0:T(128)S(1)} %reshape.302.list_ref, s32[4]{0:T(128)S(1)} %and_select_fusion.steps_ref, bf16[512,1536]{1,0:T(8,128)(2,1)S(1)} %fusion.16.q_ref, bf16[512,1024]{1,0:T(8,128)(2,1)S(1)} %copy-done.24, bf16[512,1024]{1,0:T(8,128)(2,1)S(1)} %copy-done.24, ...), custom_call_target="tpu_custom_call" | custom-call | flops 40000000000 | bytes 8000000 | tf_op jit(solution)/shard_map/attention/pallas_call | solution.py:321
  147.1 5.6 multiply_reduce_fusion.1
  154.7 11.3 %collective-permute-start.6 = (bf16[512,1536]{1,0:T(8,128)(2,1)S(1)}, bf16[512,1536]{1,0:T(8,128)(2,1)S(1)}, u32[]{:S(2)}, u32[]{:S(2)}) collective-permute-start(bf16[512,1536]{1,0:T(8,128)(2,1)S(1)} %multiply_convert_fusion.refs_0_.x_ref), channel_id=1, source_target_pairs={{0,1},{1,0},{2,3},{3,2},{4,5},{5,4},{6,7},{7,6},{8,9},{9,8},{10,11... | collective-permute-start | bytes 4718600 | tf_op jit(solution)/shard_map/ppermute | solution.py:756
  166.0 18.9 %fold.4 = (bf16[10,1536,1024]{2,1,0:T(8,128)(2,1)}, bf16[10,512,1536]{2,1,0:T(8,128)(2,1)}) custom-call(s32[1]{0:T(128)} %copy.247.chosen_ref, bf16[20,1536,1024]{2,1,0:T(8,128)(2,1)} %w1_ref.7, bf16[20,512,1536]{2,1,0:T(8,128)(2,1)} %w2_ref.7, bf16[4,20,32,1536]{3,2,1,0:T(8,128)(2,1)} %bitcast.206, bf16[4,20,2,16,512]{4,3,2,1,0:T(8,128)(2,1)S(1)} %copy-done.8, ...), custom_call_target="tpu_custom_call" | custom-call | flops 15000000512 | bytes 60000000 | tf_op jit(solution)/shard_map/fold/pallas_call | solution.py:606
  189.3 18.9 %fold.5 = (bf16[10,1536,1024]{2,1,0:T(8,128)(2,1)}, bf16[10,512,1536]{2,1,0:T(8,128)(2,1)}) custom-call(s32[1]{0:T(128)} %copy.247.chosen_ref, bf16[20,1536,1024]{2,1,0:T(8,128)(2,1)} %w1_ref.7, bf16[20,512,1536]{2,1,0:T(8,128)(2,1)} %w2_ref.7, bf16[4,20,32,1536]{3,2,1,0:T(8,128)(2,1)} %bitcast.207, ...), custom_call_target="tpu_custom_call", output_to_operand_aliasing={{0}: (7, {}), {1}: (8, {})} | custom-call | flops 15000000512 | bytes 60000000 | tf_op jit(solution)/shard_map/fold/pallas_call | solution.py:606
  210.3 75.5 %experts.2 = (bf16[512,1536]{1,0:T(8,128)(2,1)}, bf16[512,1536]{1,0:T(8,128)(2,1)}, bf16[512,1536]{1,0:T(8,128)(2,1)}, bf16[512,1536]{1,0:T(8,128)(2,1)}, f32[10...) custom-call(s32[1]{0:T(128)} %copy.247.chosen_ref, bf16[512,1536]{1,0:T(8,128)(2,1)} %copy-done.9, ...), custom_call_target="tpu_custom_call" | custom-call | flops 80000000000 | bytes 50000000 | tf_op jit(solution)/shard_map/experts/pallas_call | solution.py:524
  285.8 10.2 %all-to-all-start = ((bf16[16,80,768]{2,1,0:T(8,128)(2,1)}), bf16[16,80,768]{2,1,0:T(8,128)(2,1)}, u32[]{:S(2)}, u32[]{:S(2)}) async-start(bf16[16,80,768]{2,1,0:T(8,128)(2,1)} %bitcast.218), calls=%async_computation | async-start | bytes 3932160 | tf_op jit(solution)/shard_map/all_to_all | solution.py:1028
  296.1 77.8 %experts.3 = (bf16[512,1536]{1,0:T(8,128)(2,1)}, bf16[512,1536]{1,0:T(8,128)(2,1)}, bf16[512,1536]{1,0:T(8,128)(2,1)}, bf16[512,1536]{1,0:T(8,128)(2,1)}, f32[10...) custom-call(s32[1]{0:T(128)} %copy.247.chosen_ref, bf16[512,1536]{1,0:T(8,128)(2,1)} %copy-done.9, ...), custom_call_target="tpu_custom_call" | custom-call | flops 80000000000 | bytes 50000000 | tf_op jit(solution)/shard_map/experts/pallas_call | solution.py:524
  383.3 6.0 all-to-all-start.2
  390.9 27.0 %collective-permute-done.10 = bf16[512,1536]{1,0:T(8,128)(2,1)S(1)} collective-permute-done((bf16[512,1536]{1,0:T(8,128)(2,1)}, bf16[512,1536]{1,0:T(8,128)(2,1)S(1)}, u32[]{:S(2)}, u32[]{:S(2)}) %collective-permute-start.10) | collective-permute-done | bytes 1572896 | tf_op jit(solution)/shard_map/ppermute | solution.py:771
  431.5 9.7 %all-to-all-done.2.rows_ref = bf16[16,80,768]{2,1,0:T(8,128)(2,1)} async-done(((bf16[16,80,768]{2,1,0:T(8,128)(2,1)}), bf16[16,80,768]{2,1,0:T(8,128)(2,1)}, u32[]{:S(2)}, u32[]{:S(2)}) %all-to-all-start.2) | async-done | bytes 1966112 | tf_op jit(solution)/shard_map/all_to_all | solution.py:1028
  454.8 14.5 %attention_back.2 = (bf16[512,768]{1,0:T(8,128)(2,1)S(1)}, bf16[512,256]{1,0:T(8,128)(2,1)S(1)}, bf16[512,256]{1,0:T(8,128)(2,1)S(1)}, bf16[512,256]{1,0:T(8,128)(2,1)S(1)}, bf16[512,256]{1,0:T(8,128)(2,1)S(1)}) custom-call(s32[64]{0:T(128)S(1)} %reshape.302.list_ref, s32[4]{0:T(128)S(1)} %and_select_fusion.steps_ref, bf16[512,1536]{1,0:T(8,128)(2,1)S(1)} %copy-done.34, ...), custom_call_target="tpu_custom_call" | custom-call | flops 33999998976 | bytes 6000000 | tf_op jit(solution)/shard_map/attention_back/pallas_call | solution.py:355
  469.4 10.2 %collective-permute-start.13 = (bf16[512,512]{1,0:T(8,128)(2,1)S(1)}, bf16[512,512]{1,0:T(8,128)(2,1)S(1)}, u32[]{:S(2)}, u32[]{:S(2)}) collective-permute-start(bf16[512,512]{1,0:T(8,128)(2,1)S(1)} %pad_maximum_fusion.1), channel_id=1, source_target_pairs={{0,1},{1,0},{2,3},{3,2},{4,5},{5,4},{6,7},{7,6},{8,9},{9,8},{10,11... | collective-permute-start | bytes 1572872 | tf_op jit(solution)/shard_map/ppermute | solution.py:771
  479.6 14.5 %attention_back.3 = (bf16[512,768]{1,0:T(8,128)(2,1)S(1)}, bf16[512,256]{1,0:T(8,128)(2,1)S(1)}, bf16[512,256]{1,0:T(8,128)(2,1)S(1)}, bf16[512,256]{1,0:T(8,128)(2,1)S(1)}, bf16[512,256]{1,0:T(8,128)(2,1)S(1)}) custom-call(s32[64]{0:T(128)S(1)} %reshape.302.list_ref, s32[4]{0:T(128)S(1)} %and_select_fusion.steps_ref, bf16[512,1536]{1,0:T(8,128)(2,1)S(1)} %copy-done.34, ...), custom_call_target="tpu_custom_call" | custom-call | flops 33999998976 | bytes 6000000 | tf_op jit(solution)/shard_map/attention_back/pallas_call | solution.py:355
  494.2 8.7 %collective-permute-start.14 = (bf16[512,512]{1,0:T(8,128)(2,1)S(1)}, bf16[512,512]{1,0:T(8,128)(2,1)S(1)}, u32[]{:S(2)}, u32[]{:S(2)}) collective-permute-start(bf16[512,512]{1,0:T(8,128)(2,1)S(1)} %pad_maximum_fusion.2), channel_id=1, source_target_pairs={{0,1},{1,0},{2,3},{3,2},{4,5},{5,4},{6,7},{7,6},{8,9},{9,8},{10,11... | collective-permute-start | bytes 1572872 | tf_op jit(solution)/shard_map/ppermute | solution.py:771
  512.7 45.7 %all-to-all-start.1 = ((bf16[32,8,768]{2,1,0:T(8,128)(2,1)}), bf16[32,8,768]{2,1,0:T(8,128)(2,1)}, u32[]{:S(2)}, u32[]{:S(2)}) async-start(bf16[32,8,768]{2,1,0:T(8,128)(2,1)} %bitcast.45.refs_0_), calls=%async_computation.1 | async-start | bytes 786432 | tf_op jit(solution)/shard_map/all_to_all | solution.py:1123
  565.2 6.6 %fusion.10 = (f32[512]{0:T(512)S(1)}, f32[512,1536]{1,0:T(8,128)S(1)}) fusion(bf16[512,1536]{1,0:T(8,128)(2,1)S(1)} %copy-done.46, f32[512]{0:T(512)S(1)} %copy-done.98, f32[1536]{0:T(1024)S(1)} %copy-done.95, f32[512,1536]{1,0:T(8,128)S(1)} %fusion.40, f32[512,1536]{1,0:T(8,128)} %fusion.21, bf16[512,1536]{1,0:T(8,128)(2,1)S(1)} %copy-done.41, ...), kind=kOutput, calls=%fused_computation.22 | convolution fusion | flops 2442657280 | bytes 17311744 | tf_op jit(solution)/shard_map/dot_general | solution.py:30
  575.1 34.6 %all-gather.1 = bf16[64,8,768]{2,1,0:T(8,128)(2,1)S(1)} all-gather(bf16[4,8,768]{2,1,0:T(8,128)(2,1)S(1)} %select_reduce_fusion.1), channel_id=3, replica_groups=mesh['rep'=16,'grp'=2] {'rep'}, dimensions={0}, use_global_device_ids=true | all-gather | bytes 835584 | tf_op jit(solution)/shard_map/all_gather | solution.py:1126
  619.2 6.2 unpack.2
  628.6 6.2 unpack.3
  (435 shorter events, 142.4 us)
Async XLA Ops:
  7.2 109.3 %all-gather.9.cloned.1.call-start = ((), (), s32[]{:S(2)}) async-start(), calls=%async_computation.3 | async-start | bytes 2506752 | tf_op jit(solution)/shard_map/all_gather | solution.py:804
  9.5 69.9 %collective-permute-start.2 = (bf16[384,1024]{1,0:T(8,128)(2,1)}, bf16[384,1024]{1,0:T(8,128)(2,1)}, u32[]{:S(2)}, u32[]{:S(2)}) collective-permute-start(bf16[384,1024]{1,0:T(8,128)(2,1)} %constant_dynamic-slice_fusion.1), channel_id=1, source_target_pairs={{0,1},{1,0},{2,3},{3,2},{4,5},{5,4},{6,7},{7,6},{8,9},{9,8},{10,11... | collective-permute-start | bytes 2359304 | tf_op jit(solution)/shard_map/ppermute | solution.py:788
  21.9 52.3 %collective-permute-start = (bf16[1,128000]{1,0:T(2,128)(2,1)}, bf16[1,128000]{1,0:T(2,128)(2,1)}, u32[]{:S(2)}, u32[]{:S(2)}) collective-permute-start(bf16[1,128000]{1,0:T(2,128)(2,1)} %broadcast_in_dim.191), channel_id=1, source_target_pairs={{0,1},{1,0},{2,3},{3,2},{4,5},{5,4},{6,7},{7,6},{8,9},{9,8},{10,11... | collective-permute-start | bytes 768008 | tf_op jit(solution)/shard_map/ppermute | solution.py:756
  22.8 22.4 %collective-permute-start.1 = (bf16[48,1536]{1,0:T(8,128)(2,1)S(1)}, bf16[48,1536]{1,0:T(8,128)(2,1)S(1)}, u32[]{:S(2)}, u32[]{:S(2)}) collective-permute-start(bf16[48,1536]{1,0:T(8,128)(2,1)S(1)} %constant_dynamic-slice_fusion.2), channel_id=1, source_target_pairs={{0,1},{1,0},{2,3},{3,2},{4,5},{5,4},{6,7},{7,6},{8,9},{9,8},{10,11... | collective-permute-start | bytes 442376 | tf_op jit(solution)/shard_map/ppermute | solution.py:802
  25.9 46.7 %collective-permute-start.5 = (bf16[48,1536]{1,0:T(8,128)(2,1)S(1)}, bf16[48,1536]{1,0:T(8,128)(2,1)}, u32[]{:S(2)}, u32[]{:S(2)}) collective-permute-start(bf16[48,1536]{1,0:T(8,128)(2,1)S(1)} %constant_dynamic-slice_fusion), channel_id=1, source_target_pairs={{0,1},{1,0},{2,3},{3,2},{4,5},{5,4},{6,7},{7,6},{8,9},{9,8},{10,11... | collective-permute-start | bytes 442376 | tf_op jit(solution)/shard_map/ppermute | solution.py:802
  25.9 45.4 %collective-permute-start.8 = (s32[512,8]{0,1:T(8,128)S(1)}, s32[512,8]{0,1:T(8,128)S(1)}, u32[]{:S(2)}, u32[]{:S(2)}) collective-permute-start(s32[512,8]{0,1:T(8,128)S(1)} %copy-done.86), channel_id=1, source_target_pairs={{0,1},{1,0},{2,3},{3,2},{4,5},{5,4},{6,7},{7,6},{8,9},{9,8},{10,11... | collective-permute-start | bytes 49160 | tf_op jit(solution)/shard_map/ppermute | solution.py:756
  45.9 97.8 %all-gather.11.cloned.1.call-start = ((), (), s32[]{:S(2)}) async-start(), calls=%async_computation.4 | async-start | bytes 2924544 | tf_op jit(solution)/shard_map/all_gather | solution.py:806
  79.1 107.5 %copy-start.60 = (bf16[2,8,2,768]{3,1,2,0:T(8,128)(2,1)}, bf16[2,8,2,768]{3,1,2,0:T(8,128)(2,1)S(1)}, u32[]{:S(2)}) copy-start(bf16[2,8,2,768]{3,1,2,0:T(8,128)(2,1)S(1)} %copy.206) | copy-start | bytes 147460
  79.3 107.8 %copy-start.88 = (bf16[16,40]{1,0:T(8,128)(2,1)}, bf16[16,40]{1,0:T(8,128)(2,1)S(1)}, u32[]{:S(2)}) copy-start(bf16[16,40]{1,0:T(8,128)(2,1)S(1)} %reshape.323) | copy-start | bytes 3844
  79.4 3.1 collective-permute-start.3
  87.4 25.9 %collective-permute-start.4 = (bf16[512,1024]{1,0:T(8,128)(2,1)S(1)}, bf16[512,1024]{1,0:T(8,128)(2,1)S(1)}, u32[]{:S(2)}, u32[]{:S(2)}) collective-permute-start(bf16[512,1024]{1,0:T(8,128)(2,1)S(1)} %pad_maximum_fusion.k_ref.v_ref.refs_2_), channel_id=1, source_target_pairs={{0,1},{1,0},{2,3},{3,2},{4,5},{5,4},{6,7},{7,6},{8,9},{9,8},{10,11... | collective-permute-start | bytes 3145736 | tf_op jit(solution)/shard_map/ppermute | solution.py:756
  114.8 94.3 %collective-permute-start.7 = (bf16[512,1536]{1,0:T(8,128)(2,1)}, bf16[512,1536]{1,0:T(8,128)(2,1)}, u32[]{:S(2)}, u32[]{:S(2)}) collective-permute-start(bf16[512,1536]{1,0:T(8,128)(2,1)} %delayed.1), channel_id=1, source_target_pairs={{0,1},{1,0},{2,3},{3,2},{4,5},{5,4},{6,7},{7,6},{8,9},{9,8},{10,11... | collective-permute-start | bytes 4718600 | tf_op jit(solution)/shard_map/ppermute | solution.py:756
  154.7 54.4 %collective-permute-start.6 = (bf16[512,1536]{1,0:T(8,128)(2,1)S(1)}, bf16[512,1536]{1,0:T(8,128)(2,1)S(1)}, u32[]{:S(2)}, u32[]{:S(2)}) collective-permute-start(bf16[512,1536]{1,0:T(8,128)(2,1)S(1)} %multiply_convert_fusion.refs_0_.x_ref), channel_id=1, source_target_pairs={{0,1},{1,0},{2,3},{3,2},{4,5},{5,4},{6,7},{7,6},{8,9},{9,8},{10,11... | collective-permute-start | bytes 4718600 | tf_op jit(solution)/shard_map/ppermute | solution.py:756
  187.5 20.9 %collective-permute-start.9 = (f32[20,512]{1,0:T(8,128)S(1)}, f32[20,512]{1,0:T(8,128)S(1)}, u32[]{:S(2)}, u32[]{:S(2)}) collective-permute-start(f32[20,512]{1,0:T(8,128)S(1)} %get-tuple-element.261), channel_id=1, source_target_pairs={{0,1},{1,0},{2,3},{3,2},{4,5},{5,4},{6,7},{7,6},{8,9},{9,8},{10,11... | collective-permute-start | bytes 122888 | tf_op jit(solution)/shard_map/ppermute | solution.py:756
  285.8 88.1 %all-to-all-start = ((bf16[16,80,768]{2,1,0:T(8,128)(2,1)}), bf16[16,80,768]{2,1,0:T(8,128)(2,1)}, u32[]{:S(2)}, u32[]{:S(2)}) async-start(bf16[16,80,768]{2,1,0:T(8,128)(2,1)} %bitcast.218), calls=%async_computation | async-start | bytes 3932160 | tf_op jit(solution)/shard_map/all_to_all | solution.py:1028
  296.0 320.0 %all-gather.15.cloned.1.call-start = ((), (), s32[]{:S(2)}) async-start(), calls=%async_computation.6 | async-start | bytes 8355840 | tf_op jit(solution)/shard_map/all_gather | solution.py:1027
  380.0 9.5 %collective-permute-start.12 = (f32[20,512]{1,0:T(8,128)}, f32[20,512]{1,0:T(8,128)S(1)}, u32[]{:S(2)}, u32[]{:S(2)}) collective-permute-start(f32[20,512]{1,0:T(8,128)} %get-tuple-element.258), channel_id=1, source_target_pairs={{0,1},{1,0},{2,3},{3,2},{4,5},{5,4},{6,7},{7,6},{8,9},{9,8},{10,11... | collective-permute-start | bytes 122888 | tf_op jit(solution)/shard_map/ppermute | solution.py:756
  380.3 37.6 %collective-permute-start.10 = (bf16[512,1536]{1,0:T(8,128)(2,1)}, bf16[512,1536]{1,0:T(8,128)(2,1)S(1)}, u32[]{:S(2)}, u32[]{:S(2)}) collective-permute-start(bf16[512,1536]{1,0:T(8,128)(2,1)} %get-tuple-element.106), channel_id=1, source_target_pairs={{0,1},{1,0},{2,3},{3,2},{4,5},{5,4},{6,7},{7,6},{8,9},{9,8},{10,11... | collective-permute-start | bytes 4718600 | tf_op jit(solution)/shard_map/ppermute | solution.py:771
  383.3 57.9 %all-to-all-start.2 = ((bf16[16,80,768]{2,1,0:T(8,128)(2,1)}), bf16[16,80,768]{2,1,0:T(8,128)(2,1)}, u32[]{:S(2)}, u32[]{:S(2)}) async-start(bf16[16,80,768]{2,1,0:T(8,128)(2,1)} %bitcast.217), calls=%async_computation.2 | async-start | bytes 3932160 | tf_op jit(solution)/shard_map/all_to_all | solution.py:1028
  389.3 236.1 %all-gather.13.cloned.1.call-start = ((), (), s32[]{:S(2)}) async-start(), calls=%async_computation.5 | async-start | bytes 8355840 | tf_op jit(solution)/shard_map/all_gather | solution.py:1101
  469.4 37.0 %collective-permute-start.13 = (bf16[512,512]{1,0:T(8,128)(2,1)S(1)}, bf16[512,512]{1,0:T(8,128)(2,1)S(1)}, u32[]{:S(2)}, u32[]{:S(2)}) collective-permute-start(bf16[512,512]{1,0:T(8,128)(2,1)S(1)} %pad_maximum_fusion.1), channel_id=1, source_target_pairs={{0,1},{1,0},{2,3},{3,2},{4,5},{5,4},{6,7},{7,6},{8,9},{9,8},{10,11... | collective-permute-start | bytes 1572872 | tf_op jit(solution)/shard_map/ppermute | solution.py:771
  494.2 15.9 %collective-permute-start.14 = (bf16[512,512]{1,0:T(8,128)(2,1)S(1)}, bf16[512,512]{1,0:T(8,128)(2,1)S(1)}, u32[]{:S(2)}, u32[]{:S(2)}) collective-permute-start(bf16[512,512]{1,0:T(8,128)(2,1)S(1)} %pad_maximum_fusion.2), channel_id=1, source_target_pairs={{0,1},{1,0},{2,3},{3,2},{4,5},{5,4},{6,7},{7,6},{8,9},{9,8},{10,11... | collective-permute-start | bytes 1572872 | tf_op jit(solution)/shard_map/ppermute | solution.py:771
  504.7 108.3 %collective-permute-start.11 = (bf16[512,1536]{1,0:T(8,128)(2,1)}, bf16[512,1536]{1,0:T(8,128)(2,1)}, u32[]{:S(2)}, u32[]{:S(2)}) collective-permute-start(bf16[512,1536]{1,0:T(8,128)(2,1)} %get-tuple-element.107), channel_id=1, source_target_pairs={{0,1},{1,0},{2,3},{3,2},{4,5},{5,4},{6,7},{7,6},{8,9},{9,8},{10,11... | collective-permute-start | bytes 4718600 | tf_op jit(solution)/shard_map/ppermute | solution.py:764
  512.7 61.0 %all-to-all-start.1 = ((bf16[32,8,768]{2,1,0:T(8,128)(2,1)}), bf16[32,8,768]{2,1,0:T(8,128)(2,1)}, u32[]{:S(2)}, u32[]{:S(2)}) async-start(bf16[32,8,768]{2,1,0:T(8,128)(2,1)} %bitcast.45.refs_0_), calls=%async_computation.1 | async-start | bytes 786432 | tf_op jit(solution)/shard_map/all_to_all | solution.py:1123
  (100 other events, 1212.9 us)
Sparse Core Ops, SparseCore 0:
  46.0 44.1 all-gather.8
  93.0 42.5 all-gather.10
  377.3 103.9 all-gather.14
  483.5 70.4 all-gather.12

commit v5 on v4

--- a/solution.py
+++ b/solution.py
@@ -52,17 +52,13 @@
 def ancestry(parent_row):
     total = parent_row.shape[0]
     labels = jnp.arange(total, dtype=jnp.int32)
-
-    def climb(count, state):
-        current, table = state
-        current = jnp.sum(
-            jnp.where(current[:, None] == labels[None, :], parent_row[None, :], 0), axis=1
-        )
-        table = jnp.maximum(table, (current[:, None] == labels[None, :]).astype(jnp.int32))
-        return (current, table)
-
-    start_index = (labels[:, None] == labels[None, :]).astype(jnp.int32)
-    return lax.fori_loop(0, total, climb, (labels, start_index))[1]
+    own = labels[:, None] == labels[None, :]
+    reached = jnp.logical_or(own, parent_row[:, None] == labels[None, :])
+    steps = 1
+    while steps < total:
+        reached = jnp.any(jnp.logical_and(reached[:, :, None], reached[None, :, :]), axis=1)
+        steps *= 2
+    return reached.astype(jnp.int32)
 
 
 def tile_parts(ref_k, seg_a, seg_b):
@@ -670,13 +666,14 @@
 
 
 def add_up(first, second, third, after=()):
+    block, count = row_blocks(first)
     return pl.pallas_call(
         add_kernel,
-        in_specs=[pl.BlockSpec(memory_space=pltpu.VMEM)] * 3
-        + [pl.BlockSpec(memory_space=pl.ANY)] * len(after),
-        out_specs=pl.BlockSpec(memory_space=pltpu.VMEM),
+        grid=(count,),
+        in_specs=[block] * 3 + [pl.BlockSpec(memory_space=pl.ANY)] * len(after),
+        out_specs=block,
         out_shape=jax.ShapeDtypeStruct(first.shape, BF16),
-        compiler_params=pltpu.CompilerParams(vmem_limit_bytes=32 * 1024 * 1024),
+        compiler_params=pltpu.CompilerParams(vmem_limit_bytes=16 * 1024 * 1024),
         name="add_up",
     )(first, second, third, *after)
 
@@ -780,63 +777,61 @@
     return jnp.where(ahead, jnp.concatenate([near, far], axis=0), jnp.concatenate([far, near], axis=0))
 
 
-def gather_rows(half):
-    if lax.axis_size("grp") != 2:
-        return lax.all_gather(half, "grp", axis=0, tiled=True)
+def fetch_halves(half, after):
+    groups = lax.axis_size("grp")
+    member = lax.axis_index("grp")
+    if groups != 2:
+        return [(from_others(half), None)]
     rows = half.shape[0] // 2
     core = lax.axis_index("rep") % 2
-    got = lax.ppermute(lax.dynamic_slice_in_dim(half, core * rows, rows, 0), "grp", swap_pairs(2))
+    mine = delayed(lax.dynamic_slice_in_dim(half, core * rows, rows, 0), after)
+    got = lax.ppermute(mine, "grp", swap_pairs(2))
     other = lax.ppermute(got, "rep", swap_pairs(lax.axis_size("rep")))
-    ahead = core == 0
-    far = jnp.where(ahead, jnp.concatenate([got, other], 0), jnp.concatenate([other, got], 0))
-    return in_order(half, far)
-
-
-def gather_rows_wide(half, note=None):
+    away = (1 - member) * 2 * rows
+    return [(got, away + core * rows), (other, away + (1 - core) * rows)]
+
+
+def fetch_wide(half, note=None):
     reps = lax.axis_size("rep")
     if lax.axis_size("grp") != 2 or half.shape[0] % (reps * 16):
-        whole = lax.all_gather(half, "grp", axis=0, tiled=True)
-        return (whole, lax.all_gather(note, "rep", axis=0)) if note is not None else whole
+        notes = None if note is None else lax.all_gather(note, "rep", axis=0)
+        far = from_others(half)
+        return far, notes, half
     rows = half.shape[0] // reps
     mine = lax.dynamic_slice_in_dim(half, lax.axis_index("rep") * rows, rows, 0)
     got = lax.ppermute(mine, "grp", swap_pairs(2))
     if note is None:
-        return in_order(half, lax.all_gather(got, "rep", axis=0, tiled=True))
-    got = jnp.concatenate([got, jnp.broadcast_to(note[None], (8, note.shape[0]))], axis=0)
-    every = lax.all_gather(got, "rep", axis=0)
-    return in_order(half, every[:, :rows].reshape(half.shape)), every[:, rows]
+        return lax.all_gather(got, "rep", axis=0, tiled=True), None, mine
+    noted = jnp.concatenate([got, jnp.broadcast_to(note[None], (8, note.shape[0]))], axis=0)
+    every = lax.all_gather(noted, "rep", axis=0)
+    return every[:, :rows].reshape(half.shape), every[:, rows], mine
+
+
+def columns(rows, start, count):
+    return lax.dynamic_slice_in_dim(rows, start, count, 1)
 
 
 def delayed_kernel(rows_ref, *refs):
     refs[-1][...] = rows_ref[...]
 
 
+def row_blocks(rows):
+    count = 4 if rows.shape[0] % 64 == 0 else 1
+    shape = (rows.shape[0] // count,) + rows.shape[1:]
+    return pl.BlockSpec(shape, lambda i: (i,) + (0,) * (rows.ndim - 1)), count
+
+
 def delayed(rows, after):
+    block, count = row_blocks(rows)
     return pl.pallas_call(
         delayed_kernel,
-        in_specs=[pl.BlockSpec(memory_space=pltpu.VMEM)] + [pl.BlockSpec(memory_space=pl.ANY)] * len(after),
-        out_specs=pl.BlockSpec(memory_space=pltpu.VMEM),
+        grid=(count,),
+        in_specs=[block] + [pl.BlockSpec(memory_space=pl.ANY)] * len(after),
+        out_specs=block,
         out_shape=jax.ShapeDtypeStruct(rows.shape, rows.dtype),
         compiler_params=pltpu.CompilerParams(vmem_limit_bytes=16 * 1024 * 1024),
         name="delayed",
     )(rows, *after)
-
-
-def pack(pieces, multiple):
-    flat = jnp.concatenate([piece.reshape(-1) for piece in pieces])
-    return jnp.pad(flat, (0, -flat.shape[0] % multiple))
-
-
-def unpack(flat, shapes):
-    out = []
-    offset = 0
-    for shape in shapes:
-        size = 1
-        for extent in shape:
-            size *= extent
-        out.append(flat[..., offset : offset + size].reshape(flat.shape[:-1] + shape))
-        offset += size
-    return out
 
 
 def local(
@@ -882,59 +877,61 @@
     first = member * count
     adapters = a_qkv.shape[0]
 
-    shapes = (
-        (3 * RANK, part),
-        (RANK, part),
-        (2, RANK, kv_width // groups),
-        (RANK, part),
-        (RANK, part),
-        (RANK, part),
-        (RANK, experts_dev),
-        (experts, part),
-        (part,),
-        (part,),
-        (count,),
+    kv_part = kv_width // groups
+    odd = jnp.concatenate([b_keyval[chosen, 0], b_keyval[chosen, 1], b_router[chosen]], axis=1)
+    small = jnp.concatenate(
+        [
+            a_qkv.swapaxes(1, 2)[chosen],
+            b_query[chosen],
+            a_output.swapaxes(1, 2)[chosen],
+            b_output[chosen],
+            a_router.swapaxes(1, 2)[chosen],
+            jnp.pad(odd, ((0, 0), (0, part - odd.shape[1]))),
+            w_router.T,
+            gain_attn[None],
+            gain_ffn[None],
+            jnp.pad(padding.astype(BF16)[None], ((0, 5), (0, part - count))),
+        ],
+        axis=0,
     )
-    small = pack(
-        (
-            a_qkv[chosen].T,
-            b_query[chosen],
-            b_keyval[chosen],
-            a_output[chosen].T,
-            b_output[chosen],
-            a_router[chosen].T,
-            b_router[chosen],
-            w_router.T,
-            gain_attn,
-            gain_ffn,
-            padding.astype(BF16),
-        ),
-        1024,
-    )
-    small_all = in_order(small[None], from_others(small[None]))
-
-    def join(piece):
-        return jnp.moveaxis(piece, 0, -2).reshape(piece.shape[1:-1] + (-1,))
-
-    (
-        qkv_in,
-        query_out,
-        keyval_out,
-        output_in,
-        output_out,
-        router_in,
-        router_out,
-        router_full,
-        attn_gain,
-        ffn_gain,
-        pad_all,
-    ) = [join(piece) for piece in unpack(small_all, shapes)]
+    if groups == 2:
+        small_far = from_others(small)
+        joined = jnp.where(
+            member == 0,
+            jnp.concatenate([small, small_far], axis=1),
+            jnp.concatenate([small_far, small], axis=1),
+        )
+    else:
+        joined = in_order(small[None], from_others(small[None])).swapaxes(0, 1).reshape(-1, width)
+    qkv_in = joined[: 3 * RANK]
+    query_out = joined[3 * RANK : 4 * RANK]
+    output_in = joined[4 * RANK : 5 * RANK]
+    output_out = joined[5 * RANK : 6 * RANK]
+    router_in = joined[6 * RANK : 7 * RANK]
+    odd = joined[7 * RANK : 8 * RANK].reshape(RANK, groups, part)
+    keyval_out = [odd[:, :, n * kv_part : (n + 1) * kv_part].reshape(RANK, kv_width) for n in range(2)]
+    router_out = odd[:, :, 2 * kv_part : 2 * kv_part + experts_dev].reshape(RANK, experts)
+    router_full = joined[8 * RANK : 8 * RANK + experts]
+    last = 8 * RANK + experts
+    attn_gain = joined[last]
+    ffn_gain = joined[last + 1]
+    pad_all = joined[last + 2].reshape(groups, part)[:, :count].reshape(-1)
     attn_gain = attn_gain.astype(F32)
     ffn_gain = ffn_gain.astype(F32)
-    keyval_full = gather_rows(w_keyval)
-    query_full = gather_rows_wide(w_query)
+    query_far, _, query_piece = fetch_wide(w_query)
+    keyval_far = fetch_halves(w_keyval, (query_piece,))
+    query_full = in_order(w_query, query_far)
+    if groups == 2:
+        (got, _), (other, _) = keyval_far
+        ahead = lax.axis_index("rep") % 2 == 0
+        keyval_full = in_order(
+            w_keyval, jnp.where(ahead, jnp.concatenate([got, other], 0), jnp.concatenate([other, got], 0))
+        )
+    else:
+        keyval_full = in_order(w_keyval, keyval_far[0][0])
     note = (jnp.arange(width, dtype=jnp.int32) == chosen).astype(BF16)
-    output_full, notes = gather_rows_wide(w_output, note)
+    output_far, notes, _ = fetch_wide(w_output, note)
+    output_full = in_order(w_output, output_far)
     ids_all = jnp.sum(
         notes[:, :adapters].astype(jnp.int32) * jnp.arange(adapters, dtype=jnp.int32), axis=1
     )
@@ -956,7 +953,13 @@
     tokens_f = tokens.astype(F32)
     normed = rms_norm(tokens_f, attn_gain).astype(BF16)
     low_rank = product_back(normed, qkv_in).astype(BF16)
-    keyvals = product(normed, keyval_full)
+    own_columns = columns(normed, member * part, part)
+    if groups == 2:
+        keyvals = product(own_columns, w_keyval)
+        for piece, start in keyval_far:
+            keyvals = keyvals + product(columns(normed, start, piece.shape[0]), piece)
+    else:
+        keyvals = product(normed, keyval_full)
     keyvals = jnp.concatenate(
         [
             keyvals[:, :kv_width] + product(low_rank[:, RANK : 2 * RANK], keyval_out[0]),
@@ -967,7 +970,11 @@
     folded = [fold(0, True, first_fold, (keyvals,))]
     keyvals_far = from_others(keyvals)
     upstream_far = from_others(delayed(cotangent, (keyvals_far,)))
-    query_rows = (product(normed, query_full) + product(low_rank[:, :RANK], query_out)).astype(BF16)
+    if groups == 2:
+        query_rows = product(own_columns, w_query) + product(columns(normed, (1 - member) * part, part), query_far)
+    else:
+        query_rows = product(normed, query_full)
+    query_rows = (query_rows + product(low_rank[:, :RANK], query_out)).astype(BF16)
     pad_whole = jnp.roll(pad_all, -first)
     listing, steps, own_bias, live = visits(parents[0], pad_whole[:count], pad_whole[count:], first)
     attended, logs = run_attention(listing, steps, query_rows, keyvals, keyvals_far, own_bias, live)
@@ -1037,8 +1044,6 @@
         d_gates = lax.all_to_all(d_gates, "grp", split_axis=1, concat_axis=0, tiled=True)
     d_gates = d_gates.reshape(experts, count).T
     d_sum = to_owners(d_near, d_far)
-    result_far, d_sum = lax.optimization_barrier((result_far, d_sum))
-    mixture = owners_terms(result_near, result_far)
     upstream = cotangent.astype(F32)
     d_logits = (gates * (d_gates - jnp.sum(gates * d_gates, axis=1, keepdims=True))).astype(BF16)
 
@@ -1068,9 +1073,14 @@
             logs,
             n * pairs,
             pairs,
+            (last,) if n else (),
         )
         d_kv = to_owners(jnp.concatenate(d_kv[:2], axis=1), jnp.concatenate(d_kv[2:], axis=1)).astype(BF16)
         parts.append((d_q, d_kv[:, : kv_width // 2], d_kv[:, kv_width // 2 :]))
+        if n == 0:
+            last = totals(ids_all, swapped, adapters, after=(d_q,))
+            spread.append(lax.all_gather(last, "rep", axis=0))
+    mixture = owners_terms(result_near, delayed(result_far, (parts[1][1],)))
     d_queries, d_keys, d_values = [jnp.concatenate(pair, axis=1) for pair in zip(*parts)]
     d_keyvals = jnp.concatenate([d_keys, d_values], axis=1)
     d_rank_qkv = jnp.concatenate(
@@ -1097,8 +1107,6 @@
         axis=0,
     )
 
-    last = totals(ids_all, swapped, adapters, after=(attended_gradient,))
-    spread.append(lax.all_gather(last, "rep", axis=0))
     expert_grads = ()
     for n in range(calls):
         expert_grads = unpack_grads(spread[n], experts_dev, n * each, tuple(expert_grads), width)
@@ -1108,7 +1116,6 @@
         [grad_qkv_in, grad_query_out, grad_output_in, grad_output_out, grad_router_in], axis=0
     ).astype(BF16)
     high = tall.shape[0]
-    kv_part = kv_width // groups
     tall = tall.reshape(high, groups, part).swapaxes(0, 1)
     wide = [
         grad_keyval_out[0].reshape(RANK, groups, kv_part),

time: 649 us -> 604 us (0.931)
  starting transfers between devices: 109 us -> 76 us
  waiting for transfers between devices: 59.8 us -> 45.8 us
  blocking collectives: 34.6 us -> 20.9 us
  Pallas kernels: 297 us -> 308 us
    all_to_all x1, starting transfers between devices: 45.7 us -> 12.7 us  [local(): lax.all_to_all(dense, ('rep', 'grp'), split_axis=0, concat_axis=0, tiled=...]
    ppermute x7, waiting for transfers between devices: 4.54 us -> 33.8 us  [from_others(): return lax.ppermute(piece, 'grp', swap_pairs(2))]
    ppermute x3, waiting for transfers between devices: 30.5 us -> 6.48 us  [to_owners(): lax.ppermute(far, 'grp', swap_pairs(2)).astype(F32)]
    ppermute x4, waiting for transfers between devices: 15.1 us -> 1.2 us  [the longest x2 1.19 us: fetch_wide(): got = lax.ppermute(mine, 'grp', swap_pairs(2))]
    all_gather x1, blocking collectives: 34.6 us -> 20.9 us  [local(): lax.all_gather(dense, 'rep', axis=0).swapaxes(0, 1)]
    all_to_all x2, waiting for transfers between devices: 9.7 us -> 0.01 us  [local(): lax.all_to_all(grads.reshape(reps, -1, UNIT), 'rep', split_axis=0, concat...]
    dot_general x12 -> x15, matrix products: 24 us -> 28.4 us  [product(): return jnp.dot(left, right, preferred_element_type=F32)]
    unnamed x222 -> x231, local copies, waits for them, and re-layouts: 34.4 us -> 37.8 us
  transfers between devices with their start and end apart: 22 -> 22, of which waited for: 5 -> 5; matrix products, arithmetic and copies ran while one was open for 14% -> 14% of each run, Pallas kernels for 33% -> 38%
where the time goes in v5:
time: 604 us; the launch traced here: 592 us
  Pallas kernels  308 us (51%)
  starting transfers between devices  76 us (13%)
  local copies, waits for them, and re-layouts  53.2 us (9%)
  matrix products  50.7 us (8%)
  waiting for transfers between devices  45.8 us (8%)
  blocking collectives  20.9 us (3%)
  other arithmetic  20.7 us (3%)
  between operations  16.3 us (3%)
    pallas_call x2, Pallas kernels, run_experts(): pl.pallas_call(functools.partial(expert_kernel, blocks=blocks, rows_block...  153 us
    pallas_call x4, Pallas kernels, fold_adapters(): pl.pallas_call(fold_kernel, grid_spec=pltpu.PrefetchScalarGridSpec(num_sc...  76 us
    unnamed x231, local copies, waits for them, and re-layouts  37.8 us
    ppermute x7, waiting for transfers between devices, from_others(): return lax.ppermute(piece, 'grp', swap_pairs(2))  33.8 us
    pallas_call x2, Pallas kernels, run_attention_back(): pl.pallas_call(functools.partial(attend_back_kernel, here=here, segs=segs...  33.5 us
    dot_general x15, matrix products, product(): return jnp.dot(left, right, preferred_element_type=F32)  28.4 us
    ppermute x7, starting transfers between devices, from_others(): return lax.ppermute(piece, 'grp', swap_pairs(2))  23.9 us
    all_gather x1, blocking collectives, local(): lax.all_gather(dense, 'rep', axis=0).swapaxes(0, 1)  20.9 us
  transfers between devices with their start and end apart: 22, of which 5 were waited for; matrix products, arithmetic and copies ran while one was open for 14% of the time, Pallas kernels for 38%

profile of v5, /device:TPU:0, one launch (start us, length us, event | category | flops | bytes accessed | tf_op | source)
XLA Modules:
  0.0 592.0 jit_solution(17540908172236105464)
XLA Ops:
  35.5 19.0 %fold.6 = (bf16[10,1536,1024]{2,1,0:T(8,128)(2,1)}, bf16[10,512,1536]{2,1,0:T(8,128)(2,1)}) custom-call(s32[1]{0:T(128)} %copy.199.chosen_ref, bf16[20,1536,1024]{2,1,0:T(8,128)(2,1)} %w1_ref.7, bf16[20,512,1536]{2,1,0:T(8,128)(2,1)} %w2_ref.7, bf16[4,20,32,1536]{3,2,1,0:T(8,128)(2,1)} %bitcast.171, bf16[4,20,2,16,512]{4,3,2,1,0:T(8,128)(2,1)S(1)} %copy-done.7, ...), custom_call_target="tpu_custom_call" | custom-call | flops 15000000512 | bytes 60000000 | tf_op jit(solution)/shard_map/fold/pallas_call | solution.py:602
  71.5 19.2 %fold.7 = (bf16[10,1536,1024]{2,1,0:T(8,128)(2,1)}, bf16[10,512,1536]{2,1,0:T(8,128)(2,1)}) custom-call(s32[1]{0:T(128)} %copy.199.chosen_ref, bf16[20,1536,1024]{2,1,0:T(8,128)(2,1)} %w1_ref.7, bf16[20,512,1536]{2,1,0:T(8,128)(2,1)} %w2_ref.7, bf16[4,20,32,1536]{3,2,1,0:T(8,128)(2,1)} %bitcast.172, ...), custom_call_target="tpu_custom_call", output_to_operand_aliasing={{0}: (7, {}), {1}: (8, {})} | custom-call | flops 15000000512 | bytes 60000000 | tf_op jit(solution)/shard_map/fold/pallas_call | solution.py:602
  98.3 4.6 convolution_add_fusion.2
  104.4 18.9 %attention.1 = (bf16[512,1536]{1,0:T(8,128)(2,1)S(1)}, f32[4,512,128]{2,1,0:T(8,128)S(1)}) custom-call(s32[64]{0:T(128)S(1)} %reshape.306.list_ref, s32[4]{0:T(128)S(1)} %and_select_fusion.steps_ref, bf16[512,1536]{1,0:T(8,128)(2,1)S(1)} %fusion.28.q_ref, bf16[512,1024]{1,0:T(8,128)(2,1)S(1)} %copy-done.21, bf16[512,1024]{1,0:T(8,128)(2,1)S(1)} %copy-done.21, ...), custom_call_target="tpu_custom_call" | custom-call | flops 40000000000 | bytes 8000000 | tf_op jit(solution)/shard_map/attention/pallas_call | solution.py:317
  129.8 5.6 multiply_reduce_fusion.1
  138.0 10.8 %collective-permute-start.6 = (bf16[512,1536]{1,0:T(8,128)(2,1)S(1)}, bf16[512,1536]{1,0:T(8,128)(2,1)S(1)}, u32[]{:S(2)}, u32[]{:S(2)}) collective-permute-start(bf16[512,1536]{1,0:T(8,128)(2,1)S(1)} %multiply_convert_fusion.refs_0_.x_ref), channel_id=1, source_target_pairs={{0,1},{1,0},{2,3},{3,2},{4,5},{5,4},{6,7},{7,6},{8,9},{9,8},{10,11... | collective-permute-start | bytes 4718600 | tf_op jit(solution)/shard_map/ppermute | solution.py:753
  148.8 18.9 %fold.4 = (bf16[10,1536,1024]{2,1,0:T(8,128)(2,1)}, bf16[10,512,1536]{2,1,0:T(8,128)(2,1)}) custom-call(s32[1]{0:T(128)} %copy.199.chosen_ref, bf16[20,1536,1024]{2,1,0:T(8,128)(2,1)} %w1_ref.7, bf16[20,512,1536]{2,1,0:T(8,128)(2,1)} %w2_ref.7, bf16[4,20,32,1536]{3,2,1,0:T(8,128)(2,1)} %bitcast.173, bf16[4,20,2,16,512]{4,3,2,1,0:T(8,128)(2,1)S(1)} %copy-done.7, ...), custom_call_target="tpu_custom_call" | custom-call | flops 15000000512 | bytes 60000000 | tf_op jit(solution)/shard_map/fold/pallas_call | solution.py:602
  171.8 18.9 %fold.5 = (bf16[10,1536,1024]{2,1,0:T(8,128)(2,1)}, bf16[10,512,1536]{2,1,0:T(8,128)(2,1)}) custom-call(s32[1]{0:T(128)} %copy.199.chosen_ref, bf16[20,1536,1024]{2,1,0:T(8,128)(2,1)} %w1_ref.7, bf16[20,512,1536]{2,1,0:T(8,128)(2,1)} %w2_ref.7, bf16[4,20,32,1536]{3,2,1,0:T(8,128)(2,1)} %bitcast.174, ...), custom_call_target="tpu_custom_call", output_to_operand_aliasing={{0}: (7, {}), {1}: (8, {})} | custom-call | flops 15000000512 | bytes 60000000 | tf_op jit(solution)/shard_map/fold/pallas_call | solution.py:602
  192.8 75.7 %experts.2 = (bf16[512,1536]{1,0:T(8,128)(2,1)}, bf16[512,1536]{1,0:T(8,128)(2,1)}, bf16[512,1536]{1,0:T(8,128)(2,1)}, bf16[512,1536]{1,0:T(8,128)(2,1)}, f32[10...) custom-call(s32[1]{0:T(128)} %copy.199.chosen_ref, bf16[512,1536]{1,0:T(8,128)(2,1)} %copy-done.8, ...), custom_call_target="tpu_custom_call" | custom-call | flops 80000000000 | bytes 50000000 | tf_op jit(solution)/shard_map/experts/pallas_call | solution.py:520
  268.5 11.4 %all-to-all-start = ((bf16[16,80,768]{2,1,0:T(8,128)(2,1)}), bf16[16,80,768]{2,1,0:T(8,128)(2,1)}, u32[]{:S(2)}, u32[]{:S(2)}) async-start(bf16[16,80,768]{2,1,0:T(8,128)(2,1)} %bitcast.184), calls=%async_computation | async-start | bytes 3932160 | tf_op jit(solution)/shard_map/all_to_all | solution.py:1035
  280.0 77.5 %experts.3 = (bf16[512,1536]{1,0:T(8,128)(2,1)}, bf16[512,1536]{1,0:T(8,128)(2,1)}, bf16[512,1536]{1,0:T(8,128)(2,1)}, bf16[512,1536]{1,0:T(8,128)(2,1)}, f32[10...) custom-call(s32[1]{0:T(128)} %copy.199.chosen_ref, bf16[512,1536]{1,0:T(8,128)(2,1)} %copy-done.8, ...), custom_call_target="tpu_custom_call" | custom-call | flops 80000000000 | bytes 50000000 | tf_op jit(solution)/shard_map/experts/pallas_call | solution.py:520
  363.1 6.0 %all-to-all-start.1 = ((bf16[16,80,768]{2,1,0:T(8,128)(2,1)}), bf16[16,80,768]{2,1,0:T(8,128)(2,1)}, u32[]{:S(2)}, u32[]{:S(2)}) async-start(bf16[16,80,768]{2,1,0:T(8,128)(2,1)} %bitcast.31), calls=%async_computation.1 | async-start | bytes 3932160 | tf_op jit(solution)/shard_map/all_to_all | solution.py:1035
  369.2 29.7 %collective-permute-done.11 = f32[20,512]{1,0:T(8,128)S(1)} collective-permute-done((f32[20,512]{1,0:T(8,128)S(1)}, f32[20,512]{1,0:T(8,128)S(1)}, u32[]{:S(2)}, u32[]{:S(2)}) %collective-permute-start.11) | collective-permute-done | bytes 40992 | tf_op jit(solution)/shard_map/ppermute | solution.py:753
  412.7 16.8 %attention_back.2 = (bf16[512,768]{1,0:T(8,128)(2,1)S(1)}, bf16[512,256]{1,0:T(8,128)(2,1)S(1)}, bf16[512,256]{1,0:T(8,128)(2,1)S(1)}, bf16[512,256]{1,0:T(8,128)(2,1)S(1)}, bf16[512,256]{1,0:T(8,128)(2,1)S(1)}) custom-call(s32[64]{0:T(128)S(1)} %reshape.306.list_ref, s32[4]{0:T(128)S(1)} %and_select_fusion.steps_ref, bf16[512,1536]{1,0:T(8,128)(2,1)S(1)} %copy-done.31, ...), custom_call_target="tpu_custom_call" | custom-call | flops 33999998976 | bytes 6000000 | tf_op jit(solution)/shard_map/attention_back/pallas_call | solution.py:351
  446.0 9.1 %collective-permute-start.14 = (bf16[512,512]{1,0:T(8,128)(2,1)S(1)}, bf16[512,512]{1,0:T(8,128)(2,1)S(1)}, u32[]{:S(2)}, u32[]{:S(2)}) collective-permute-start(bf16[512,512]{1,0:T(8,128)(2,1)S(1)} %pad_maximum_fusion.2), channel_id=1, source_target_pairs={{0,1},{1,0},{2,3},{3,2},{4,5},{5,4},{6,7},{7,6},{8,9},{9,8},{10,11... | collective-permute-start | bytes 1572872 | tf_op jit(solution)/shard_map/ppermute | solution.py:768
  464.2 16.7 %attention_back.3 = (bf16[512,768]{1,0:T(8,128)(2,1)S(1)}, bf16[512,256]{1,0:T(8,128)(2,1)S(1)}, bf16[512,256]{1,0:T(8,128)(2,1)S(1)}, bf16[512,256]{1,0:T(8,128)(2,1)S(1)}, bf16[512,256]{1,0:T(8,128)(2,1)S(1)}) custom-call(s32[64]{0:T(128)S(1)} %reshape.306.list_ref, s32[4]{0:T(128)S(1)} %and_select_fusion.steps_ref, bf16[512,1536]{1,0:T(8,128)(2,1)S(1)} %copy-done.32, ...), custom_call_target="tpu_custom_call" | custom-call | flops 33999998976 | bytes 6000000 | tf_op jit(solution)/shard_map/attention_back/pallas_call | solution.py:351
  480.9 8.5 %collective-permute-start.12 = (bf16[512,512]{1,0:T(8,128)(2,1)S(1)}, bf16[512,512]{1,0:T(8,128)(2,1)S(1)}, u32[]{:S(2)}, u32[]{:S(2)}) collective-permute-start(bf16[512,512]{1,0:T(8,128)(2,1)S(1)} %pad_maximum_fusion.1), channel_id=1, source_target_pairs={{0,1},{1,0},{2,3},{3,2},{4,5},{5,4},{6,7},{7,6},{8,9},{9,8},{10,11... | collective-permute-start | bytes 1572872 | tf_op jit(solution)/shard_map/ppermute | solution.py:768
  492.3 6.5 %collective-permute-done.12 = bf16[512,512]{1,0:T(8,128)(2,1)S(1)} collective-permute-done((bf16[512,512]{1,0:T(8,128)(2,1)S(1)}, bf16[512,512]{1,0:T(8,128)(2,1)S(1)}, u32[]{:S(2)}, u32[]{:S(2)}) %collective-permute-start.12) | collective-permute-done | bytes 524320 | tf_op jit(solution)/shard_map/ppermute | solution.py:768
  501.6 12.7 %all-to-all-start.2 = ((bf16[32,8,768]{2,1,0:T(8,128)(2,1)}), bf16[32,8,768]{2,1,0:T(8,128)(2,1)}, u32[]{:S(2)}, u32[]{:S(2)}) async-start(bf16[32,8,768]{2,1,0:T(8,128)(2,1)} %bitcast.169), calls=%async_computation.2 | async-start | bytes 786432 | tf_op jit(solution)/shard_map/all_to_all | solution.py:1130
  524.5 6.6 %fusion.15 = (f32[512]{0:T(512)S(1)}, f32[512,1536]{1,0:T(8,128)S(1)}) fusion(bf16[512,1536]{1,0:T(8,128)(2,1)S(1)} %copy-done.59, f32[512]{0:T(512)S(1)} %copy-done.105, f32[1536]{0:T(1024)S(1)} %copy-done.103, f32[512,1536]{1,0:T(8,128)S(1)} %fusion.52, f32[512,1536]{1,0:T(8,128)} %fusion.21, bf16[512,1536]{1,0:T(8,128)(2,1)S(1)} %copy-done.61, ...), kind=kOutput, calls=%fused_computation.23 | convolution fusion | flops 2442657280 | bytes 17311744 | tf_op jit(solution)/shard_map/dot_general | solution.py:30
  533.0 4.3 all-to-all-done.2
  538.6 20.9 %all-gather.1 = bf16[64,8,768]{2,1,0:T(8,128)(2,1)S(1)} all-gather(bf16[4,8,768]{2,1,0:T(8,128)(2,1)S(1)} %select_reduce_fusion), channel_id=3, replica_groups=mesh['rep'=16,'grp'=2] {'rep'}, dimensions={0}, use_global_device_ids=true | all-gather | bytes 835584 | tf_op jit(solution)/shard_map/all_gather | solution.py:1133
  569.7 6.2 %unpack.2 = (f32[4,20,32,1536]{3,2,1,0:T(8,128)}, f32[4,20,2,16,512]{4,3,2,1,0:T(8,128)}, f32[4,20,16,512]{3,2,1,0:T(8,128)}, f32[4,20,16,1536]{3,2,1,0:T(8,128)}) custom-call(bf16[16,4,80,768]{3,2,1,0:T(8,128)(2,1)S(1)} %bitcast.168), custom_call_target="tpu_custom_call" | custom-call | bytes 30000000 | tf_op jit(solution)/shard_map/unpack/pallas_call | solution.py:720
  579.1 6.2 %unpack.3 = (f32[4,20,32,1536]{3,2,1,0:T(8,128)}, f32[4,20,2,16,512]{4,3,2,1,0:T(8,128)}, f32[4,20,16,512]{3,2,1,0:T(8,128)}, f32[4,20,16,1536]{3,2,1,0:T(8,128)}) custom-call(bf16[16,4,80,768]{3,2,1,0:T(8,128)(2,1)S(1)} %bitcast.167, ...), custom_call_target="tpu_custom_call", output_to_operand_aliasing={{0}: (1, {}), {1}: (2, {}), {2}: (3, {}), {3}: (4, {})} | custom-call | bytes 30000000 | tf_op jit(solution)/shard_map/unpack/pallas_call | solution.py:720
  (419 shorter events, 145.3 us)
Async XLA Ops:
  7.2 91.1 %all-gather.9.cloned.1.call-start = ((), (), s32[]{:S(2)}) async-start(), calls=%async_computation.3 | async-start | bytes 2506752 | tf_op jit(solution)/shard_map/all_gather | solution.py:804
  13.9 42.7 %collective-permute-start = (bf16[176,768]{1,0:T(8,128)(2,1)S(1)}, bf16[176,768]{1,0:T(8,128)(2,1)}, u32[]{:S(2)}, u32[]{:S(2)}) collective-permute-start(bf16[176,768]{1,0:T(8,128)(2,1)S(1)} %concatenate.119), channel_id=1, source_target_pairs={{0,1},{1,0},{2,3},{3,2},{4,5},{5,4},{6,7},{7,6},{8,9},{9,8},{10,11... | collective-permute-start | bytes 811016 | tf_op jit(solution)/shard_map/ppermute | solution.py:753
  17.8 9.5 %collective-permute-start.1 = (bf16[48,1536]{1,0:T(8,128)(2,1)S(1)}, bf16[48,1536]{1,0:T(8,128)(2,1)S(1)}, u32[]{:S(2)}, u32[]{:S(2)}) collective-permute-start(bf16[48,1536]{1,0:T(8,128)(2,1)S(1)} %constant_dynamic-slice_fusion.2.refs_0_), channel_id=1, source_target_pairs={{0,1},{1,0},{2,3},{3,2},{4,5},{5,4},{6,7},{7,6},{8,9},{9,8},{10,11... | collective-permute-start | bytes 442376 | tf_op jit(solution)/shard_map/ppermute | solution.py:802
  20.8 41.2 %collective-permute-start.2 = (bf16[384,1024]{1,0:T(8,128)(2,1)}, bf16[384,1024]{1,0:T(8,128)(2,1)}, u32[]{:S(2)}, u32[]{:S(2)}) collective-permute-start(bf16[384,1024]{1,0:T(8,128)(2,1)} %delayed.3), channel_id=1, source_target_pairs={{0,1},{1,0},{2,3},{3,2},{4,5},{5,4},{6,7},{7,6},{8,9},{9,8},{10,11... | collective-permute-start | bytes 2359304 | tf_op jit(solution)/shard_map/ppermute | solution.py:788
  23.7 32.2 %collective-permute-start.5 = (bf16[48,1536]{1,0:T(8,128)(2,1)S(1)}, bf16[48,1536]{1,0:T(8,128)(2,1)S(1)}, u32[]{:S(2)}, u32[]{:S(2)}) collective-permute-start(bf16[48,1536]{1,0:T(8,128)(2,1)S(1)} %constant_dynamic-slice_fusion), channel_id=1, source_target_pairs={{0,1},{1,0},{2,3},{3,2},{4,5},{5,4},{6,7},{7,6},{8,9},{9,8},{10,11... | collective-permute-start | bytes 442376 | tf_op jit(solution)/shard_map/ppermute | solution.py:802
  23.8 30.8 %collective-permute-start.8 = (s32[512,8]{0,1:T(8,128)S(1)}, s32[512,8]{0,1:T(8,128)S(1)}, u32[]{:S(2)}, u32[]{:S(2)}) collective-permute-start(s32[512,8]{0,1:T(8,128)S(1)} %copy-done.95), channel_id=1, source_target_pairs={{0,1},{1,0},{2,3},{3,2},{4,5},{5,4},{6,7},{7,6},{8,9},{9,8},{10,11... | collective-permute-start | bytes 49160 | tf_op jit(solution)/shard_map/ppermute | solution.py:753
  28.1 99.2 %all-gather.11.cloned.1.call-start = ((), (), s32[]{:S(2)}) async-start(), calls=%async_computation.4 | async-start | bytes 2924544 | tf_op jit(solution)/shard_map/all_gather | solution.py:806
  57.8 111.1 %copy-start.62 = (bf16[176,1536]{1,0:T(8,128)(2,1)}, bf16[176,1536]{1,0:T(8,128)(2,1)S(1)}, u32[]{:S(2)}) copy-start(bf16[176,1536]{1,0:T(8,128)(2,1)S(1)} %maximum_select_fusion.14) | copy-start | bytes 1622020
  58.4 110.3 %copy-start.98 = (bf16[16,40]{1,0:T(8,128)(2,1)}, bf16[16,40]{1,0:T(8,128)(2,1)S(1)}, u32[]{:S(2)}) copy-start(bf16[16,40]{1,0:T(8,128)(2,1)S(1)} %reshape.312) | copy-start | bytes 3844
  62.0 5.6 collective-permute-start.3
  69.3 25.5 %collective-permute-start.4 = (bf16[512,1024]{1,0:T(8,128)(2,1)S(1)}, bf16[512,1024]{1,0:T(8,128)(2,1)S(1)}, u32[]{:S(2)}, u32[]{:S(2)}) collective-permute-start(bf16[512,1024]{1,0:T(8,128)(2,1)S(1)} %pad_maximum_fusion.k_ref.v_ref.refs_2_), channel_id=1, source_target_pairs={{0,1},{1,0},{2,3},{3,2},{4,5},{5,4},{6,7},{7,6},{8,9},{9,8},{10,11... | collective-permute-start | bytes 3145736 | tf_op jit(solution)/shard_map/ppermute | solution.py:753
  96.6 95.1 %collective-permute-start.7 = (bf16[512,1536]{1,0:T(8,128)(2,1)}, bf16[512,1536]{1,0:T(8,128)(2,1)}, u32[]{:S(2)}, u32[]{:S(2)}) collective-permute-start(bf16[512,1536]{1,0:T(8,128)(2,1)} %delayed.4), channel_id=1, source_target_pairs={{0,1},{1,0},{2,3},{3,2},{4,5},{5,4},{6,7},{7,6},{8,9},{9,8},{10,11... | collective-permute-start | bytes 4718600 | tf_op jit(solution)/shard_map/ppermute | solution.py:753
  138.0 53.7 %collective-permute-start.6 = (bf16[512,1536]{1,0:T(8,128)(2,1)S(1)}, bf16[512,1536]{1,0:T(8,128)(2,1)S(1)}, u32[]{:S(2)}, u32[]{:S(2)}) collective-permute-start(bf16[512,1536]{1,0:T(8,128)(2,1)S(1)} %multiply_convert_fusion.refs_0_.x_ref), channel_id=1, source_target_pairs={{0,1},{1,0},{2,3},{3,2},{4,5},{5,4},{6,7},{7,6},{8,9},{9,8},{10,11... | collective-permute-start | bytes 4718600 | tf_op jit(solution)/shard_map/ppermute | solution.py:753
  169.7 21.2 %collective-permute-start.9 = (f32[20,512]{1,0:T(8,128)S(1)}, f32[20,512]{1,0:T(8,128)S(1)}, u32[]{:S(2)}, u32[]{:S(2)}) collective-permute-start(f32[20,512]{1,0:T(8,128)S(1)} %get-tuple-element.190), channel_id=1, source_target_pairs={{0,1},{1,0},{2,3},{3,2},{4,5},{5,4},{6,7},{7,6},{8,9},{9,8},{10,11... | collective-permute-start | bytes 122888 | tf_op jit(solution)/shard_map/ppermute | solution.py:753
  268.5 89.0 %all-to-all-start = ((bf16[16,80,768]{2,1,0:T(8,128)(2,1)}), bf16[16,80,768]{2,1,0:T(8,128)(2,1)}, u32[]{:S(2)}, u32[]{:S(2)}) async-start(bf16[16,80,768]{2,1,0:T(8,128)(2,1)} %bitcast.184), calls=%async_computation | async-start | bytes 3932160 | tf_op jit(solution)/shard_map/all_to_all | solution.py:1035
  279.9 286.6 %all-gather.15.cloned.1.call-start = ((), (), s32[]{:S(2)}) async-start(), calls=%async_computation.6 | async-start | bytes 8355840 | tf_op jit(solution)/shard_map/all_gather | solution.py:1034
  360.9 39.7 %collective-permute-start.10 = (bf16[512,1536]{1,0:T(8,128)(2,1)}, bf16[512,1536]{1,0:T(8,128)(2,1)}, u32[]{:S(2)}, u32[]{:S(2)}) collective-permute-start(bf16[512,1536]{1,0:T(8,128)(2,1)} %get-tuple-element.73), channel_id=1, source_target_pairs={{0,1},{1,0},{2,3},{3,2},{4,5},{5,4},{6,7},{7,6},{8,9},{9,8},{10,11... | collective-permute-start | bytes 4718600 | tf_op jit(solution)/shard_map/ppermute | solution.py:768
  361.0 37.8 %collective-permute-start.11 = (f32[20,512]{1,0:T(8,128)S(1)}, f32[20,512]{1,0:T(8,128)S(1)}, u32[]{:S(2)}, u32[]{:S(2)}) collective-permute-start(f32[20,512]{1,0:T(8,128)S(1)} %get-tuple-element.187), channel_id=1, source_target_pairs={{0,1},{1,0},{2,3},{3,2},{4,5},{5,4},{6,7},{7,6},{8,9},{9,8},{10,11... | collective-permute-start | bytes 122888 | tf_op jit(solution)/shard_map/ppermute | solution.py:753
  363.1 71.3 %all-to-all-start.1 = ((bf16[16,80,768]{2,1,0:T(8,128)(2,1)}), bf16[16,80,768]{2,1,0:T(8,128)(2,1)}, u32[]{:S(2)}, u32[]{:S(2)}) async-start(bf16[16,80,768]{2,1,0:T(8,128)(2,1)} %bitcast.31), calls=%async_computation.1 | async-start | bytes 3932160 | tf_op jit(solution)/shard_map/all_to_all | solution.py:1035
  369.1 206.7 %all-gather.13.cloned.1.call-start = ((), (), s32[]{:S(2)}) async-start(), calls=%async_computation.5 | async-start | bytes 8355840 | tf_op jit(solution)/shard_map/all_gather | solution.py:1082
  446.0 46.1 %collective-permute-start.14 = (bf16[512,512]{1,0:T(8,128)(2,1)S(1)}, bf16[512,512]{1,0:T(8,128)(2,1)S(1)}, u32[]{:S(2)}, u32[]{:S(2)}) collective-permute-start(bf16[512,512]{1,0:T(8,128)(2,1)S(1)} %pad_maximum_fusion.2), channel_id=1, source_target_pairs={{0,1},{1,0},{2,3},{3,2},{4,5},{5,4},{6,7},{7,6},{8,9},{9,8},{10,11... | collective-permute-start | bytes 1572872 | tf_op jit(solution)/shard_map/ppermute | solution.py:768
  480.9 17.9 %collective-permute-start.12 = (bf16[512,512]{1,0:T(8,128)(2,1)S(1)}, bf16[512,512]{1,0:T(8,128)(2,1)S(1)}, u32[]{:S(2)}, u32[]{:S(2)}) collective-permute-start(bf16[512,512]{1,0:T(8,128)(2,1)S(1)} %pad_maximum_fusion.1), channel_id=1, source_target_pairs={{0,1},{1,0},{2,3},{3,2},{4,5},{5,4},{6,7},{7,6},{8,9},{9,8},{10,11... | collective-permute-start | bytes 1572872 | tf_op jit(solution)/shard_map/ppermute | solution.py:768
  501.6 35.7 %all-to-all-start.2 = ((bf16[32,8,768]{2,1,0:T(8,128)(2,1)}), bf16[32,8,768]{2,1,0:T(8,128)(2,1)}, u32[]{:S(2)}, u32[]{:S(2)}) async-start(bf16[32,8,768]{2,1,0:T(8,128)(2,1)} %bitcast.169), calls=%async_computation.2 | async-start | bytes 786432 | tf_op jit(solution)/shard_map/all_to_all | solution.py:1130
  517.4 45.3 %collective-permute-start.13 = (bf16[512,1536]{1,0:T(8,128)(2,1)}, bf16[512,1536]{1,0:T(8,128)(2,1)}, u32[]{:S(2)}, u32[]{:S(2)}) collective-permute-start(bf16[512,1536]{1,0:T(8,128)(2,1)} %delayed.5), channel_id=1, source_target_pairs={{0,1},{1,0},{2,3},{3,2},{4,5},{5,4},{6,7},{7,6},{8,9},{9,8},{10,11... | collective-permute-start | bytes 4718600 | tf_op jit(solution)/shard_map/ppermute | solution.py:761
  (108 other events, 947.4 us)
Sparse Core Ops, SparseCore 0:
  28.2 43.8 all-gather.8
  75.0 42.5 all-gather.10
  361.0 104.3 all-gather.14
  467.5 75.8 all-gather.12

commit v6 on v5

--- a/solution.py
+++ b/solution.py
@@ -331,7 +331,7 @@
             jax.ShapeDtypeStruct((pairs, count, narrow), F32),
         ],
         compiler_params=pltpu.CompilerParams(
-            vmem_limit_bytes=40 * 1024 * 1024, dimension_semantics=("arbitrary",)
+            vmem_limit_bytes=60 * 1024 * 1024, dimension_semantics=("arbitrary",)
         ),
         cost_estimate=pl.CostEstimate(flops=40_000_000_000, bytes_accessed=8_000_000, transcendentals=10_000_000),
         name="attention",
@@ -366,7 +366,7 @@
         + [jax.ShapeDtypeStruct((count, pairs * narrow), BF16)] * 2
         + [jax.ShapeDtypeStruct((far.shape[0], pairs * narrow), BF16)] * 2,
         compiler_params=pltpu.CompilerParams(
-            vmem_limit_bytes=40 * 1024 * 1024, dimension_semantics=("arbitrary",)
+            vmem_limit_bytes=60 * 1024 * 1024, dimension_semantics=("arbitrary",)
         ),
         cost_estimate=pl.CostEstimate(
             flops=17_000_000_000 * pairs, bytes_accessed=3_000_000 * pairs, transcendentals=0
@@ -377,6 +377,7 @@
 
 def expert_kernel(
     chosen_ref,
+    most_ref,
     x_ref,
     x_far,
     g_ref,
@@ -395,6 +396,7 @@
     cap,
     flush,
     carried,
+    first,
 ):
     held = refs[:4] if carried else ()
     (
@@ -423,6 +425,8 @@
     @pl.when(e == 0)
     def _():
         b1_s[...] = jnp.zeros_like(b1_s)
+        o_s[...] = jnp.zeros_like(o_s)
+        dx_s[...] = jnp.zeros_like(dx_s)
         if carried:
             for n, acc in enumerate((accr, accd)):
                 acc[0:rows_block, :] = held[2 * n][...].astype(F32)
@@ -432,62 +436,78 @@
             accd[...] = jnp.zeros_like(accd)
 
     at = pl.multiple_of(slot * cap, 16)
-    for b in range(blocks):
-        rows_ref, g_rows_ref = (x_ref, g_ref) if b == 0 else (x_far, g_far)
-        here = pl.ds(max(b - 1, 0) * rows_block, rows_block)
-        there = pl.ds(b * cap, cap)
-        places = lax.broadcasted_iota(jnp.int32, (cap, rows_block), 0)
-        hit = places == pos_ref[0, b : b + 1, :]
-        hot = hit.astype(F32).astype(BF16)
-        hot_s[b, pl.ds(at, cap), :] = hot
-        x_s[there, :] = product(hot, rows_ref[here, :]).astype(BF16)
-        g_s[there, :] = product(hot, g_rows_ref[here, :]).astype(BF16)
-        gate_s[there, :] = jnp.sum(
-            jnp.where(hit, gate_ref[0, b : b + 1, :], 0.0), axis=1, keepdims=True
-        )
     b1_s[0:RANK, 0:FF] = b1_ref[0, 0, 0]
     b1_s[RANK : 2 * RANK, FF : 2 * FF] = b1_ref[0, 0, 1]
-
-    x = x_s[...]
-    gate_col = gate_s[...]
-    rank_in = product_back(a1_ref[0, 0], x).astype(BF16)
-    pre = product(x, w1_ref[0])
-    gate_pre = pre[:, :FF]
-    up_pre = pre[:, FF:]
-    sig = 1.0 / (1.0 + jnp.exp(-gate_pre))
-    act = gate_pre * sig
-    hidden = (act * up_pre).astype(BF16)
-    rank_down = product_back(a2_ref[0, 0], hidden).astype(BF16)
-    out = product(hidden, w2_ref[0]).astype(BF16).astype(F32)
-    g = g_s[...].astype(F32)
-    d_gate_col = jnp.sum(g * out, axis=1, keepdims=True)
-    out = (gate_col * out).astype(BF16)
-    d_exp = (gate_col * g).astype(BF16)
-    d_rank_down = product_back(b2_ref[0, 0], d_exp).astype(BF16)
-    d_hidden = product_back(d_exp, w2_ref[0])
-    dgu_s[:, :FF] = (d_hidden * up_pre * sig * (1.0 + gate_pre * (1.0 - sig))).astype(BF16)
-    dgu_s[:, FF:] = (d_hidden * act).astype(BF16)
-    dgu = dgu_s[...]
-    d_rank_in = product_back(b1_s[...], dgu).astype(BF16)
-    dx = product_back(dgu, w1_ref[0]).astype(BF16)
-    for b in range(blocks):
-        o_s[b, pl.ds(at, cap), :] = out[b * cap : (b + 1) * cap]
-        dx_s[b, pl.ds(at, cap), :] = dx[b * cap : (b + 1) * cap]
-        places = lax.broadcasted_iota(jnp.int32, (cap, rows_block), 0)
-        hit = places == pos_ref[0, b : b + 1, :]
-        dg_out[0, b : b + 1, :] = jnp.sum(
-            jnp.where(hit, d_gate_col[b * cap : (b + 1) * cap], 0.0), axis=0, keepdims=True
-        )
-
-    grad_a1 = product(d_rank_in, x)
-    grad_b1 = product(rank_in, dgu)
-    grad_a2 = product(d_rank_down, hidden)
-    grad_b2 = product(rank_down, d_exp)
-    last = jnp.concatenate([grad_b1[:RANK, :FF], grad_b1[RANK:, FF:], grad_a2], axis=1)
-    for n, piece in enumerate((grad_a1[:RANK], grad_a1[RANK:], grad_b2, last)):
-        for half in range(halves):
-            rows = slice((n * halves + half) * RANK, (n * halves + half + 1) * RANK)
-            grad_out[0, rows, :] = piece[:, half * UNIT : (half + 1) * UNIT].astype(BF16)
+    most = most_ref[e + first]
+
+    def run(used):
+        for b in range(blocks):
+            rows_ref, g_rows_ref = (x_ref, g_ref) if b == 0 else (x_far, g_far)
+            here = pl.ds(max(b - 1, 0) * rows_block, rows_block)
+            there = pl.ds(b * used, used)
+            places = lax.broadcasted_iota(jnp.int32, (used, rows_block), 0)
+            hit = places == pos_ref[0, b : b + 1, :]
+            hot = hit.astype(F32).astype(BF16)
+            hot_s[b, pl.ds(at, used), :] = hot
+            if used < cap:
+                hot_s[b, pl.ds(at + used, cap - used), :] = jnp.zeros((cap - used, rows_block), BF16)
+            x_s[there, :] = product(hot, rows_ref[here, :]).astype(BF16)
+            g_s[there, :] = product(hot, g_rows_ref[here, :]).astype(BF16)
+            gate_s[there, :] = jnp.sum(
+                jnp.where(hit, gate_ref[0, b : b + 1, :], 0.0), axis=1, keepdims=True
+            )
+
+        rows = slice(0, blocks * used)
+        x = x_s[rows]
+        gate_col = gate_s[rows]
+        rank_in = product_back(a1_ref[0, 0], x).astype(BF16)
+        pre = product(x, w1_ref[0])
+        gate_pre = pre[:, :FF]
+        up_pre = pre[:, FF:]
+        sig = 1.0 / (1.0 + jnp.exp(-gate_pre))
+        act = gate_pre * sig
+        hidden = (act * up_pre).astype(BF16)
+        rank_down = product_back(a2_ref[0, 0], hidden).astype(BF16)
+        out = product(hidden, w2_ref[0]).astype(BF16).astype(F32)
+        g = g_s[rows].astype(F32)
+        d_gate_col = jnp.sum(g * out, axis=1, keepdims=True)
+        out = (gate_col * out).astype(BF16)
+        d_exp = (gate_col * g).astype(BF16)
+        d_rank_down = product_back(b2_ref[0, 0], d_exp).astype(BF16)
+        d_hidden = product_back(d_exp, w2_ref[0])
+        dgu_s[rows, :FF] = (d_hidden * up_pre * sig * (1.0 + gate_pre * (1.0 - sig))).astype(BF16)
+        dgu_s[rows, FF:] = (d_hidden * act).astype(BF16)
+        dgu = dgu_s[rows]
+        d_rank_in = product_back(b1_s[...], dgu).astype(BF16)
+        dx = product_back(dgu, w1_ref[0]).astype(BF16)
+        for b in range(blocks):
+            o_s[b, pl.ds(at, used), :] = out[b * used : (b + 1) * used]
+            dx_s[b, pl.ds(at, used), :] = dx[b * used : (b + 1) * used]
+            places = lax.broadcasted_iota(jnp.int32, (used, rows_block), 0)
+            hit = places == pos_ref[0, b : b + 1, :]
+            dg_out[0, b : b + 1, :] = jnp.sum(
+                jnp.where(hit, d_gate_col[b * used : (b + 1) * used], 0.0), axis=0, keepdims=True
+            )
+
+        grad_a1 = product(d_rank_in, x)
+        grad_b1 = product(rank_in, dgu)
+        grad_a2 = product(d_rank_down, hidden)
+        grad_b2 = product(rank_down, d_exp)
+        last = jnp.concatenate([grad_b1[:RANK, :FF], grad_b1[RANK:, FF:], grad_a2], axis=1)
+        for n, piece in enumerate((grad_a1[:RANK], grad_a1[RANK:], grad_b2, last)):
+            for half in range(halves):
+                rows = slice((n * halves + half) * RANK, (n * halves + half + 1) * RANK)
+                grad_out[0, rows, :] = piece[:, half * UNIT : (half + 1) * UNIT].astype(BF16)
+
+
+    sizes = sorted({min(cap, size) for size in (96, 112, cap)})
+    for n, size in enumerate(sizes):
+        fits = most <= size
+        if n + 1 == len(sizes):
+            fits = most > sizes[n - 1] if n else most >= 0
+        elif n:
+            fits = jnp.logical_and(fits, most > sizes[n - 1])
+        pl.when(fits)(functools.partial(run, size))
 
     @pl.when(slot == flush - 1)
     def _():
@@ -504,17 +524,17 @@
         d_far[...] = accd[rows_block:, :].astype(BF16)
 
 
-def run_experts(chosen, x, x_far, g, g_far, pos, gate, w1, w2, a1, b1, a2, b2, held, cap, first, count):
+def run_experts(chosen, most, x, x_far, g, g_far, pos, gate, w1, w2, a1, b1, a2, b2, held, cap, first, count):
     _, blocks, rows_block = pos.shape
     width = x.shape[1]
     tokens = blocks * rows_block
     rows = blocks * cap
     flush = FLUSH if count % FLUSH == 0 else 1
     record = 4 * RANK * width // UNIT
-    lead = lambda e, c: (e, 0, 0)
-    shifted = lambda e, c: (e + first, 0, 0)
-    near = pl.BlockSpec((rows_block, width), lambda e, c: (0, 0), pipeline_mode=pl.Buffered(1))
-    away = pl.BlockSpec((tokens - rows_block, width), lambda e, c: (0, 0), pipeline_mode=pl.Buffered(1))
+    lead = lambda e, c, m: (e, 0, 0)
+    shifted = lambda e, c, m: (e + first, 0, 0)
+    near = pl.BlockSpec((rows_block, width), lambda e, c, m: (0, 0), pipeline_mode=pl.Buffered(1))
+    away = pl.BlockSpec((tokens - rows_block, width), lambda e, c, m: (0, 0), pipeline_mode=pl.Buffered(1))
     near_shape = jax.ShapeDtypeStruct((rows_block, width), BF16)
     away_shape = jax.ShapeDtypeStruct((tokens - rows_block, width), BF16)
     return pl.pallas_call(
@@ -525,9 +545,10 @@
             cap=cap,
             flush=flush,
             carried=bool(held),
+            first=first,
         ),
         grid_spec=pltpu.PrefetchScalarGridSpec(
-            num_scalar_prefetch=1,
+            num_scalar_prefetch=2,
             grid=(count,),
             in_specs=[
                 near,
@@ -538,10 +559,10 @@
                 pl.BlockSpec((1, blocks, rows_block), shifted),
                 pl.BlockSpec((1, width, 2 * FF), lead),
                 pl.BlockSpec((1, FF, width), lead),
-                pl.BlockSpec((1, 1, 2 * RANK, width), lambda e, c: (c[0], e + first, 0, 0)),
-                pl.BlockSpec((1, 1, 2, RANK, FF), lambda e, c: (c[0], e + first, 0, 0, 0)),
-                pl.BlockSpec((1, 1, RANK, FF), lambda e, c: (c[0], e + first, 0, 0)),
-                pl.BlockSpec((1, 1, RANK, width), lambda e, c: (c[0], e + first, 0, 0)),
+                pl.BlockSpec((1, 1, 2 * RANK, width), lambda e, c, m: (c[0], e + first, 0, 0)),
+                pl.BlockSpec((1, 1, 2, RANK, FF), lambda e, c, m: (c[0], e + first, 0, 0, 0)),
+                pl.BlockSpec((1, 1, RANK, FF), lambda e, c, m: (c[0], e + first, 0, 0)),
+                pl.BlockSpec((1, 1, RANK, width), lambda e, c, m: (c[0], e + first, 0, 0)),
             ]
             + ([near, away, near, away] if held else []),
             out_specs=[
@@ -582,7 +603,7 @@
             transcendentals=rows * FF * count,
         ),
         name="experts",
-    )(chosen, x, x_far, g, g_far, pos, gate, w1, w2, a1, b1, a2, b2, *held)
+    )(chosen, most, x, x_far, g, g_far, pos, gate, w1, w2, a1, b1, a2, b2, *held)
 
 
 def fold_kernel(chosen_ref, w1_ref, w2_ref, a1_ref, b1_ref, a2_ref, b2_ref, *refs):
@@ -621,7 +642,7 @@
         ],
         input_output_aliases={7 + n: n for n in range(len(held))},
         compiler_params=pltpu.CompilerParams(
-            vmem_limit_bytes=40 * 1024 * 1024, dimension_semantics=("arbitrary",)
+            vmem_limit_bytes=60 * 1024 * 1024, dimension_semantics=("arbitrary",)
         ),
         cost_estimate=pl.CostEstimate(
             flops=3_000_000_000 * count, bytes_accessed=12_000_000 * count, transcendentals=0
@@ -654,7 +675,7 @@
             scratch_shapes=[pltpu.VMEM(shape, F32)],
         ),
         out_shape=jax.ShapeDtypeStruct(shape, BF16),
-        compiler_params=pltpu.CompilerParams(vmem_limit_bytes=32 * 1024 * 1024),
+        compiler_params=pltpu.CompilerParams(vmem_limit_bytes=60 * 1024 * 1024),
         cost_estimate=pl.CostEstimate(flops=0, bytes_accessed=5_000_000, transcendentals=0),
         name="totals",
     )(ids, rows, *after)
@@ -999,6 +1020,7 @@
     ranks = jnp.einsum("ts,gse->get", before, hits.astype(BF16), preferred_element_type=F32)
     places = jnp.where(hits.transpose(0, 2, 1), ranks.astype(jnp.int32), -1).transpose(1, 0, 2)
 
+    most = jnp.max(places, axis=(1, 2)) + 1
     rows_far = from_others(normed_ffn)
     gates_t = gates.T
     if groups == 2:
@@ -1015,6 +1037,7 @@
     for n in range(calls):
         *sums, terms, grads = run_experts(
             adapter_ids,
+            most,
             normed_ffn,
             rows_far,
             cotangent,
@@ -1073,13 +1096,9 @@
             logs,
             n * pairs,
             pairs,
-            (last,) if n else (),
         )
         d_kv = to_owners(jnp.concatenate(d_kv[:2], axis=1), jnp.concatenate(d_kv[2:], axis=1)).astype(BF16)
         parts.append((d_q, d_kv[:, : kv_width // 2], d_kv[:, kv_width // 2 :]))
-        if n == 0:
-            last = totals(ids_all, swapped, adapters, after=(d_q,))
-            spread.append(lax.all_gather(last, "rep", axis=0))
     mixture = owners_terms(result_near, delayed(result_far, (parts[1][1],)))
     d_queries, d_keys, d_values = [jnp.concatenate(pair, axis=1) for pair in zip(*parts)]
     d_keyvals = jnp.concatenate([d_keys, d_values], axis=1)
@@ -1107,6 +1126,8 @@
         axis=0,
     )
 
+    last = totals(ids_all, swapped, adapters, after=(parts[0][0],))
+    spread.append(lax.all_gather(last, "rep", axis=0))
     expert_grads = ()
     for n in range(calls):
         expert_grads = unpack_grads(spread[n], experts_dev, n * each, tuple(expert_grads), width)
@@ -1130,7 +1151,8 @@
     dense = lax.all_to_all(dense, ("rep", "grp"), split_axis=0, concat_axis=0, tiled=True)
     owner_hot = (jnp.arange(adapters, dtype=jnp.int32)[:, None] == jnp.repeat(ids_all, groups)[None, :])
     dense = jnp.sum(jnp.where(owner_hot[:, :, None, None], dense.astype(F32)[None], 0.0), axis=1).astype(BF16)
-    dense = lax.all_gather(dense, "rep", axis=0).swapaxes(0, 1).reshape(adapters, -1, part).astype(F32)
+    dense = jnp.broadcast_to(dense[None], (reps,) + dense.shape)
+    dense = lax.all_to_all(dense, "rep", split_axis=0, concat_axis=0, tiled=True).swapaxes(0, 1).reshape(adapters, -1, part).astype(F32)
     wide = dense[:, high:]
     owned = [
         dense[:, : 3 * RANK],

time: 604 us -> 610 us (level)
  blocking collectives: 20.9 us -> 0 us
  local copies, waits for them, and re-layouts: 53.2 us -> 35.1 us
  starting transfers between devices: 76 us -> 93.6 us
  matrix products: 50.7 us -> 64 us
  waiting for transfers between devices: 45.8 us -> 55.2 us
    unnamed x231 -> x155, local copies, waits for them, and re-layouts: 37.8 us -> 15.8 us
    all_gather x1 -> x0, blocking collectives: 20.9 us -> none  [local(): lax.all_gather(dense, 'rep', axis=0).swapaxes(0, 1)]
    pallas_call x2, Pallas kernels: 153 us -> 163 us  [run_experts(): pl.pallas_call(functools.partial(expert_kernel, blocks=blocks, rows_block...]
    dot_general x13, matrix products: 18.5 us -> 25.2 us  [product_back(): lax.dot_general(left, right, (((1,), (1,)), ((), ())), preferred_element_...]
    all_to_all x1, waiting for transfers between devices: 4.3 us -> 10.8 us  [local(): lax.all_to_all(dense, ('rep', 'grp'), split_axis=0, concat_axis=0, tiled=...]
  transfers between devices with their start and end apart: 22 -> 23, of which waited for: 5 -> 7; matrix products, arithmetic and copies ran while one was open for 14% -> 17% of each run, Pallas kernels for 38% -> 38%
where the time goes in v6:
time: 610 us; the launch traced here: 601 us
  Pallas kernels  314 us (51%)
  starting transfers between devices  93.6 us (15%)
  matrix products  64 us (10%)
  waiting for transfers between devices  55.2 us (9%)
  local copies, waits for them, and re-layouts  35.1 us (6%)
  other arithmetic  23.1 us (4%)
  between operations  16.1 us (3%)
    pallas_call x2, Pallas kernels, run_experts(): pl.pallas_call(functools.partial(expert_kernel, blocks=blocks, rows_block...  163 us
    pallas_call x4, Pallas kernels, fold_adapters(): pl.pallas_call(fold_kernel, grid_spec=pltpu.PrefetchScalarGridSpec(num_sc...  75.8 us
    ppermute x7, waiting for transfers between devices, from_others(): return lax.ppermute(piece, 'grp', swap_pairs(2))  33.8 us
    dot_general x15, matrix products, product(): return jnp.dot(left, right, preferred_element_type=F32)  33.1 us
    pallas_call x2, Pallas kernels, run_attention_back(): pl.pallas_call(functools.partial(attend_back_kernel, here=here, segs=segs...  32.6 us
    dot_general x13, matrix products, product_back(): lax.dot_general(left, right, (((1,), (1,)), ((), ())), preferred_element_...  25.2 us
    ppermute x7, starting transfers between devices, from_others(): return lax.ppermute(piece, 'grp', swap_pairs(2))  24.7 us
    ppermute x3, starting transfers between devices, to_owners(): lax.ppermute(far, 'grp', swap_pairs(2)).astype(F32)  22.4 us
  transfers between devices with their start and end apart: 23, of which 7 were waited for; matrix products, arithmetic and copies ran while one was open for 17% of the time, Pallas kernels for 38%

profile of v6, /device:TPU:0, one launch (start us, length us, event | category | flops | bytes accessed | tf_op | source)
XLA Modules:
  0.0 601.2 jit_solution(10226133449187798944)
XLA Ops:
  30.4 18.9 %fold.6 = (bf16[10,1536,1024]{2,1,0:T(8,128)(2,1)}, bf16[10,512,1536]{2,1,0:T(8,128)(2,1)}) custom-call(s32[1]{0:T(128)} %copy.224.chosen_ref, bf16[20,1536,1024]{2,1,0:T(8,128)(2,1)} %w1_ref.7, bf16[20,512,1536]{2,1,0:T(8,128)(2,1)} %w2_ref.7, bf16[4,20,32,1536]{3,2,1,0:T(8,128)(2,1)} %bitcast.162, bf16[4,20,2,16,512]{4,3,2,1,0:T(8,128)(2,1)} %b1_ref.11, ...), custom_call_target="tpu_custom_call" | custom-call | flops 15000000512 | bytes 60000000 | tf_op jit(solution)/shard_map/fold/pallas_call | solution.py:623
  67.4 19.1 %fold.7 = (bf16[10,1536,1024]{2,1,0:T(8,128)(2,1)}, bf16[10,512,1536]{2,1,0:T(8,128)(2,1)}) custom-call(s32[1]{0:T(128)} %copy.224.chosen_ref, bf16[20,1536,1024]{2,1,0:T(8,128)(2,1)} %w1_ref.7, bf16[20,512,1536]{2,1,0:T(8,128)(2,1)} %w2_ref.7, bf16[4,20,32,1536]{3,2,1,0:T(8,128)(2,1)} %bitcast.163, ...), custom_call_target="tpu_custom_call", output_to_operand_aliasing={{0}: (7, {}), {1}: (8, {})} | custom-call | flops 15000000512 | bytes 60000000 | tf_op jit(solution)/shard_map/fold/pallas_call | solution.py:623
  86.5 4.7 collective-permute-done.4.k_far.v_far.refs_0_
  102.2 17.7 %attention.1 = (bf16[512,1536]{1,0:T(8,128)(2,1)}, f32[4,512,128]{2,1,0:T(8,128)}) custom-call(s32[64]{0:T(128)} %reshape.301.list_ref, s32[4]{0:T(128)} %and_select_fusion.steps_ref, bf16[512,1536]{1,0:T(8,128)(2,1)} %fusion.28.q_ref, bf16[512,1024]{1,0:T(8,128)(2,1)} %copy-done.24, bf16[512,1024]{1,0:T(8,128)(2,1)} %copy-done.24, ...), custom_call_target="tpu_custom_call" | custom-call | flops 40000000000 | bytes 8000000 | tf_op jit(solution)/shard_map/attention/pallas_call | solution.py:317
  127.5 5.6 multiply_reduce_fusion.1
  135.0 13.8 %collective-permute-start.7 = (bf16[512,1536]{1,0:T(8,128)(2,1)S(1)}, bf16[512,1536]{1,0:T(8,128)(2,1)}, u32[]{:S(2)}, u32[]{:S(2)}) collective-permute-start(bf16[512,1536]{1,0:T(8,128)(2,1)S(1)} %multiply_convert_fusion.refs_0_.x_ref), channel_id=1, source_target_pairs={{0,1},{1,0},{2,3},{3,2},{4,5},{5,4},{6,7},{7,6},{8,9},{9,8},{10,11... | collective-permute-start | bytes 4718600 | tf_op jit(solution)/shard_map/ppermute | solution.py:774
  148.8 18.9 %fold.4 = (bf16[10,1536,1024]{2,1,0:T(8,128)(2,1)}, bf16[10,512,1536]{2,1,0:T(8,128)(2,1)}) custom-call(s32[1]{0:T(128)} %copy.224.chosen_ref, bf16[20,1536,1024]{2,1,0:T(8,128)(2,1)} %w1_ref.7, bf16[20,512,1536]{2,1,0:T(8,128)(2,1)} %w2_ref.7, bf16[4,20,32,1536]{3,2,1,0:T(8,128)(2,1)} %bitcast.164, bf16[4,20,2,16,512]{4,3,2,1,0:T(8,128)(2,1)} %b1_ref.11, ...), custom_call_target="tpu_custom_call" | custom-call | flops 15000000512 | bytes 60000000 | tf_op jit(solution)/shard_map/fold/pallas_call | solution.py:623
  171.5 18.9 %fold.5 = (bf16[10,1536,1024]{2,1,0:T(8,128)(2,1)}, bf16[10,512,1536]{2,1,0:T(8,128)(2,1)}) custom-call(s32[1]{0:T(128)} %copy.224.chosen_ref, bf16[20,1536,1024]{2,1,0:T(8,128)(2,1)} %w1_ref.7, bf16[20,512,1536]{2,1,0:T(8,128)(2,1)} %w2_ref.7, bf16[4,20,32,1536]{3,2,1,0:T(8,128)(2,1)} %bitcast.165, ...), custom_call_target="tpu_custom_call", output_to_operand_aliasing={{0}: (7, {}), {1}: (8, {})} | custom-call | flops 15000000512 | bytes 60000000 | tf_op jit(solution)/shard_map/fold/pallas_call | solution.py:623
  191.8 73.6 %experts.2 = (bf16[512,1536]{1,0:T(8,128)(2,1)}, bf16[512,1536]{1,0:T(8,128)(2,1)}, bf16[512,1536]{1,0:T(8,128)(2,1)}, bf16[512,1536]{1,0:T(8,128)(2,1)}, f32[10...) custom-call(s32[1]{0:T(128)} %copy.224.chosen_ref, s32[20]{0:T(128)} %broadcast_add_fusion.most_ref, ...), custom_call_target="tpu_custom_call" | custom-call | flops 80000000000 | bytes 50000000 | tf_op jit(solution)/shard_map/experts/pallas_call | solution.py:540
  265.4 14.3 %all-to-all-start = ((bf16[16,80,768]{2,1,0:T(8,128)(2,1)}), bf16[16,80,768]{2,1,0:T(8,128)(2,1)}, u32[]{:S(2)}, u32[]{:S(2)}) async-start(bf16[16,80,768]{2,1,0:T(8,128)(2,1)} %bitcast.181), calls=%async_computation | async-start | bytes 3932160 | tf_op jit(solution)/shard_map/all_to_all | solution.py:1058
  279.9 89.0 %experts.3 = (bf16[512,1536]{1,0:T(8,128)(2,1)}, bf16[512,1536]{1,0:T(8,128)(2,1)}, bf16[512,1536]{1,0:T(8,128)(2,1)}, bf16[512,1536]{1,0:T(8,128)(2,1)}, f32[10...) custom-call(s32[1]{0:T(128)} %copy.224.chosen_ref, s32[20]{0:T(128)} %broadcast_add_fusion.most_ref, ...), custom_call_target="tpu_custom_call" | custom-call | flops 80000000000 | bytes 50000000 | tf_op jit(solution)/shard_map/experts/pallas_call | solution.py:540
  375.6 6.2 %all-to-all-start.3 = ((bf16[16,80,768]{2,1,0:T(8,128)(2,1)}), bf16[16,80,768]{2,1,0:T(8,128)(2,1)}, u32[]{:S(2)}, u32[]{:S(2)}) async-start(bf16[16,80,768]{2,1,0:T(8,128)(2,1)} %bitcast.180), calls=%async_computation.3 | async-start | bytes 3932160 | tf_op jit(solution)/shard_map/all_to_all | solution.py:1058
  381.8 29.1 %collective-permute-done.11 = f32[20,512]{1,0:T(8,128)S(1)} collective-permute-done((f32[20,512]{1,0:T(8,128)S(1)}, f32[20,512]{1,0:T(8,128)S(1)}, u32[]{:S(2)}, u32[]{:S(2)}) %collective-permute-start.11) | collective-permute-done | bytes 40992 | tf_op jit(solution)/shard_map/ppermute | solution.py:774
  424.6 16.2 %attention_back.3 = (bf16[512,768]{1,0:T(8,128)(2,1)}, bf16[512,256]{1,0:T(8,128)(2,1)}, bf16[512,256]{1,0:T(8,128)(2,1)}, bf16[512,256]{1,0:T(8,128)(2,1)}, bf16[512,256]{1,0:T(8,128)(2,1)}) custom-call(s32[64]{0:T(128)} %reshape.301.list_ref, s32[4]{0:T(128)} %and_select_fusion.steps_ref, bf16[512,1536]{1,0:T(8,128)(2,1)} %fusion.28.q_ref, ...), custom_call_target="tpu_custom_call" | custom-call | flops 33999998976 | bytes 6000000 | tf_op jit(solution)/shard_map/attention_back/pallas_call | solution.py:351
  452.3 11.0 %collective-permute-start.14 = (bf16[512,512]{1,0:T(8,128)(2,1)}, bf16[512,512]{1,0:T(8,128)(2,1)S(1)}, u32[]{:S(2)}, u32[]{:S(2)}) collective-permute-start(bf16[512,512]{1,0:T(8,128)(2,1)} %pad_maximum_fusion.2), channel_id=1, source_target_pairs={{0,1},{1,0},{2,3},{3,2},{4,5},{5,4},{6,7},{7,6},{8,9},{9,8},{10,11... | collective-permute-start | bytes 1572872 | tf_op jit(solution)/shard_map/ppermute | solution.py:789
  463.4 16.4 %attention_back.2 = (bf16[512,768]{1,0:T(8,128)(2,1)}, bf16[512,256]{1,0:T(8,128)(2,1)}, bf16[512,256]{1,0:T(8,128)(2,1)}, bf16[512,256]{1,0:T(8,128)(2,1)}, bf16[512,256]{1,0:T(8,128)(2,1)}) custom-call(s32[64]{0:T(128)} %reshape.301.list_ref, s32[4]{0:T(128)} %and_select_fusion.steps_ref, bf16[512,1536]{1,0:T(8,128)(2,1)} %fusion.28.q_ref, ...), custom_call_target="tpu_custom_call" | custom-call | flops 33999998976 | bytes 6000000 | tf_op jit(solution)/shard_map/attention_back/pallas_call | solution.py:351
  481.0 10.8 %collective-permute-start.12 = (bf16[512,512]{1,0:T(8,128)(2,1)S(1)}, bf16[512,512]{1,0:T(8,128)(2,1)S(1)}, u32[]{:S(2)}, u32[]{:S(2)}) collective-permute-start(bf16[512,512]{1,0:T(8,128)(2,1)S(1)} %pad_maximum_fusion.1), channel_id=1, source_target_pairs={{0,1},{1,0},{2,3},{3,2},{4,5},{5,4},{6,7},{7,6},{8,9},{9,8},{10,11... | collective-permute-start | bytes 1572872 | tf_op jit(solution)/shard_map/ppermute | solution.py:789
  498.8 4.9 collective-permute-done.12
  506.1 17.1 %all-to-all-start.1 = ((bf16[32,8,768]{2,1,0:T(8,128)(2,1)}), bf16[32,8,768]{2,1,0:T(8,128)(2,1)}, u32[]{:S(2)}, u32[]{:S(2)}) async-start(bf16[32,8,768]{2,1,0:T(8,128)(2,1)} %bitcast.36.refs_0_), calls=%async_computation.1 | async-start | bytes 786432 | tf_op jit(solution)/shard_map/all_to_all | solution.py:1151
  534.9 10.8 %all-to-all-done.1 = bf16[32,8,768]{2,1,0:T(8,128)(2,1)} async-done(((bf16[32,8,768]{2,1,0:T(8,128)(2,1)}), bf16[32,8,768]{2,1,0:T(8,128)(2,1)}, u32[]{:S(2)}, u32[]{:S(2)}) %all-to-all-start.1) | async-done | bytes 393248 | tf_op jit(solution)/shard_map/all_to_all | solution.py:1151
  548.0 4.5 all-to-all-start.2
  552.6 9.8 %fusion.15 = (f32[512]{0:T(512)S(1)}, f32[512,1536]{1,0:T(8,128)S(1)}) fusion(bf16[512,1536]{1,0:T(8,128)(2,1)} %param.25, f32[512]{0:T(512)S(1)} %copy-done.67, f32[1536]{0:T(1024)S(1)} %copy-done.65, f32[512,1536]{1,0:T(8,128)} %fusion.53, f32[512,1536]{1,0:T(8,128)} %fusion.21, bf16[512,1536]{1,0:T(8,128)(2,1)} %copy-done.21, ...), kind=kOutput, calls=%fused_computation.23 | convolution fusion | flops 2442657280 | bytes 17311744 | tf_op jit(solution)/shard_map/dot_general | solution.py:30
  578.9 6.2 %unpack.2 = (f32[4,20,32,1536]{3,2,1,0:T(8,128)}, f32[4,20,2,16,512]{4,3,2,1,0:T(8,128)}, f32[4,20,16,512]{3,2,1,0:T(8,128)}, f32[4,20,16,1536]{3,2,1,0:T(8,128)}) custom-call(bf16[16,4,80,768]{3,2,1,0:T(8,128)(2,1)S(1)} %bitcast.161), custom_call_target="tpu_custom_call" | custom-call | bytes 30000000 | tf_op jit(solution)/shard_map/unpack/pallas_call | solution.py:741
  588.3 6.2 %unpack.3 = (f32[4,20,32,1536]{3,2,1,0:T(8,128)}, f32[4,20,2,16,512]{4,3,2,1,0:T(8,128)}, f32[4,20,16,512]{3,2,1,0:T(8,128)}, f32[4,20,16,1536]{3,2,1,0:T(8,128)}) custom-call(bf16[16,4,80,768]{3,2,1,0:T(8,128)(2,1)S(1)} %bitcast.160, ...), custom_call_target="tpu_custom_call", output_to_operand_aliasing={{0}: (1, {}), {1}: (2, {}), {2}: (3, {}), {3}: (4, {})} | custom-call | bytes 30000000 | tf_op jit(solution)/shard_map/unpack/pallas_call | solution.py:741
  (347 shorter events, 141.4 us)
Async XLA Ops:
  7.2 88.2 %all-gather.8.cloned.1.call-start = ((), (), s32[]{:S(2)}) async-start(), calls=%async_computation.4 | async-start | bytes 2506752 | tf_op jit(solution)/shard_map/all_gather | solution.py:825
  14.0 39.0 %collective-permute-start = (bf16[176,768]{1,0:T(8,128)(2,1)S(1)}, bf16[176,768]{1,0:T(8,128)(2,1)}, u32[]{:S(2)}, u32[]{:S(2)}) collective-permute-start(bf16[176,768]{1,0:T(8,128)(2,1)S(1)} %concatenate.119), channel_id=1, source_target_pairs={{0,1},{1,0},{2,3},{3,2},{4,5},{5,4},{6,7},{7,6},{8,9},{9,8},{10,11... | collective-permute-start | bytes 811016 | tf_op jit(solution)/shard_map/ppermute | solution.py:774
  17.9 9.5 %collective-permute-start.1 = (bf16[48,1536]{1,0:T(8,128)(2,1)S(1)}, bf16[48,1536]{1,0:T(8,128)(2,1)S(1)}, u32[]{:S(2)}, u32[]{:S(2)}) collective-permute-start(bf16[48,1536]{1,0:T(8,128)(2,1)S(1)} %constant_dynamic-slice_fusion.2.refs_0_), channel_id=1, source_target_pairs={{0,1},{1,0},{2,3},{3,2},{4,5},{5,4},{6,7},{7,6},{8,9},{9,8},{10,11... | collective-permute-start | bytes 442376 | tf_op jit(solution)/shard_map/ppermute | solution.py:823
  19.3 38.5 %collective-permute-start.2 = (bf16[384,1024]{1,0:T(8,128)(2,1)S(1)}, bf16[384,1024]{1,0:T(8,128)(2,1)}, u32[]{:S(2)}, u32[]{:S(2)}) collective-permute-start(bf16[384,1024]{1,0:T(8,128)(2,1)S(1)} %delayed.3), channel_id=1, source_target_pairs={{0,1},{1,0},{2,3},{3,2},{4,5},{5,4},{6,7},{7,6},{8,9},{9,8},{10,11... | collective-permute-start | bytes 2359304 | tf_op jit(solution)/shard_map/ppermute | solution.py:809
  22.3 30.0 %collective-permute-start.5 = (bf16[48,1536]{1,0:T(8,128)(2,1)S(1)}, bf16[48,1536]{1,0:T(8,128)(2,1)S(1)}, u32[]{:S(2)}, u32[]{:S(2)}) collective-permute-start(bf16[48,1536]{1,0:T(8,128)(2,1)S(1)} %constant_dynamic-slice_fusion), channel_id=1, source_target_pairs={{0,1},{1,0},{2,3},{3,2},{4,5},{5,4},{6,7},{7,6},{8,9},{9,8},{10,11... | collective-permute-start | bytes 442376 | tf_op jit(solution)/shard_map/ppermute | solution.py:823
  22.4 27.6 %collective-permute-start.6 = (s32[512,8]{0,1:T(8,128)S(1)}, s32[512,8]{0,1:T(8,128)S(1)}, u32[]{:S(2)}, u32[]{:S(2)}) collective-permute-start(s32[512,8]{0,1:T(8,128)S(1)} %copy-done.58), channel_id=1, source_target_pairs={{0,1},{1,0},{2,3},{3,2},{4,5},{5,4},{6,7},{7,6},{8,9},{9,8},{10,11... | collective-permute-start | bytes 49160 | tf_op jit(solution)/shard_map/ppermute | solution.py:774
  28.1 96.8 %all-gather.10.cloned.1.call-start = ((), (), s32[]{:S(2)}) async-start(), calls=%async_computation.5 | async-start | bytes 2924544 | tf_op jit(solution)/shard_map/all_gather | solution.py:827
  55.3 113.4 %copy-start.60 = (bf16[16,40]{1,0:T(8,128)(2,1)}, bf16[16,40]{1,0:T(8,128)(2,1)S(1)}, u32[]{:S(2)}) copy-start(bf16[16,40]{1,0:T(8,128)(2,1)S(1)} %reshape.307) | copy-start | bytes 3844
  57.8 5.7 collective-permute-start.3
  65.2 26.0 %collective-permute-start.4 = (bf16[512,1024]{1,0:T(8,128)(2,1)S(1)}, bf16[512,1024]{1,0:T(8,128)(2,1)S(1)}, u32[]{:S(2)}, u32[]{:S(2)}) collective-permute-start(bf16[512,1024]{1,0:T(8,128)(2,1)S(1)} %pad_maximum_fusion.k_ref.v_ref.refs_2_), channel_id=1, source_target_pairs={{0,1},{1,0},{2,3},{3,2},{4,5},{5,4},{6,7},{7,6},{8,9},{9,8},{10,11... | collective-permute-start | bytes 3145736 | tf_op jit(solution)/shard_map/ppermute | solution.py:774
  93.7 98.2 %collective-permute-start.8 = (bf16[512,1536]{1,0:T(8,128)(2,1)S(1)}, bf16[512,1536]{1,0:T(8,128)(2,1)}, u32[]{:S(2)}, u32[]{:S(2)}) collective-permute-start(bf16[512,1536]{1,0:T(8,128)(2,1)S(1)} %delayed.4), channel_id=1, source_target_pairs={{0,1},{1,0},{2,3},{3,2},{4,5},{5,4},{6,7},{7,6},{8,9},{9,8},{10,11... | collective-permute-start | bytes 4718600 | tf_op jit(solution)/shard_map/ppermute | solution.py:774
  135.0 56.8 %collective-permute-start.7 = (bf16[512,1536]{1,0:T(8,128)(2,1)S(1)}, bf16[512,1536]{1,0:T(8,128)(2,1)}, u32[]{:S(2)}, u32[]{:S(2)}) collective-permute-start(bf16[512,1536]{1,0:T(8,128)(2,1)S(1)} %multiply_convert_fusion.refs_0_.x_ref), channel_id=1, source_target_pairs={{0,1},{1,0},{2,3},{3,2},{4,5},{5,4},{6,7},{7,6},{8,9},{9,8},{10,11... | collective-permute-start | bytes 4718600 | tf_op jit(solution)/shard_map/ppermute | solution.py:774
  171.1 20.0 %collective-permute-start.9 = (f32[20,512]{1,0:T(8,128)S(1)}, f32[20,512]{1,0:T(8,128)S(1)}, u32[]{:S(2)}, u32[]{:S(2)}) collective-permute-start(f32[20,512]{1,0:T(8,128)S(1)} %get-tuple-element.203), channel_id=1, source_target_pairs={{0,1},{1,0},{2,3},{3,2},{4,5},{5,4},{6,7},{7,6},{8,9},{9,8},{10,11... | collective-permute-start | bytes 122888 | tf_op jit(solution)/shard_map/ppermute | solution.py:774
  265.4 103.4 %all-to-all-start = ((bf16[16,80,768]{2,1,0:T(8,128)(2,1)}), bf16[16,80,768]{2,1,0:T(8,128)(2,1)}, u32[]{:S(2)}, u32[]{:S(2)}) async-start(bf16[16,80,768]{2,1,0:T(8,128)(2,1)} %bitcast.181), calls=%async_computation | async-start | bytes 3932160 | tf_op jit(solution)/shard_map/all_to_all | solution.py:1058
  279.8 295.8 %all-gather.14.cloned.1.call-start = ((), (), s32[]{:S(2)}) async-start(), calls=%async_computation.7 | async-start | bytes 8355840 | tf_op jit(solution)/shard_map/all_gather | solution.py:1057
  372.6 40.1 %collective-permute-start.10 = (bf16[512,1536]{1,0:T(8,128)(2,1)}, bf16[512,1536]{1,0:T(8,128)(2,1)}, u32[]{:S(2)}, u32[]{:S(2)}) collective-permute-start(bf16[512,1536]{1,0:T(8,128)(2,1)} %get-tuple-element.73), channel_id=1, source_target_pairs={{0,1},{1,0},{2,3},{3,2},{4,5},{5,4},{6,7},{7,6},{8,9},{9,8},{10,11... | collective-permute-start | bytes 4718600 | tf_op jit(solution)/shard_map/ppermute | solution.py:789
  374.0 36.9 %collective-permute-start.11 = (f32[20,512]{1,0:T(8,128)S(1)}, f32[20,512]{1,0:T(8,128)S(1)}, u32[]{:S(2)}, u32[]{:S(2)}) collective-permute-start(f32[20,512]{1,0:T(8,128)S(1)} %get-tuple-element.200), channel_id=1, source_target_pairs={{0,1},{1,0},{2,3},{3,2},{4,5},{5,4},{6,7},{7,6},{8,9},{9,8},{10,11... | collective-permute-start | bytes 122888 | tf_op jit(solution)/shard_map/ppermute | solution.py:774
  375.6 65.2 %all-to-all-start.3 = ((bf16[16,80,768]{2,1,0:T(8,128)(2,1)}), bf16[16,80,768]{2,1,0:T(8,128)(2,1)}, u32[]{:S(2)}, u32[]{:S(2)}) async-start(bf16[16,80,768]{2,1,0:T(8,128)(2,1)} %bitcast.180), calls=%async_computation.3 | async-start | bytes 3932160 | tf_op jit(solution)/shard_map/all_to_all | solution.py:1058
  381.8 203.3 %all-gather.12.cloned.1.call-start = ((), (), s32[]{:S(2)}) async-start(), calls=%async_computation.6 | async-start | bytes 8355840 | tf_op jit(solution)/shard_map/all_gather | solution.py:1130
  452.3 46.2 %collective-permute-start.14 = (bf16[512,512]{1,0:T(8,128)(2,1)}, bf16[512,512]{1,0:T(8,128)(2,1)S(1)}, u32[]{:S(2)}, u32[]{:S(2)}) collective-permute-start(bf16[512,512]{1,0:T(8,128)(2,1)} %pad_maximum_fusion.2), channel_id=1, source_target_pairs={{0,1},{1,0},{2,3},{3,2},{4,5},{5,4},{6,7},{7,6},{8,9},{9,8},{10,11... | collective-permute-start | bytes 1572872 | tf_op jit(solution)/shard_map/ppermute | solution.py:789
  481.0 22.7 %collective-permute-start.12 = (bf16[512,512]{1,0:T(8,128)(2,1)S(1)}, bf16[512,512]{1,0:T(8,128)(2,1)S(1)}, u32[]{:S(2)}, u32[]{:S(2)}) collective-permute-start(bf16[512,512]{1,0:T(8,128)(2,1)S(1)} %pad_maximum_fusion.1), channel_id=1, source_target_pairs={{0,1},{1,0},{2,3},{3,2},{4,5},{5,4},{6,7},{7,6},{8,9},{9,8},{10,11... | collective-permute-start | bytes 1572872 | tf_op jit(solution)/shard_map/ppermute | solution.py:789
  506.1 39.6 %all-to-all-start.1 = ((bf16[32,8,768]{2,1,0:T(8,128)(2,1)}), bf16[32,8,768]{2,1,0:T(8,128)(2,1)}, u32[]{:S(2)}, u32[]{:S(2)}) async-start(bf16[32,8,768]{2,1,0:T(8,128)(2,1)} %bitcast.36.refs_0_), calls=%async_computation.1 | async-start | bytes 786432 | tf_op jit(solution)/shard_map/all_to_all | solution.py:1151
  526.3 39.8 %collective-permute-start.13 = (bf16[512,1536]{1,0:T(8,128)(2,1)}, bf16[512,1536]{1,0:T(8,128)(2,1)}, u32[]{:S(2)}, u32[]{:S(2)}) collective-permute-start(bf16[512,1536]{1,0:T(8,128)(2,1)} %delayed.5), channel_id=1, source_target_pairs={{0,1},{1,0},{2,3},{3,2},{4,5},{5,4},{6,7},{7,6},{8,9},{9,8},{10,11... | collective-permute-start | bytes 4718600 | tf_op jit(solution)/shard_map/ppermute | solution.py:782
  548.0 23.3 %all-to-all-start.2 = ((bf16[16,4,8,768]{3,2,1,0:T(8,128)(2,1)}), bf16[16,4,8,768]{3,2,1,0:T(8,128)(2,1)}, u32[]{:S(2)}, u32[]{:S(2)}) async-start(bf16[16,4,8,768]{3,2,1,0:T(8,128)(2,1)} %broadcast_in_dim.216), calls=%async_computation.2 | async-start | bytes 1572864 | tf_op jit(solution)/shard_map/all_to_all | solution.py:1155
  (71 other events, 932.5 us)
Sparse Core Ops, SparseCore 0:
  28.3 44.0 all-gather.7
  75.2 42.4 all-gather.9
  372.7 105.2 all-gather.13
  480.2 76.2 all-gather.11

commit v7 on v5

--- a/solution.py
+++ b/solution.py
@@ -331,7 +331,7 @@
             jax.ShapeDtypeStruct((pairs, count, narrow), F32),
         ],
         compiler_params=pltpu.CompilerParams(
-            vmem_limit_bytes=40 * 1024 * 1024, dimension_semantics=("arbitrary",)
+            vmem_limit_bytes=60 * 1024 * 1024, dimension_semantics=("arbitrary",)
         ),
         cost_estimate=pl.CostEstimate(flops=40_000_000_000, bytes_accessed=8_000_000, transcendentals=10_000_000),
         name="attention",
@@ -366,7 +366,7 @@
         + [jax.ShapeDtypeStruct((count, pairs * narrow), BF16)] * 2
         + [jax.ShapeDtypeStruct((far.shape[0], pairs * narrow), BF16)] * 2,
         compiler_params=pltpu.CompilerParams(
-            vmem_limit_bytes=40 * 1024 * 1024, dimension_semantics=("arbitrary",)
+            vmem_limit_bytes=60 * 1024 * 1024, dimension_semantics=("arbitrary",)
         ),
         cost_estimate=pl.CostEstimate(
             flops=17_000_000_000 * pairs, bytes_accessed=3_000_000 * pairs, transcendentals=0
@@ -621,7 +621,7 @@
         ],
         input_output_aliases={7 + n: n for n in range(len(held))},
         compiler_params=pltpu.CompilerParams(
-            vmem_limit_bytes=40 * 1024 * 1024, dimension_semantics=("arbitrary",)
+            vmem_limit_bytes=60 * 1024 * 1024, dimension_semantics=("arbitrary",)
         ),
         cost_estimate=pl.CostEstimate(
             flops=3_000_000_000 * count, bytes_accessed=12_000_000 * count, transcendentals=0
@@ -654,7 +654,7 @@
             scratch_shapes=[pltpu.VMEM(shape, F32)],
         ),
         out_shape=jax.ShapeDtypeStruct(shape, BF16),
-        compiler_params=pltpu.CompilerParams(vmem_limit_bytes=32 * 1024 * 1024),
+        compiler_params=pltpu.CompilerParams(vmem_limit_bytes=60 * 1024 * 1024),
         cost_estimate=pl.CostEstimate(flops=0, bytes_accessed=5_000_000, transcendentals=0),
         name="totals",
     )(ids, rows, *after)
@@ -1073,13 +1073,9 @@
             logs,
             n * pairs,
             pairs,
-            (last,) if n else (),
         )
         d_kv = to_owners(jnp.concatenate(d_kv[:2], axis=1), jnp.concatenate(d_kv[2:], axis=1)).astype(BF16)
         parts.append((d_q, d_kv[:, : kv_width // 2], d_kv[:, kv_width // 2 :]))
-        if n == 0:
-            last = totals(ids_all, swapped, adapters, after=(d_q,))
-            spread.append(lax.all_gather(last, "rep", axis=0))
     mixture = owners_terms(result_near, delayed(result_far, (parts[1][1],)))
     d_queries, d_keys, d_values = [jnp.concatenate(pair, axis=1) for pair in zip(*parts)]
     d_keyvals = jnp.concatenate([d_keys, d_values], axis=1)
@@ -1107,6 +1103,8 @@
         axis=0,
     )
 
+    last = totals(ids_all, swapped, adapters, after=(parts[0][0],))
+    spread.append(lax.all_gather(last, "rep", axis=0))
     expert_grads = ()
     for n in range(calls):
         expert_grads = unpack_grads(spread[n], experts_dev, n * each, tuple(expert_grads), width)
@@ -1130,7 +1128,8 @@
     dense = lax.all_to_all(dense, ("rep", "grp"), split_axis=0, concat_axis=0, tiled=True)
     owner_hot = (jnp.arange(adapters, dtype=jnp.int32)[:, None] == jnp.repeat(ids_all, groups)[None, :])
     dense = jnp.sum(jnp.where(owner_hot[:, :, None, None], dense.astype(F32)[None], 0.0), axis=1).astype(BF16)
-    dense = lax.all_gather(dense, "rep", axis=0).swapaxes(0, 1).reshape(adapters, -1, part).astype(F32)
+    dense = jnp.broadcast_to(dense[None], (reps,) + dense.shape)
+    dense = lax.all_to_all(dense, "rep", split_axis=0, concat_axis=0, tiled=True).swapaxes(0, 1).reshape(adapters, -1, part).astype(F32)
     wide = dense[:, high:]
     owned = [
         dense[:, : 3 * RANK],

time: 604 us -> 597 us (0.988)
  blocking collectives: 20.9 us -> 0 us
  local copies, waits for them, and re-layouts: 53.2 us -> 35.5 us
  matrix products: 50.7 us -> 64.1 us
  starting transfers between devices: 76 us -> 86.6 us
    unnamed x231 -> x155, local copies, waits for them, and re-layouts: 37.8 us -> 16.2 us
    all_gather x1 -> x0, blocking collectives: 20.9 us -> none  [local(): lax.all_gather(dense, 'rep', axis=0).swapaxes(0, 1)]
    ppermute x3, starting transfers between devices: 17.7 us -> 24.9 us  [to_owners(): lax.ppermute(far, 'grp', swap_pairs(2)).astype(F32)]
    dot_general x13, matrix products: 18.5 us -> 25.2 us  [product_back(): lax.dot_general(left, right, (((1,), (1,)), ((), ())), preferred_element_...]
    all_to_all x1, waiting for transfers between devices: 4.3 us -> 10.9 us  [local(): lax.all_to_all(dense, ('rep', 'grp'), split_axis=0, concat_axis=0, tiled=...]
  transfers between devices with their start and end apart: 22 -> 23, of which waited for: 5 -> 7; matrix products, arithmetic and copies ran while one was open for 14% -> 17% of each run, Pallas kernels for 38% -> 39%
where the time goes in v7:
time: 597 us; the launch traced here: 588 us
  Pallas kernels  312 us (52%)
  starting transfers between devices  86.6 us (15%)
  matrix products  64.1 us (11%)
  waiting for transfers between devices  51.5 us (9%)
  local copies, waits for them, and re-layouts  35.5 us (6%)
  other arithmetic  22.1 us (4%)
  between operations  16.2 us (3%)
    pallas_call x2, Pallas kernels, run_experts(): pl.pallas_call(functools.partial(expert_kernel, blocks=blocks, rows_block...  153 us
    pallas_call x4, Pallas kernels, fold_adapters(): pl.pallas_call(fold_kernel, grid_spec=pltpu.PrefetchScalarGridSpec(num_sc...  75.8 us
    pallas_call x2, Pallas kernels, run_attention_back(): pl.pallas_call(functools.partial(attend_back_kernel, here=here, segs=segs...  37 us
    dot_general x15, matrix products, product(): return jnp.dot(left, right, preferred_element_type=F32)  33.1 us
    ppermute x7, waiting for transfers between devices, from_others(): return lax.ppermute(piece, 'grp', swap_pairs(2))  33 us
    dot_general x13, matrix products, product_back(): lax.dot_general(left, right, (((1,), (1,)), ((), ())), preferred_element_...  25.2 us
    ppermute x3, starting transfers between devices, to_owners(): lax.ppermute(far, 'grp', swap_pairs(2)).astype(F32)  24.9 us
    ppermute x7, starting transfers between devices, from_others(): return lax.ppermute(piece, 'grp', swap_pairs(2))  22.8 us
  transfers between devices with their start and end apart: 23, of which 7 were waited for; matrix products, arithmetic and copies ran while one was open for 17% of the time, Pallas kernels for 39%

profile of v7, /device:TPU:0, one launch (start us, length us, event | category | flops | bytes accessed | tf_op | source)
XLA Modules:
  0.0 587.9 jit_solution(12698176981849522101)
XLA Ops:
  30.6 18.9 %fold.6 = (bf16[10,1536,1024]{2,1,0:T(8,128)(2,1)}, bf16[10,512,1536]{2,1,0:T(8,128)(2,1)}) custom-call(s32[1]{0:T(128)} %copy.218.chosen_ref, bf16[20,1536,1024]{2,1,0:T(8,128)(2,1)} %w1_ref.7, bf16[20,512,1536]{2,1,0:T(8,128)(2,1)} %w2_ref.7, bf16[4,20,32,1536]{3,2,1,0:T(8,128)(2,1)} %bitcast.160, bf16[4,20,2,16,512]{4,3,2,1,0:T(8,128)(2,1)} %b1_ref.11, ...), custom_call_target="tpu_custom_call" | custom-call | flops 15000000512 | bytes 60000000 | tf_op jit(solution)/shard_map/fold/pallas_call | solution.py:602
  66.7 19.1 %fold.7 = (bf16[10,1536,1024]{2,1,0:T(8,128)(2,1)}, bf16[10,512,1536]{2,1,0:T(8,128)(2,1)}) custom-call(s32[1]{0:T(128)} %copy.218.chosen_ref, bf16[20,1536,1024]{2,1,0:T(8,128)(2,1)} %w1_ref.7, bf16[20,512,1536]{2,1,0:T(8,128)(2,1)} %w2_ref.7, bf16[4,20,32,1536]{3,2,1,0:T(8,128)(2,1)} %bitcast.161, ...), custom_call_target="tpu_custom_call", output_to_operand_aliasing={{0}: (7, {}), {1}: (8, {})} | custom-call | flops 15000000512 | bytes 60000000 | tf_op jit(solution)/shard_map/fold/pallas_call | solution.py:602
  85.8 4.8 collective-permute-done.4.k_far.v_far.refs_0_
  94.8 4.2 convolution_add_fusion.2
  101.6 20.6 %attention.1 = (bf16[512,1536]{1,0:T(8,128)(2,1)}, f32[4,512,128]{2,1,0:T(8,128)}) custom-call(s32[64]{0:T(128)} %reshape.301.list_ref, s32[4]{0:T(128)} %and_select_fusion.steps_ref, bf16[512,1536]{1,0:T(8,128)(2,1)} %fusion.28.q_ref, bf16[512,1024]{1,0:T(8,128)(2,1)} %copy-done.24, bf16[512,1024]{1,0:T(8,128)(2,1)} %copy-done.24, ...), custom_call_target="tpu_custom_call" | custom-call | flops 40000000000 | bytes 8000000 | tf_op jit(solution)/shard_map/attention/pallas_call | solution.py:317
  129.8 5.6 multiply_reduce_fusion.1
  137.2 13.4 %collective-permute-start.6 = (bf16[512,1536]{1,0:T(8,128)(2,1)S(1)}, bf16[512,1536]{1,0:T(8,128)(2,1)}, u32[]{:S(2)}, u32[]{:S(2)}) collective-permute-start(bf16[512,1536]{1,0:T(8,128)(2,1)S(1)} %multiply_convert_fusion.refs_0_.x_ref), channel_id=1, source_target_pairs={{0,1},{1,0},{2,3},{3,2},{4,5},{5,4},{6,7},{7,6},{8,9},{9,8},{10,11... | collective-permute-start | bytes 4718600 | tf_op jit(solution)/shard_map/ppermute | solution.py:753
  150.6 18.9 %fold.4 = (bf16[10,1536,1024]{2,1,0:T(8,128)(2,1)}, bf16[10,512,1536]{2,1,0:T(8,128)(2,1)}) custom-call(s32[1]{0:T(128)} %copy.218.chosen_ref, bf16[20,1536,1024]{2,1,0:T(8,128)(2,1)} %w1_ref.7, bf16[20,512,1536]{2,1,0:T(8,128)(2,1)} %w2_ref.7, bf16[4,20,32,1536]{3,2,1,0:T(8,128)(2,1)} %bitcast.162, bf16[4,20,2,16,512]{4,3,2,1,0:T(8,128)(2,1)} %b1_ref.11, ...), custom_call_target="tpu_custom_call" | custom-call | flops 15000000512 | bytes 60000000 | tf_op jit(solution)/shard_map/fold/pallas_call | solution.py:602
  173.3 18.9 %fold.5 = (bf16[10,1536,1024]{2,1,0:T(8,128)(2,1)}, bf16[10,512,1536]{2,1,0:T(8,128)(2,1)}) custom-call(s32[1]{0:T(128)} %copy.218.chosen_ref, bf16[20,1536,1024]{2,1,0:T(8,128)(2,1)} %w1_ref.7, bf16[20,512,1536]{2,1,0:T(8,128)(2,1)} %w2_ref.7, bf16[4,20,32,1536]{3,2,1,0:T(8,128)(2,1)} %bitcast.163, ...), custom_call_target="tpu_custom_call", output_to_operand_aliasing={{0}: (7, {}), {1}: (8, {})} | custom-call | flops 15000000512 | bytes 60000000 | tf_op jit(solution)/shard_map/fold/pallas_call | solution.py:602
  193.7 75.7 %experts.2 = (bf16[512,1536]{1,0:T(8,128)(2,1)}, bf16[512,1536]{1,0:T(8,128)(2,1)}, bf16[512,1536]{1,0:T(8,128)(2,1)}, bf16[512,1536]{1,0:T(8,128)(2,1)}, f32[10...) custom-call(s32[1]{0:T(128)} %copy.218.chosen_ref, bf16[512,1536]{1,0:T(8,128)(2,1)} %copy-done.15, ...), custom_call_target="tpu_custom_call" | custom-call | flops 80000000000 | bytes 50000000 | tf_op jit(solution)/shard_map/experts/pallas_call | solution.py:520
  269.4 10.2 %all-to-all-start = ((bf16[16,80,768]{2,1,0:T(8,128)(2,1)}), bf16[16,80,768]{2,1,0:T(8,128)(2,1)}, u32[]{:S(2)}, u32[]{:S(2)}) async-start(bf16[16,80,768]{2,1,0:T(8,128)(2,1)} %bitcast.179), calls=%async_computation | async-start | bytes 3932160 | tf_op jit(solution)/shard_map/all_to_all | solution.py:1035
  279.6 77.6 %experts.3 = (bf16[512,1536]{1,0:T(8,128)(2,1)}, bf16[512,1536]{1,0:T(8,128)(2,1)}, bf16[512,1536]{1,0:T(8,128)(2,1)}, bf16[512,1536]{1,0:T(8,128)(2,1)}, f32[10...) custom-call(s32[1]{0:T(128)} %copy.218.chosen_ref, bf16[512,1536]{1,0:T(8,128)(2,1)} %copy-done.15, ...), custom_call_target="tpu_custom_call" | custom-call | flops 80000000000 | bytes 50000000 | tf_op jit(solution)/shard_map/experts/pallas_call | solution.py:520
  364.0 6.3 %all-to-all-start.3 = ((bf16[16,80,768]{2,1,0:T(8,128)(2,1)}), bf16[16,80,768]{2,1,0:T(8,128)(2,1)}, u32[]{:S(2)}, u32[]{:S(2)}) async-start(bf16[16,80,768]{2,1,0:T(8,128)(2,1)} %bitcast.178), calls=%async_computation.3 | async-start | bytes 3932160 | tf_op jit(solution)/shard_map/all_to_all | solution.py:1035
  370.7 28.2 %collective-permute-done.11 = f32[20,512]{1,0:T(8,128)S(1)} collective-permute-done((f32[20,512]{1,0:T(8,128)S(1)}, f32[20,512]{1,0:T(8,128)S(1)}, u32[]{:S(2)}, u32[]{:S(2)}) %collective-permute-start.11) | collective-permute-done | bytes 40992 | tf_op jit(solution)/shard_map/ppermute | solution.py:753
  412.5 18.4 %attention_back.3 = (bf16[512,768]{1,0:T(8,128)(2,1)}, bf16[512,256]{1,0:T(8,128)(2,1)}, bf16[512,256]{1,0:T(8,128)(2,1)}, bf16[512,256]{1,0:T(8,128)(2,1)}, bf16[512,256]{1,0:T(8,128)(2,1)}) custom-call(s32[64]{0:T(128)} %reshape.301.list_ref, s32[4]{0:T(128)} %and_select_fusion.steps_ref, bf16[512,1536]{1,0:T(8,128)(2,1)} %fusion.28.q_ref, ...), custom_call_target="tpu_custom_call" | custom-call | flops 33999998976 | bytes 6000000 | tf_op jit(solution)/shard_map/attention_back/pallas_call | solution.py:351
  442.4 12.4 %collective-permute-start.14 = (bf16[512,512]{1,0:T(8,128)(2,1)}, bf16[512,512]{1,0:T(8,128)(2,1)S(1)}, u32[]{:S(2)}, u32[]{:S(2)}) collective-permute-start(bf16[512,512]{1,0:T(8,128)(2,1)} %pad_maximum_fusion.2), channel_id=1, source_target_pairs={{0,1},{1,0},{2,3},{3,2},{4,5},{5,4},{6,7},{7,6},{8,9},{9,8},{10,11... | collective-permute-start | bytes 1572872 | tf_op jit(solution)/shard_map/ppermute | solution.py:768
  454.8 18.6 %attention_back.2 = (bf16[512,768]{1,0:T(8,128)(2,1)}, bf16[512,256]{1,0:T(8,128)(2,1)}, bf16[512,256]{1,0:T(8,128)(2,1)}, bf16[512,256]{1,0:T(8,128)(2,1)}, bf16[512,256]{1,0:T(8,128)(2,1)}) custom-call(s32[64]{0:T(128)} %reshape.301.list_ref, s32[4]{0:T(128)} %and_select_fusion.steps_ref, bf16[512,1536]{1,0:T(8,128)(2,1)} %fusion.28.q_ref, ...), custom_call_target="tpu_custom_call" | custom-call | flops 33999998976 | bytes 6000000 | tf_op jit(solution)/shard_map/attention_back/pallas_call | solution.py:351
  474.7 10.6 %collective-permute-start.12 = (bf16[512,512]{1,0:T(8,128)(2,1)S(1)}, bf16[512,512]{1,0:T(8,128)(2,1)S(1)}, u32[]{:S(2)}, u32[]{:S(2)}) collective-permute-start(bf16[512,512]{1,0:T(8,128)(2,1)S(1)} %pad_maximum_fusion.1), channel_id=1, source_target_pairs={{0,1},{1,0},{2,3},{3,2},{4,5},{5,4},{6,7},{7,6},{8,9},{9,8},{10,11... | collective-permute-start | bytes 1572872 | tf_op jit(solution)/shard_map/ppermute | solution.py:768
  495.4 13.5 %all-to-all-start.1 = ((bf16[32,8,768]{2,1,0:T(8,128)(2,1)}), bf16[32,8,768]{2,1,0:T(8,128)(2,1)}, u32[]{:S(2)}, u32[]{:S(2)}) async-start(bf16[32,8,768]{2,1,0:T(8,128)(2,1)} %bitcast.35.refs_0_), calls=%async_computation.1 | async-start | bytes 786432 | tf_op jit(solution)/shard_map/all_to_all | solution.py:1128
  520.7 10.9 %all-to-all-done.1 = bf16[32,8,768]{2,1,0:T(8,128)(2,1)} async-done(((bf16[32,8,768]{2,1,0:T(8,128)(2,1)}), bf16[32,8,768]{2,1,0:T(8,128)(2,1)}, u32[]{:S(2)}, u32[]{:S(2)}) %all-to-all-start.1) | async-done | bytes 393248 | tf_op jit(solution)/shard_map/all_to_all | solution.py:1128
  533.9 4.3 all-to-all-start.2
  538.2 9.8 %fusion.15 = (f32[512]{0:T(512)S(1)}, f32[512,1536]{1,0:T(8,128)S(1)}) fusion(bf16[512,1536]{1,0:T(8,128)(2,1)} %param.25, f32[512]{0:T(512)S(1)} %copy-done.67, f32[1536]{0:T(1024)S(1)} %copy-done.65, f32[512,1536]{1,0:T(8,128)} %fusion.52, f32[512,1536]{1,0:T(8,128)} %fusion.21, bf16[512,1536]{1,0:T(8,128)(2,1)} %copy-done.21, ...), kind=kOutput, calls=%fused_computation.23 | convolution fusion | flops 2442657280 | bytes 17311744 | tf_op jit(solution)/shard_map/dot_general | solution.py:30
  565.6 6.2 %unpack.2 = (f32[4,20,32,1536]{3,2,1,0:T(8,128)}, f32[4,20,2,16,512]{4,3,2,1,0:T(8,128)}, f32[4,20,16,512]{3,2,1,0:T(8,128)}, f32[4,20,16,1536]{3,2,1,0:T(8,128)}) custom-call(bf16[16,4,80,768]{3,2,1,0:T(8,128)(2,1)S(1)} %bitcast.159), custom_call_target="tpu_custom_call" | custom-call | bytes 30000000 | tf_op jit(solution)/shard_map/unpack/pallas_call | solution.py:720
  575.0 6.2 %unpack.3 = (f32[4,20,32,1536]{3,2,1,0:T(8,128)}, f32[4,20,2,16,512]{4,3,2,1,0:T(8,128)}, f32[4,20,16,512]{3,2,1,0:T(8,128)}, f32[4,20,16,1536]{3,2,1,0:T(8,128)}) custom-call(bf16[16,4,80,768]{3,2,1,0:T(8,128)(2,1)S(1)} %bitcast.158, ...), custom_call_target="tpu_custom_call", output_to_operand_aliasing={{0}: (1, {}), {1}: (2, {}), {2}: (3, {}), {3}: (4, {})} | custom-call | bytes 30000000 | tf_op jit(solution)/shard_map/unpack/pallas_call | solution.py:720
  (345 shorter events, 138.6 us)
Async XLA Ops:
  7.2 87.6 %all-gather.8.cloned.1.call-start = ((), (), s32[]{:S(2)}) async-start(), calls=%async_computation.4 | async-start | bytes 2506752 | tf_op jit(solution)/shard_map/all_gather | solution.py:804
  14.0 38.3 %collective-permute-start = (bf16[176,768]{1,0:T(8,128)(2,1)S(1)}, bf16[176,768]{1,0:T(8,128)(2,1)}, u32[]{:S(2)}, u32[]{:S(2)}) collective-permute-start(bf16[176,768]{1,0:T(8,128)(2,1)S(1)} %concatenate.119), channel_id=1, source_target_pairs={{0,1},{1,0},{2,3},{3,2},{4,5},{5,4},{6,7},{7,6},{8,9},{9,8},{10,11... | collective-permute-start | bytes 811016 | tf_op jit(solution)/shard_map/ppermute | solution.py:753
  17.9 9.5 %collective-permute-start.1 = (bf16[48,1536]{1,0:T(8,128)(2,1)S(1)}, bf16[48,1536]{1,0:T(8,128)(2,1)S(1)}, u32[]{:S(2)}, u32[]{:S(2)}) collective-permute-start(bf16[48,1536]{1,0:T(8,128)(2,1)S(1)} %constant_dynamic-slice_fusion.2.refs_0_), channel_id=1, source_target_pairs={{0,1},{1,0},{2,3},{3,2},{4,5},{5,4},{6,7},{7,6},{8,9},{9,8},{10,11... | collective-permute-start | bytes 442376 | tf_op jit(solution)/shard_map/ppermute | solution.py:802
  19.3 38.1 %collective-permute-start.2 = (bf16[384,1024]{1,0:T(8,128)(2,1)S(1)}, bf16[384,1024]{1,0:T(8,128)(2,1)}, u32[]{:S(2)}, u32[]{:S(2)}) collective-permute-start(bf16[384,1024]{1,0:T(8,128)(2,1)S(1)} %delayed.3), channel_id=1, source_target_pairs={{0,1},{1,0},{2,3},{3,2},{4,5},{5,4},{6,7},{7,6},{8,9},{9,8},{10,11... | collective-permute-start | bytes 2359304 | tf_op jit(solution)/shard_map/ppermute | solution.py:788
  22.3 29.2 %collective-permute-start.5 = (bf16[48,1536]{1,0:T(8,128)(2,1)S(1)}, bf16[48,1536]{1,0:T(8,128)(2,1)S(1)}, u32[]{:S(2)}, u32[]{:S(2)}) collective-permute-start(bf16[48,1536]{1,0:T(8,128)(2,1)S(1)} %constant_dynamic-slice_fusion), channel_id=1, source_target_pairs={{0,1},{1,0},{2,3},{3,2},{4,5},{5,4},{6,7},{7,6},{8,9},{9,8},{10,11... | collective-permute-start | bytes 442376 | tf_op jit(solution)/shard_map/ppermute | solution.py:802
  22.4 27.8 %collective-permute-start.8 = (s32[512,8]{0,1:T(8,128)S(1)}, s32[512,8]{0,1:T(8,128)S(1)}, u32[]{:S(2)}, u32[]{:S(2)}) collective-permute-start(s32[512,8]{0,1:T(8,128)S(1)} %copy-done.58), channel_id=1, source_target_pairs={{0,1},{1,0},{2,3},{3,2},{4,5},{5,4},{6,7},{7,6},{8,9},{9,8},{10,11... | collective-permute-start | bytes 49160 | tf_op jit(solution)/shard_map/ppermute | solution.py:753
  28.1 99.0 %all-gather.10.cloned.1.call-start = ((), (), s32[]{:S(2)}) async-start(), calls=%async_computation.5 | async-start | bytes 2924544 | tf_op jit(solution)/shard_map/all_gather | solution.py:806
  54.6 116.0 %copy-start.60 = (bf16[16,40]{1,0:T(8,128)(2,1)}, bf16[16,40]{1,0:T(8,128)(2,1)S(1)}, u32[]{:S(2)}) copy-start(bf16[16,40]{1,0:T(8,128)(2,1)S(1)} %reshape.307) | copy-start | bytes 3844
  57.4 5.7 collective-permute-start.3
  64.9 25.7 %collective-permute-start.4 = (bf16[512,1024]{1,0:T(8,128)(2,1)S(1)}, bf16[512,1024]{1,0:T(8,128)(2,1)S(1)}, u32[]{:S(2)}, u32[]{:S(2)}) collective-permute-start(bf16[512,1024]{1,0:T(8,128)(2,1)S(1)} %pad_maximum_fusion.k_ref.v_ref.refs_2_), channel_id=1, source_target_pairs={{0,1},{1,0},{2,3},{3,2},{4,5},{5,4},{6,7},{7,6},{8,9},{9,8},{10,11... | collective-permute-start | bytes 3145736 | tf_op jit(solution)/shard_map/ppermute | solution.py:753
  93.0 100.7 %collective-permute-start.7 = (bf16[512,1536]{1,0:T(8,128)(2,1)S(1)}, bf16[512,1536]{1,0:T(8,128)(2,1)}, u32[]{:S(2)}, u32[]{:S(2)}) collective-permute-start(bf16[512,1536]{1,0:T(8,128)(2,1)S(1)} %delayed.4), channel_id=1, source_target_pairs={{0,1},{1,0},{2,3},{3,2},{4,5},{5,4},{6,7},{7,6},{8,9},{9,8},{10,11... | collective-permute-start | bytes 4718600 | tf_op jit(solution)/shard_map/ppermute | solution.py:753
  137.2 56.4 %collective-permute-start.6 = (bf16[512,1536]{1,0:T(8,128)(2,1)S(1)}, bf16[512,1536]{1,0:T(8,128)(2,1)}, u32[]{:S(2)}, u32[]{:S(2)}) collective-permute-start(bf16[512,1536]{1,0:T(8,128)(2,1)S(1)} %multiply_convert_fusion.refs_0_.x_ref), channel_id=1, source_target_pairs={{0,1},{1,0},{2,3},{3,2},{4,5},{5,4},{6,7},{7,6},{8,9},{9,8},{10,11... | collective-permute-start | bytes 4718600 | tf_op jit(solution)/shard_map/ppermute | solution.py:753
  172.9 20.0 %collective-permute-start.9 = (f32[20,512]{1,0:T(8,128)S(1)}, f32[20,512]{1,0:T(8,128)S(1)}, u32[]{:S(2)}, u32[]{:S(2)}) collective-permute-start(f32[20,512]{1,0:T(8,128)S(1)} %get-tuple-element.203), channel_id=1, source_target_pairs={{0,1},{1,0},{2,3},{3,2},{4,5},{5,4},{6,7},{7,6},{8,9},{9,8},{10,11... | collective-permute-start | bytes 122888 | tf_op jit(solution)/shard_map/ppermute | solution.py:753
  269.4 87.9 %all-to-all-start = ((bf16[16,80,768]{2,1,0:T(8,128)(2,1)}), bf16[16,80,768]{2,1,0:T(8,128)(2,1)}, u32[]{:S(2)}, u32[]{:S(2)}) async-start(bf16[16,80,768]{2,1,0:T(8,128)(2,1)} %bitcast.179), calls=%async_computation | async-start | bytes 3932160 | tf_op jit(solution)/shard_map/all_to_all | solution.py:1035
  279.5 282.8 %all-gather.14.cloned.1.call-start = ((), (), s32[]{:S(2)}) async-start(), calls=%async_computation.7 | async-start | bytes 8355840 | tf_op jit(solution)/shard_map/all_gather | solution.py:1034
  360.9 39.7 %collective-permute-start.10 = (bf16[512,1536]{1,0:T(8,128)(2,1)}, bf16[512,1536]{1,0:T(8,128)(2,1)}, u32[]{:S(2)}, u32[]{:S(2)}) collective-permute-start(bf16[512,1536]{1,0:T(8,128)(2,1)} %get-tuple-element.73), channel_id=1, source_target_pairs={{0,1},{1,0},{2,3},{3,2},{4,5},{5,4},{6,7},{7,6},{8,9},{9,8},{10,11... | collective-permute-start | bytes 4718600 | tf_op jit(solution)/shard_map/ppermute | solution.py:768
  363.6 35.3 %collective-permute-start.11 = (f32[20,512]{1,0:T(8,128)S(1)}, f32[20,512]{1,0:T(8,128)S(1)}, u32[]{:S(2)}, u32[]{:S(2)}) collective-permute-start(f32[20,512]{1,0:T(8,128)S(1)} %get-tuple-element.200), channel_id=1, source_target_pairs={{0,1},{1,0},{2,3},{3,2},{4,5},{5,4},{6,7},{7,6},{8,9},{9,8},{10,11... | collective-permute-start | bytes 122888 | tf_op jit(solution)/shard_map/ppermute | solution.py:753
  364.0 66.9 %all-to-all-start.3 = ((bf16[16,80,768]{2,1,0:T(8,128)(2,1)}), bf16[16,80,768]{2,1,0:T(8,128)(2,1)}, u32[]{:S(2)}, u32[]{:S(2)}) async-start(bf16[16,80,768]{2,1,0:T(8,128)(2,1)} %bitcast.178), calls=%async_computation.3 | async-start | bytes 3932160 | tf_op jit(solution)/shard_map/all_to_all | solution.py:1035
  370.2 201.5 %all-gather.12.cloned.1.call-start = ((), (), s32[]{:S(2)}) async-start(), calls=%async_computation.6 | async-start | bytes 8355840 | tf_op jit(solution)/shard_map/all_gather | solution.py:1107
  442.4 49.6 %collective-permute-start.14 = (bf16[512,512]{1,0:T(8,128)(2,1)}, bf16[512,512]{1,0:T(8,128)(2,1)S(1)}, u32[]{:S(2)}, u32[]{:S(2)}) collective-permute-start(bf16[512,512]{1,0:T(8,128)(2,1)} %pad_maximum_fusion.2), channel_id=1, source_target_pairs={{0,1},{1,0},{2,3},{3,2},{4,5},{5,4},{6,7},{7,6},{8,9},{9,8},{10,11... | collective-permute-start | bytes 1572872 | tf_op jit(solution)/shard_map/ppermute | solution.py:768
  474.7 18.3 %collective-permute-start.12 = (bf16[512,512]{1,0:T(8,128)(2,1)S(1)}, bf16[512,512]{1,0:T(8,128)(2,1)S(1)}, u32[]{:S(2)}, u32[]{:S(2)}) collective-permute-start(bf16[512,512]{1,0:T(8,128)(2,1)S(1)} %pad_maximum_fusion.1), channel_id=1, source_target_pairs={{0,1},{1,0},{2,3},{3,2},{4,5},{5,4},{6,7},{7,6},{8,9},{9,8},{10,11... | collective-permute-start | bytes 1572872 | tf_op jit(solution)/shard_map/ppermute | solution.py:768
  495.4 36.1 %all-to-all-start.1 = ((bf16[32,8,768]{2,1,0:T(8,128)(2,1)}), bf16[32,8,768]{2,1,0:T(8,128)(2,1)}, u32[]{:S(2)}, u32[]{:S(2)}) async-start(bf16[32,8,768]{2,1,0:T(8,128)(2,1)} %bitcast.35.refs_0_), calls=%async_computation.1 | async-start | bytes 786432 | tf_op jit(solution)/shard_map/all_to_all | solution.py:1128
  512.1 39.9 %collective-permute-start.13 = (bf16[512,1536]{1,0:T(8,128)(2,1)}, bf16[512,1536]{1,0:T(8,128)(2,1)}, u32[]{:S(2)}, u32[]{:S(2)}) collective-permute-start(bf16[512,1536]{1,0:T(8,128)(2,1)} %delayed.5), channel_id=1, source_target_pairs={{0,1},{1,0},{2,3},{3,2},{4,5},{5,4},{6,7},{7,6},{8,9},{9,8},{10,11... | collective-permute-start | bytes 4718600 | tf_op jit(solution)/shard_map/ppermute | solution.py:761
  533.9 24.1 %all-to-all-start.2 = ((bf16[16,4,8,768]{3,2,1,0:T(8,128)(2,1)}), bf16[16,4,8,768]{3,2,1,0:T(8,128)(2,1)}, u32[]{:S(2)}, u32[]{:S(2)}) async-start(bf16[16,4,8,768]{3,2,1,0:T(8,128)(2,1)} %broadcast_in_dim.213), calls=%async_computation.2 | async-start | bytes 1572864 | tf_op jit(solution)/shard_map/all_to_all | solution.py:1132
  (71 other events, 892.0 us)
Sparse Core Ops, SparseCore 0:
  28.3 44.0 all-gather.7
  75.2 42.5 all-gather.9
  361.1 105.4 all-gather.13
  468.7 82.1 all-gather.11
